TPU v7x, 128 devices: a whole 4x4x4 slice. The times are simulated.
128 devices in a mesh: dp: 8 (over z, core), expert: 16 (over y, x).
Axes of the slice: x: 4, y: 4, z: 4, core: 2. Of those that a mesh axis runs over, the one named last changes fastest.
Arguments:
- tokens: bfloat16 [16384, 1536], P(('dp', 'expert')), may hold values from -6 to 6
- cotangent: bfloat16 [16384, 1536], P(('dp', 'expert')), may hold values from -6 to 6
- lengths: int32 [128, 4], P(('dp', 'expert')), may hold values from 1 to 64, 128 in all within a row
- routes: int32 [2, 16384, 4], P(None, ('dp', 'expert')), may hold values from 0 to 15, all different within a row; in each aligned block of 128 rows (0 to 127, 128 to 255, ..., all dimensions but the last counted through in order) at most 48 rows name the same one
- norm_attn: bfloat16 [2, 1536], P(None, 'dp'), may hold values from 0.5 to 1.5
- w_query: bfloat16 [2, 1536, 1536], P(None, 'dp'), may hold values from -0.15625 to 0.15625
- key_projection: bfloat16 [2, 1536, 256], P(None, 'dp'), may hold values from -0.15625 to 0.15625
- value_projection: bfloat16 [2, 1536, 256], P(None, 'dp'), may hold values from -0.15625 to 0.15625
- w_out: bfloat16 [2, 1536, 1536], P(None, 'dp'), may hold values from -0.625 to 0.625
- norm_ffn: bfloat16 [2, 1536], P(None, 'dp'), may hold values from 0.5 to 1.5
- w_router: bfloat16 [2, 1536, 16], P(None, 'dp'), may hold values from -0.078125 to 0.078125
- w_gate: bfloat16 [2, 16, 1536, 768], P(None, 'expert'), may hold values from -0.15625 to 0.15625
- w_up: bfloat16 [2, 16, 1536, 768], P(None, 'expert'), may hold values from -0.15625 to 0.15625
- w_down: bfloat16 [2, 16, 768, 1536], P(None, 'expert'), may hold values from -0.875 to 0.875
Outputs:
- mixed: bfloat16 [16384, 1536], P(('dp', 'expert'))
- grad_tokens: float32 [16384, 1536], P(('dp', 'expert'))
- grad_norm_attn: float32 [2, 1536], P(None, 'dp')
- grad_query: float32 [2, 1536, 1536], P(None, 'dp')
- grad_key: float32 [2, 1536, 256], P(None, 'dp')
- grad_value: float32 [2, 1536, 256], P(None, 'dp')
- grad_out: float32 [2, 1536, 1536], P(None, 'dp')
- grad_norm_ffn: float32 [2, 1536], P(None, 'dp')
- grad_router: float32 [2, 1536, 16], P(None, 'dp')
- grad_gate: float32 [2, 16, 1536, 768], P(None, 'expert', 'dp')
- grad_up: float32 [2, 16, 1536, 768], P(None, 'expert', 'dp')
- grad_down: float32 [2, 16, 768, 1536], P(None, 'expert', 'dp')
Inputs may be any that keep to these rules, and one draw needn't show every extreme that they name: `lengths`: each device's row sums to 128 and its longest sequence has 64 tokens. `routes`: each token names 4 different experts; in each layer, among one device's 128 tokens no expert is named more than 48 times, a bound that some block reaches.
All inputs are finite; a program needn't handle non-finite values.
Results may differ from a plain program's by a relative error of at most 0.025.
Values may be sent and summed in bfloat16 or wider, within the bound.
No kernel may reach another device: no remote copies, remote signals or barrier semaphores. Data moves between devices by JAX's collectives and lax.ppermute only.
A program may use at most 192 MiB of HBM per device.

v0:
```python
import jax
import jax.numpy as jnp
from jax import lax
from jax.experimental import pallas as pl
from jax.experimental.pallas import tpu as pltpu
from jax.sharding import PartitionSpec as P

QUERY_HEADS = 12
KEY_VALUE_HEADS = 2
GROUPS = QUERY_HEADS // KEY_VALUE_HEADS
HEAD = 128
LAYERS = 2
WIDTH = 1536
FF = 768
ROWS = 128
EXPERTS = 16
CAP = 48
SLOTS = EXPERTS * CAP
DP = 8
SHARD = WIDTH // DP
Q_END = QUERY_HEADS * HEAD
K_END = Q_END + KEY_VALUE_HEADS * HEAD
QKV = K_END + KEY_VALUE_HEADS * HEAD
SMALL = QKV + WIDTH
PACKED = SMALL + HEAD
GAIN_ATTN, GAIN_FFN = 16, 17
GAIN_HIGH, GAIN_LOW = 16, 32
PIECES = WIDTH // HEAD
TILE = 256
PARTS = 3
PART = SLOTS // PARTS
PART_ROWS = CAP // PARTS
CHUNKS, CHUNK = 16, 256
COLUMNS = 3 * WIDTH
EPSILON = 1e-06
ROPE_BASE = 1000000.0
SCALE = HEAD ** (-0.5)
GELU_A = 0.7978845608028654
GELU_B = 0.044715
VMEM_BYTES = 56 << 20
BF = jnp.bfloat16
F32 = jnp.float32
ANY = pl.BlockSpec(memory_space=pl.ANY)


def dot(left, right, left_dim=1, right_dim=0):
    return lax.dot_general(
        left, right, (((left_dim,), (right_dim,)), ((), ())), preferred_element_type=F32
    )


def split(values):
    high = values.astype(BF)
    return high, (values - high.astype(F32)).astype(BF)


def unit(values):
    return lax.rsqrt(jnp.mean(values * values, axis=-1, keepdims=True) + EPSILON)


def turn(values, cosine, sine):
    return values * cosine + pltpu.roll(values, HEAD // 2, 1) * sine


def expert_lanes(transposed=False, in_parts=False):
    shape = (SLOTS, HEAD) if transposed else (HEAD, SLOTS)
    slot = lax.broadcasted_iota(jnp.int32, shape, 0 if transposed else 1)
    expert = lax.broadcasted_iota(jnp.int32, shape, 1 if transposed else 0)
    if in_parts:
        held = ((slot & (PART - 1)) >> 4) == expert
    else:
        held = (slot >= expert * CAP) & (slot < expert * CAP + CAP)
    return held.astype(F32).astype(BF)


def gain_rows(small):
    row = lax.broadcasted_iota(jnp.int32, (8, HEAD), 0)
    lane = lax.broadcasted_iota(jnp.int32, (8, HEAD), 1)
    pick = ((lane == row + GAIN_ATTN) & (row < 2)).astype(F32).astype(BF)
    rows = dot(pick, small, 1, 1)
    return rows[0:1], rows[1:2]


def router_probs(rows, small):
    logits = dot(rows, small)
    lane = lax.broadcasted_iota(jnp.int32, logits.shape, 1)
    logits = jnp.where(lane < EXPERTS, logits, -1e30)
    powers = jnp.exp(logits - jnp.max(logits, axis=-1, keepdims=True))
    return powers / jnp.sum(powers, axis=-1, keepdims=True)


def start_all(pairs, sems):
    copies = [
        pltpu.make_async_copy(source, target, sems.at[i]) for i, (source, target) in enumerate(pairs)
    ]
    for copy in copies:
        copy.start()
    return copies


class Writer:
    def __init__(self, sems):
        self.sems, self.copies = sems, []

    def send(self, source, target):
        copy = pltpu.make_async_copy(source, target, self.sems.at[len(self.copies)])
        copy.start()
        self.copies.append(copy)

    def finish(self):
        for copy in self.copies:
            copy.wait()


class Reader:
    def __init__(self, sems, pairs):
        self.copies = start_all(pairs, sems)

    def take(self, count=1):
        for _ in range(count):
            self.copies.pop(0).wait()


def tiles(width):
    return [slice(at, at + TILE) for at in range(0, width, TILE)]


def small_block(w_hbm, w):
    last = w_hbm.shape[1] - HEAD
    return (w_hbm.at[:, pl.ds(last, HEAD)], w.at[:, pl.ds(SMALL, HEAD)])


def column_block(w_hbm, w, at):
    return (w_hbm.at[:, pl.ds(at, TILE)], w.at[:, pl.ds(at, TILE)])


def ring_blocks(me, blocks, w):
    pairs = []
    for core in range(2):
        start = me if core == 0 else me + 1 - 2 * (me % 2)
        for block, step in enumerate((0, DP - 2, 2, 4, 4)):
            ref = blocks[core * 5 + block]
            at = (start + step) % DP * SHARD + (SHARD // 2 if block == 4 else 0)
            at = pl.multiple_of(at, SHARD // 2)
            pairs += [(ref, w.at[pl.ds(at, ref.shape[0]), pl.ds(QKV, WIDTH)])]
    return pairs


def attn_forward_kernel(first, ins, outs, scratch):
    (x_hbm, w_hbm, cosine_hbm, sine_hbm, allowed_hbm, take_hbm, give_hbm), ins = ins[:7], ins[7:]
    (columns_hbm, qrot_hbm, krot_hbm, value_hbm, probs_hbm, after_hbm, router_hbm, high_hbm, low_hbm,
     rows_hbm), outs = outs[:10], outs[10:]
    (x_in, w, cosine, sine, allowed, take, give, returned, gates, x, columns, qrot, krot, value, probs,
     after, router, high, low, rows, in_sems, out_sems) = scratch
    acts = columns.at[:, :WIDTH]
    attended = columns.at[:, WIDTH : 2 * WIDTH]
    acts_two = columns.at[:, 2 * WIDTH :]
    pairs = []
    if first:
        out_pairs = ring_blocks(ins[0][0], ins[1:], w)
    else:
        out_pairs = [column_block(w_hbm, w, at) for at in range(QKV, SMALL, TILE)]
        high_below, low_below, returned_hbm = ins
        pairs += [(high_below, gates.at[:ROWS]), (low_below, gates.at[ROWS:])]
        pairs += [(returned_hbm, returned)]
    pairs += [(x_hbm, x_in), small_block(w_hbm, w)]
    pairs += [column_block(w_hbm, w, at) for at in range(0, QKV, TILE)]
    pairs += [(cosine_hbm, cosine), (sine_hbm, sine), (allowed_hbm, allowed)]
    pairs += out_pairs + [(take_hbm, take), (give_hbm, give)]
    reader, writer = Reader(in_sems, pairs), Writer(out_sems)
    if first:
        reader.take()
        x[...] = x_in[...].astype(F32)
    else:
        reader.take(4)
        for tile in tiles(WIDTH):
            both = dot(gates[...], returned[:, tile])
            x[:, tile] = x_in[:, tile] + both[:ROWS] + both[ROWS:]
        writer.send(x, outs[0])
    reader.take()
    small = w[:, SMALL:]
    gain_attn, gain_ffn = gain_rows(small)
    total = x[...]
    acts[...] = (total * unit(total) * gain_attn).astype(BF)
    wide = []
    for tile in tiles(QKV):
        reader.take()
        wide += [dot(acts[...], w[:, tile])]
    reader.take(3)
    for tile in range(QKV // TILE):
        for half in range(TILE // HEAD):
            head = tile * (TILE // HEAD) + half
            part = wide[tile][:, half * HEAD : (half + 1) * HEAD]
            if head < QUERY_HEADS:
                qrot[head] = turn(part, cosine[...], sine[...]).astype(BF)
            elif head < QUERY_HEADS + KEY_VALUE_HEADS:
                krot[head - QUERY_HEADS] = turn(part, cosine[...], sine[...]).astype(BF)
            else:
                value[head - QUERY_HEADS - KEY_VALUE_HEADS] = part.astype(BF)
    writer.send(qrot, qrot_hbm)
    writer.send(krot, krot_hbm)
    writer.send(value, value_hbm)
    open_scores = (allowed[...] > 0.5)[None]
    for k in range(KEY_VALUE_HEADS):
        heads = slice(k * GROUPS, (k + 1) * GROUPS)
        scores = dot(qrot[heads].reshape(GROUPS * ROWS, HEAD), krot[k], 1, 1) * SCALE
        scores = jnp.where(open_scores, scores.reshape(GROUPS, ROWS, ROWS), -1000000000.0)
        powers = jnp.exp(scores - jnp.max(scores, axis=-1, keepdims=True))
        shares = powers / jnp.sum(powers, axis=-1, keepdims=True)
        probs[heads] = shares
        mixed = dot(shares.astype(BF).reshape(GROUPS * ROWS, ROWS), value[k]).astype(BF)
        for group in range(GROUPS):
            at = (k * GROUPS + group) * HEAD
            attended[:, at : at + HEAD] = mixed[group * ROWS : (group + 1) * ROWS]
    writer.send(probs, probs_hbm)
    if first:
        reader.take(len(out_pairs))
    for tile in tiles(WIDTH):
        if not first:
            reader.take()
        after[:, tile] = x[:, tile] + dot(
            attended[...], w[:, QKV + tile.start : QKV + tile.stop]
        )
    writer.send(after, after_hbm)
    total = after[...]
    acts_two[...] = (total * unit(total) * gain_ffn).astype(BF)
    writer.send(columns, columns_hbm)
    reader.take(2)
    for tile in tiles(WIDTH):
        rows[:, tile] = dot(take[...], acts_two[:, tile]).astype(BF)
        writer.send(rows.at[:, tile], rows_hbm.at[:, tile])
    shares = router_probs(acts_two[...], small)
    router[...] = shares
    spread = expert_lanes(in_parts=not first)
    both = dot(jnp.concatenate(split(shares), axis=0), spread).astype(BF)
    high[...] = both[:ROWS] * give[...]
    low[...] = both[ROWS:] * give[...]
    writer.send(router, router_hbm)
    writer.send(high, high_hbm)
    writer.send(low, low_hbm)
    writer.finish()


HEADS = (QUERY_HEADS, ROWS, HEAD)
KEYS = (KEY_VALUE_HEADS, ROWS, HEAD)
TABLE = (ROWS, HEAD)
TOKENS = (ROWS, WIDTH)
WIDE = (SLOTS, WIDTH)


def specs_of(ins):
    return [pl.BlockSpec(memory_space=pltpu.SMEM if a.dtype == jnp.int32 else pl.ANY) for a in ins]


def run_attn(kernel, name, ins, order, outs, scratch, in_copies, out_copies, vmem):
    sd = jax.ShapeDtypeStruct

    def body(*refs):
        first_out = len(ins) + len(order)
        first_scratch = first_out + len(outs)
        kernel(refs[: len(ins)], refs[first_out:first_scratch], refs[first_scratch:])

    return pl.pallas_call(
        body,
        out_shape=[sd(shape, kind) for shape, kind in outs],
        in_specs=specs_of(ins) + [ANY] * len(order),
        out_specs=[ANY] * len(outs),
        scratch_shapes=[pltpu.VMEM(shape, kind) for shape, kind in scratch]
        + [pltpu.SemaphoreType.DMA((in_copies,)), pltpu.SemaphoreType.DMA((out_copies,))],
        compiler_params=pltpu.CompilerParams(vmem_limit_bytes=vmem),
        cost_estimate=pl.CostEstimate(
            flops=2 * ROWS * WIDTH * PACKED, bytes_accessed=20 << 20, transcendentals=200000
        ),
        name=name,
    )(*ins, *order)


def attn_forward(x, combine, w, ring, tables, take, give, order):
    first = combine is None
    outs = [
        ((ROWS, COLUMNS), BF), (HEADS, BF), (KEYS, BF), (KEYS, BF), ((QUERY_HEADS, ROWS, ROWS), F32),
        (TOKENS, F32), (TABLE, F32), ((ROWS, SLOTS), BF), ((ROWS, SLOTS), BF), (WIDE, BF),
    ]
    names = [
        "columns", "qrot", "krot", "value", "probs", "after", "router", "high", "low", "rows"
    ]
    scratch = [(TOKENS, x.dtype), ((WIDTH, PACKED), BF)] + [(TABLE, F32)] * 3
    scratch += [((SLOTS, ROWS), BF), ((ROWS, SLOTS), BF)]
    scratch += [((16, HEAD), BF)] * 2 if first else [(WIDE, BF), ((2 * ROWS, SLOTS), BF)]
    scratch += [(TOKENS, F32)] + outs
    ins = [x, w, *tables, take, give]
    if first:
        ins += ring
    else:
        high, low, returned = combine
        ins += [high, low, returned]
        outs = outs + [(TOKENS, F32)]
        names += ["x"]
    result = run_attn(
        lambda *refs: attn_forward_kernel(first, *refs), "attn_forward", ins, order, outs, scratch,
        20 + QKV // TILE, 20, VMEM_BYTES,
    )
    return dict(zip(names, result))


def norm_back(grad, gain, values):
    scale = unit(values)
    inner = grad * gain
    return scale * inner - values * (scale * scale * scale) * jnp.mean(
        inner * values, axis=-1, keepdims=True
    )


def attn_backward_kernel(last, ins, outs, scratch):
    (dx_hbm, back_hbm, w_hbm, cosine_hbm, sine_hbm, give_hbm, router_hbm, after_hbm, x_hbm, probs_hbm,
     qrot_hbm, krot_hbm, value_hbm), ins = ins[:13], ins[13:]
    (dx_in, back, w, cosine, sine, give, router, after, x_in, probs, qrot, krot, value, wide_in,
     small_in, datt, dx_out, packed), scratch = scratch[:18], scratch[18:]
    if last:
        rows, scratch = scratch[0], scratch[1:]
    in_sems, out_sems = scratch
    pairs = [(give_hbm, give), (back_hbm, back), (router_hbm, router), (dx_hbm, dx_in)]
    if not last:
        pairs += [(ins[0], wide_in)]
    pairs += [small_block(w_hbm, w), (after_hbm, after)]
    if last:
        for at in range(0, WIDTH, TILE):
            block = (pl.ds(at, TILE), pl.ds(QKV, WIDTH))
            pairs += [(w_hbm.at[block], w.at[block])]
    else:
        pairs += ring_blocks(ins[1][0], ins[2:], w)
    pairs += [(probs_hbm, probs), (value_hbm, value), (krot_hbm, krot), (qrot_hbm, qrot)]
    pairs += [(cosine_hbm, cosine), (sine_hbm, sine)]
    for at in range(0, WIDTH, TILE):
        block = (pl.ds(at, TILE), pl.ds(0, QKV))
        pairs += [(w_hbm.at[block], w.at[block])]
    pairs += [(x_hbm, x_in)]
    if last:
        pairs += [(ins[0], wide_in), (ins[1], small_in)]
    reader, writer = Reader(in_sems, pairs), Writer(out_sems)
    reader.take(4)
    dx = dx_in[...].astype(F32)
    spread = expert_lanes(True)
    if last:
        dgate = back[:, WIDTH:].astype(F32)
        drouter = dot(give[...], (dgate[:, 0:1] * spread).astype(BF))
        drouter += dot(give[...], (dgate[:, 1:2] * spread).astype(BF))
    else:
        reader.take()
        dgate = dot(dx.astype(BF), wide_in[...], 1, 1) * give[...]
        both = dot(jnp.concatenate(split(dgate), axis=0), spread)
        drouter = both[:ROWS] + both[ROWS:]
    reader.take(2)
    small = w[:, SMALL:]
    gain_attn, gain_ffn = gain_rows(small)
    shares = router[...]
    dlogits = shares * (drouter - jnp.sum(drouter * shares, axis=-1, keepdims=True))
    dlogits = dlogits.astype(BF)
    dacts_two = dot(dlogits, small, 1, 1) + dot(give[...], back[:, :WIDTH])
    total = after[...]
    scale = unit(total)
    dafter = dx + norm_back(dacts_two, gain_ffn, total)
    dx_out[...] = dafter
    packed[:, QKV:SMALL] = dafter.astype(BF)
    dgain = jnp.sum(dacts_two * total * scale, axis=0, keepdims=True)
    dgain_high, dgain_low = split(dgain)
    pieces = [jnp.zeros((GAIN_HIGH, HEAD), F32)]
    for part in (dgain_high.astype(F32), dgain_low.astype(F32)):
        pieces += [part[:, at : at + HEAD] for at in range(0, WIDTH, HEAD)]
        pieces += [jnp.zeros((GAIN_LOW - GAIN_HIGH - PIECES, HEAD), F32)]
    pieces += [jnp.zeros((HEAD - 2 * GAIN_LOW + GAIN_HIGH, HEAD), F32)]
    packed[:, SMALL:] = (dlogits.astype(F32) + jnp.concatenate(pieces, axis=0).T).astype(BF)
    writer.send(packed.at[:, QKV:], outs[1].at[:, QKV:])
    if not last:
        reader.take(len(ins) - 2)
    for tile in tiles(WIDTH):
        if last:
            reader.take()
        wide = dot(packed[:, QKV:SMALL], w[tile, QKV:SMALL], 1, 1).astype(BF)
        for half in range(TILE // HEAD):
            datt[tile.start // HEAD + half] = wide[:, half * HEAD : (half + 1) * HEAD]
    reader.take(6)
    for k in range(KEY_VALUE_HEADS):
        heads = slice(k * GROUPS, (k + 1) * GROUPS)
        datt_k = datt[heads].reshape(GROUPS * ROWS, HEAD)
        p = probs[heads].reshape(GROUPS * ROWS, ROWS)
        dprobs = dot(datt_k, value[k], 1, 1)
        dvalue = dot(p.astype(BF), datt_k, 0, 0)
        dscores = (p * (dprobs - jnp.sum(dprobs * p, axis=-1, keepdims=True))).astype(BF)
        dqrot = dot(dscores, krot[k]) * SCALE
        dkrot = dot(dscores, qrot[heads].reshape(GROUPS * ROWS, HEAD), 0, 0) * SCALE
        for group in range(GROUPS):
            at = (k * GROUPS + group) * HEAD
            part = dqrot[group * ROWS : (group + 1) * ROWS]
            packed[:, at : at + HEAD] = turn(part, cosine[...], -sine[...]).astype(BF)
        at = Q_END + k * HEAD
        packed[:, at : at + HEAD] = turn(dkrot, cosine[...], -sine[...]).astype(BF)
        at = K_END + k * HEAD
        packed[:, at : at + HEAD] = dvalue.astype(BF)
    writer.send(packed.at[:, :QKV], outs[1].at[:, :QKV])
    parts = []
    for tile in tiles(WIDTH):
        reader.take()
        parts += [dot(packed[:, :QKV], w[tile, :QKV], 1, 1)]
    dacts = jnp.concatenate(parts, axis=1)
    reader.take()
    dx = dx_out[...] + norm_back(dacts, gain_attn, x_in[...].astype(F32))
    dx_out[...] = dx
    writer.send(dx_out, outs[0])
    if last:
        reader.take(2)
        dx_low = dx.astype(BF)
        both = dot(spread, jnp.concatenate(split(small_in[...]), axis=0), 1, 1).astype(BF)
        gates = jnp.concatenate([both[:, :ROWS] * wide_in[...], both[:, ROWS:] * wide_in[...]], axis=1)
        twice = jnp.concatenate([dx_low, dx_low], axis=0)
        for tile in tiles(WIDTH):
            rows[:, tile] = dot(gates, twice[:, tile]).astype(BF)
            writer.send(rows.at[:, tile], outs[2].at[:, tile])
    writer.finish()


def attn_backward(dx, back, x, kept, w, ring, tables, give, below, returned, order):
    last = below is not None
    outs = [(TOKENS, F32), ((ROWS, PACKED), BF)]
    if last:
        outs += [(WIDE, BF)]
    ins = [dx, back, w, tables[0], tables[1], give, kept["router"], kept["after"], x]
    ins += [kept[n] for n in ("probs", "qrot", "krot", "value")]
    ins += list(below) if last else [returned, *ring]
    scratch = [
        (TOKENS, dx.dtype), (back.shape, BF), ((WIDTH, PACKED), BF), (TABLE, F32), (TABLE, F32),
        ((ROWS, SLOTS), BF), (TABLE, F32), (TOKENS, F32), (TOKENS, x.dtype),
        ((QUERY_HEADS, ROWS, ROWS), F32), (HEADS, BF), (KEYS, BF), (KEYS, BF),
        ((SLOTS, ROWS), BF) if last else (WIDE, BF), (TABLE, F32), (HEADS, BF),
    ] + outs
    return run_attn(
        lambda *refs: attn_backward_kernel(last, *refs), "attn_backward", ins, order, outs, scratch,
        24 + WIDTH // TILE, 12, VMEM_BYTES,
    )


def gelu_parts(gate):
    square = gate * gate
    bend = jnp.tanh(GELU_A * gate * (1.0 + GELU_B * square))
    return bend, square


def gelu(gate):
    bend, _ = gelu_parts(gate)
    return 0.5 * gate * (1.0 + bend)


def gelu_both(gate):
    bend, square = gelu_parts(gate)
    slope = 0.5 * (1.0 + bend) + 0.5 * gate * (1.0 - bend * bend) * GELU_A * (
        1.0 + 3.0 * GELU_B * square
    )
    return 0.5 * gate * (1.0 + bend), slope


def weight_pairs(l, gate_hbm, up_hbm, down_hbm, gate_w, up_w, down_w):
    gate_up = []
    for at in range(0, FF, TILE):
        block = (slice(None), pl.ds(at, TILE))
        gate_up += [(gate_hbm.at[l, 0].at[block], gate_w.at[block])]
        gate_up += [(up_hbm.at[l, 0].at[block], up_w.at[block])]
    down = [(down_hbm.at[l, 0], down_w)]
    return gate_up, down


def run_experts(kernel, name, ins, order, outs, scratch, in_copies, flops):
    sd = jax.ShapeDtypeStruct
    count = len(ins) + len(order)

    def body(*refs):
        kernel(*refs[: len(ins)], *refs[count:])

    return pl.pallas_call(
        body,
        out_shape=[sd(shape, BF) for shape in outs],
        in_specs=specs_of(ins) + [ANY] * len(order),
        out_specs=[ANY] * len(outs),
        scratch_shapes=[pltpu.VMEM(shape, kind) for shape, kind in scratch]
        + [pltpu.SemaphoreType.DMA((in_copies,)), pltpu.SemaphoreType.DMA((40,))],
        compiler_params=pltpu.CompilerParams(vmem_limit_bytes=VMEM_BYTES),
        cost_estimate=pl.CostEstimate(
            flops=flops, bytes_accessed=20 << 20, transcendentals=SLOTS * FF
        ),
        name=name,
    )(*ins, *order)


def experts_forward_kernel(
    received_hbm, gate_hbm, up_hbm, down_hbm, act_hbm, slope_hbm, hidden_hbm, out_hbm,
    received, gate_w, up_w, down_w, act_s, slope_s, hidden, out, in_sems, out_sems,
):
    gate_up, down = weight_pairs(0, gate_hbm, up_hbm, down_hbm, gate_w, up_w, down_w)
    copies = start_all([(received_hbm, received)] + gate_up + down, in_sems)
    writer = Writer(out_sems)
    copies.pop(0).wait()
    for tile in tiles(FF):
        copies.pop(0).wait()
        copies.pop(0).wait()
        gate = dot(received[...], gate_w[:, tile])
        up = dot(received[...], up_w[:, tile])
        act, slope = gelu_both(gate)
        act_s[:, tile] = act.astype(BF)
        slope_s[:, tile] = (slope * up).astype(BF)
        hidden[:, tile] = (act * up).astype(BF)
    copies.pop(0).wait()
    writer.send(act_s, act_hbm)
    writer.send(slope_s, slope_hbm)
    writer.send(hidden, hidden_hbm)
    for tile in tiles(WIDTH):
        out[:, tile] = dot(hidden[...], down_w[:, tile]).astype(BF)
        writer.send(out.at[:, tile], out_hbm.at[:, tile])
    writer.finish()


EXPERT_SCRATCH = [((WIDTH, FF), BF), ((WIDTH, FF), BF), ((FF, WIDTH), BF)]


def experts_forward(received, weights, order):
    small = (SLOTS, FF)
    wide = (SLOTS, WIDTH)
    return run_experts(
        experts_forward_kernel, "experts_forward", [received, *weights], order,
        [small, small, small, wide],
        [(wide, BF)] + EXPERT_SCRATCH + [(small, BF)] * 3 + [(wide, BF)],
        8, 6 * SLOTS * WIDTH * FF,
    )


def back_tiles(dgate, dup, gate_w, up_w, back, back_hbm, writer):
    for tile in tiles(WIDTH):
        back[:, tile] = (
            dot(dgate[...], gate_w[tile], 1, 1) + dot(dup[...], up_w[tile], 1, 1)
        ).astype(BF)
        writer.send(back.at[:, tile], back_hbm.at[:, tile])


def experts_both_kernel(
    me, received_hbm, dx_hbm, w_hbm, gate_hbm, up_hbm, down_hbm,
    hidden_hbm, part0_hbm, part1_hbm, part2_hbm, dslot_hbm, dgate_hbm, dup_hbm, back_hbm,
    received, dx, small, gate_w, up_w, down_w, act_s, slope_s, hidden, part0, part1, part2, dslot, dgate, dup,
    back, in_sems, out_sems,
):
    gate_up, down = weight_pairs(1, gate_hbm, up_hbm, down_hbm, gate_w, up_w, down_w)
    pairs = [(received_hbm, received)] + gate_up
    pairs += [(w_hbm.at[:, pl.ds(SMALL, HEAD)], small), (dx_hbm, dx)] + down
    copies = start_all(pairs, in_sems)
    writer = Writer(out_sems)
    copies.pop(0).wait()
    for tile in tiles(FF):
        copies.pop(0).wait()
        copies.pop(0).wait()
        gate = dot(received[...], gate_w[:, tile])
        up = dot(received[...], up_w[:, tile])
        act, slope = gelu_both(gate)
        act_s[:, tile] = act
        slope_s[:, tile] = slope * up
        hidden[:, tile] = (act * up).astype(BF)
    for copy in copies:
        copy.wait()
    writer.send(hidden, hidden_hbm)
    shares = router_probs(received[...], small[...])
    lane = lax.broadcasted_iota(jnp.int32, shares.shape, 1)
    weight = jnp.sum(jnp.where(lane == me[0], shares, 0.0), axis=-1, keepdims=True)
    total = jnp.zeros((SLOTS, 1), F32)
    for tile in tiles(WIDTH):
        part = dot(hidden[...], down_w[:, tile]).astype(BF)
        for expert in range(EXPERTS):
            for p, target in enumerate((part0, part1, part2)):
                at = expert * CAP + p * PART_ROWS
                target[expert, :, tile] = part[at : at + PART_ROWS]
        wide = dx[:, tile].astype(F32)
        total += jnp.sum(wide * part.astype(F32), axis=-1, keepdims=True)
        dslot[:, tile] = (weight * wide).astype(BF)
    writer.send(part0, part0_hbm)
    writer.send(part1, part1_hbm)
    writer.send(part2, part2_hbm)
    writer.send(dslot, dslot_hbm)
    high, low = split(total)
    back[:, WIDTH:] = jnp.where(
        lane == 0, high.astype(F32), jnp.where(lane == 1, low.astype(F32), 0.0)
    ).astype(BF)
    writer.send(back.at[:, WIDTH:], back_hbm.at[:, WIDTH:])
    for tile in tiles(FF):
        dhidden = dot(dslot[...], down_w[tile], 1, 1)
        dgate[:, tile] = (dhidden * slope_s[:, tile]).astype(BF)
        dup[:, tile] = (dhidden * act_s[:, tile]).astype(BF)
    writer.send(dgate, dgate_hbm)
    writer.send(dup, dup_hbm)
    back_tiles(dgate, dup, gate_w, up_w, back, back_hbm, writer)
    writer.finish()


def experts_both(me, received, dx, w, weights, order):
    small = (SLOTS, FF)
    wide = (SLOTS, WIDTH)
    part = (EXPERTS, PART_ROWS, WIDTH)
    back = (SLOTS, WIDTH + HEAD)
    return run_experts(
        experts_both_kernel, "experts_both", [me, received, dx, w, *weights], order,
        [small, part, part, part, wide, small, small, back],
        [(wide, BF), (wide, BF), ((WIDTH, HEAD), BF)] + EXPERT_SCRATCH
        + [(small, F32), (small, F32), (small, BF), (part, BF), (part, BF), (part, BF),
           (wide, BF), (small, BF), (small, BF), (back, BF)],
        10, 12 * SLOTS * WIDTH * FF,
    )


def experts_backward_kernel(
    dslot_hbm, act_hbm, slope_hbm, gate_hbm, up_hbm, down_hbm, dgate_hbm, dup_hbm, back_hbm,
    dslot, act_s, slope_s, gate_w, up_w, down_w, dgate, dup, back, in_sems, out_sems,
):
    pairs = [(dslot_hbm, dslot)]
    for tile in tiles(FF):
        block = pl.ds(tile.start, TILE)
        pairs += [(down_hbm.at[0, 0].at[block], down_w.at[block])]
    pairs += [(slope_hbm, slope_s), (act_hbm, act_s)]
    for tile in tiles(WIDTH):
        block = pl.ds(tile.start, TILE)
        pairs += [(gate_hbm.at[0, 0].at[block], gate_w.at[block])]
        pairs += [(up_hbm.at[0, 0].at[block], up_w.at[block])]
    copies = start_all(pairs, in_sems)
    writer = Writer(out_sems)
    copies.pop(0).wait()
    dhidden = []
    for tile in tiles(FF):
        copies.pop(0).wait()
        dhidden += [dot(dslot[...], down_w[tile], 1, 1)]
    copies.pop(0).wait()
    copies.pop(0).wait()
    for tile, part in zip(tiles(FF), dhidden):
        dgate[:, tile] = (part * slope_s[:, tile].astype(F32)).astype(BF)
        dup[:, tile] = (part * act_s[:, tile].astype(F32)).astype(BF)
    writer.send(dgate, dgate_hbm)
    writer.send(dup, dup_hbm)
    for copy in copies:
        copy.wait()
    back_tiles(dgate, dup, gate_w, up_w, back, back_hbm, writer)
    writer.finish()


def experts_backward(dslot, act, slope, weights, order):
    small = (SLOTS, FF)
    wide = (SLOTS, WIDTH)
    return run_experts(
        experts_backward_kernel, "experts_backward", [dslot, act, slope, *weights], order,
        [small, small, wide],
        [(wide, BF), (small, BF), (small, BF)] + EXPERT_SCRATCH
        + [(small, BF), (small, BF), (wide, BF)],
        6 + 2 * WIDTH // TILE, 6 * SLOTS * WIDTH * FF,
    )


def expert_grads_kernel(received, dgate_pre, dup_pre, hidden, dslot, packed):
    gate = dot(received[...], dgate_pre[...], 0, 0).astype(BF)
    up = dot(received[...], dup_pre[...], 0, 0).astype(BF)
    down = dot(hidden[...], dslot[...], 0, 0).astype(BF)
    for part in range(DP // 2):
        packed[part, :SHARD, :FF] = gate[part * SHARD : (part + 1) * SHARD]
        packed[part, :SHARD, FF:] = up[part * SHARD : (part + 1) * SHARD]
        packed[part, SHARD:] = down[part * FF // DP : (part + 1) * FF // DP]


def expert_grads(received, dgate_pre, dup_pre, hidden, dslot):
    rows = SHARD + FF // DP
    whole = lambda width: pl.BlockSpec((SLOTS, width), lambda i: (0, 0))
    part = lambda width: pl.BlockSpec((SLOTS, width), lambda i: (0, i))
    return pl.pallas_call(
        expert_grads_kernel,
        grid=(2,),
        out_shape=jax.ShapeDtypeStruct((DP, rows, WIDTH), BF),
        in_specs=[part(WIDTH // 2), whole(FF), whole(FF), part(FF // 2), whole(WIDTH)],
        out_specs=pl.BlockSpec((DP // 2, rows, WIDTH), lambda i: (i, 0, 0)),
        compiler_params=pltpu.CompilerParams(vmem_limit_bytes=VMEM_BYTES),
        cost_estimate=pl.CostEstimate(
            flops=6 * SLOTS * WIDTH * FF, bytes_accessed=14 << 20, transcendentals=0
        ),
        name="expert_grads",
    )(received, dgate_pre, dup_pre, hidden, dslot).reshape(DP * rows, WIDTH)


def pack_kernel(
    l, query_hbm, key_hbm, value_hbm, out_hbm, router_hbm, gain_attn, gain_ffn, packed_hbm, *rest
):
    if l == 0:
        out_copy, packed, out, router, sems, out_sems = rest
    else:
        packed, router, sems, out_sems = rest
        out = packed.at[:, pl.ds(QKV, WIDTH)]
    pairs = [
        (router_hbm.at[l], router),
        (query_hbm.at[l], packed.at[:, pl.ds(0, Q_END)]),
        (key_hbm.at[l], packed.at[:, pl.ds(Q_END, K_END - Q_END)]),
        (value_hbm.at[l], packed.at[:, pl.ds(K_END, QKV - K_END)]),
        (out_hbm.at[l], out),
    ]
    reader, writer = Reader(sems, pairs), Writer(out_sems)
    reader.take()
    small = [router[...].astype(F32), gain_attn[l : l + 1].astype(F32)]
    small += [gain_ffn[l : l + 1].astype(F32), jnp.zeros((HEAD - EXPERTS - 2, SHARD), F32)]
    small = jnp.concatenate(small, axis=0)
    small = jnp.concatenate([small, jnp.zeros((HEAD, TILE - SHARD), F32)], axis=1).T
    packed[:, packed.shape[1] - HEAD :] = small[:SHARD].astype(BF)
    reader.take(3)
    if l == 0:
        writer.send(packed, packed_hbm)
        reader.take()
        writer.send(out, out_copy)
    else:
        reader.take()
        writer.send(packed, packed_hbm)
    writer.finish()


def pack(l, query, key, value, out, router, gain_attn, gain_ffn):
    sd = jax.ShapeDtypeStruct
    vmem = pl.BlockSpec(memory_space=pltpu.VMEM)
    packed = (SHARD, QKV + HEAD) if l == 0 else (SHARD, PACKED)
    outs = [packed] + [(SHARD, WIDTH)] * (l == 0)
    return pl.pallas_call(
        lambda *refs: pack_kernel(l, *refs),
        out_shape=[sd(shape, BF) for shape in outs],
        in_specs=[ANY] * 5 + [vmem] * 2,
        out_specs=[ANY] * len(outs),
        scratch_shapes=[pltpu.VMEM(shape, BF) for shape in outs]
        + [pltpu.VMEM((EXPERTS, SHARD), BF)]
        + [pltpu.SemaphoreType.DMA((5,)), pltpu.SemaphoreType.DMA((2,))],
        compiler_params=pltpu.CompilerParams(vmem_limit_bytes=VMEM_BYTES),
        name="pack",
    )(query, key, value, out, router.transpose(0, 2, 1), gain_attn, gain_ffn)


def ring(block):
    def move(values, step):
        return lax.ppermute(values, "dp", [(i, (i + step) % DP) for i in range(DP)])

    half = block.shape[0] // 2
    previous, following = move(block, 2), move(block, -2)
    far = [move(previous[:half], 2), move(following[half:], -2)]
    mine = [block, previous, following, *far]
    swap = [(i, i ^ 1) for i in range(DP)]
    return mine + [lax.ppermute(values, "dp", swap) for values in mine]


def seq_tables(counts):
    ends = jnp.cumsum(counts)
    starts = ends - counts
    place = jnp.arange(ROWS, dtype=jnp.int32)
    member = (place[:, None] >= starts[None, :]) & (place[:, None] < ends[None, :])
    index = jnp.arange(counts.shape[0], dtype=jnp.int32)
    segment = jnp.sum(jnp.where(member, index[None, :], 0), axis=1)
    position = place - jnp.sum(jnp.where(member, starts[None, :], 0), axis=1)
    allowed = (segment[:, None] == segment[None, :]) & (place[:, None] >= place[None, :])
    freqs = ROPE_BASE ** (-2.0 * jnp.arange(HEAD // 2, dtype=F32) / HEAD)
    angle = position.astype(F32)[:, None] * freqs[None, :]
    cosine, sine = jnp.cos(angle), jnp.sin(angle)
    return (
        jnp.concatenate([cosine, cosine], axis=1),
        jnp.concatenate([-sine, sine], axis=1),
        allowed.astype(F32),
    )


def slot_matrix(choices, in_parts=False):
    experts = jnp.arange(EXPERTS, dtype=jnp.int32)
    member = jnp.any(choices[:, :, None] == experts[None, None, :], axis=1).astype(BF)
    row = lax.broadcasted_iota(jnp.int32, (ROWS, ROWS), 0)
    column = lax.broadcasted_iota(jnp.int32, (ROWS, ROWS), 1)
    rank = dot((column < row).astype(BF), member).astype(BF)
    slot = jnp.arange(SLOTS, dtype=jnp.int32)[None, :]
    if in_parts:
        owner, place = slot % PART // PART_ROWS, slot // PART * PART_ROWS + slot % PART_ROWS
    else:
        owner, place = slot // CAP, slot % CAP
    expand = (owner == experts[:, None]).astype(BF)
    return ((dot(member, expand) > 0.5) & (dot(rank, expand) == place.astype(F32))).astype(BF)


def exchange(rows):
    width = rows.shape[-1]
    moved = lax.all_to_all(
        rows.reshape(EXPERTS, -1, width), "expert", split_axis=0, concat_axis=0, tiled=True
    )
    return moved.reshape(-1, width)


def after(values, *order):
    return pl.pallas_call(
        lambda *refs: None,
        out_shape=jax.ShapeDtypeStruct(values.shape, values.dtype),
        in_specs=[ANY] * (1 + len(order)),
        out_specs=ANY,
        input_output_aliases={0: 0},
        name="after",
    )(values, *order)


def turn_columns_kernel(me, columns_hbm, turned_hbm, columns, turned, in_sems, out_sems):
    base = me[0] * SHARD // HEAD * HEAD
    pairs = []
    for i in range(3):
        at = pl.multiple_of(base + i * WIDTH, HEAD)
        pairs += [(columns_hbm.at[:, pl.ds(at, TILE)], columns.at[:, pl.ds(i * TILE, TILE)])]
    reader, writer = Reader(in_sems, pairs), Writer(out_sems)
    for i in range(3):
        reader.take()
        turned[i] = columns[:, i * TILE : (i + 1) * TILE].T
        writer.send(turned.at[i], turned_hbm.at[i])
    writer.finish()


def turn_columns(me, columns):
    tokens = DP * ROWS
    return pl.pallas_call(
        turn_columns_kernel,
        out_shape=jax.ShapeDtypeStruct((3, TILE, tokens), BF),
        in_specs=[pl.BlockSpec(memory_space=pltpu.SMEM), ANY],
        out_specs=ANY,
        scratch_shapes=[
            pltpu.VMEM((tokens, 3 * TILE), BF),
            pltpu.VMEM((3, TILE, tokens), BF),
            pltpu.SemaphoreType.DMA((3,)),
            pltpu.SemaphoreType.DMA((3,)),
        ],
        compiler_params=pltpu.CompilerParams(vmem_limit_bytes=VMEM_BYTES),
        cost_estimate=pl.CostEstimate(flops=0, bytes_accessed=4 << 20, transcendentals=0),
        name="turn_columns",
    )(me, columns)


def dense_grads_kernel(me, turned_hbm, factors_hbm, pieces_hbm, turned, factors, total, pieces,
                       in_sems, out_sems):
    start = me[0] * SHARD
    shift = start % HEAD
    base = start - shift
    copies = Writer(out_sems)
    pairs = [(turned_hbm, turned)]
    for at in range(0, PACKED, CHUNK):
        block = (slice(None), pl.ds(at, min(CHUNK, PACKED - at)))
        pairs += [(factors_hbm.at[block], factors.at[block])]
    reader = Reader(in_sems, pairs)
    reader.take()

    def put(chunk, values):
        pieces[chunk] = values.astype(BF)
        copies.send(pieces.at[chunk], pieces_hbm.at[chunk])

    for chunk in range(SMALL // CHUNK):
        reader.take()
        total[chunk % 2] = dot(
            turned[0 if chunk < QKV // CHUNK else 1],
            factors[:, chunk * CHUNK : (chunk + 1) * CHUNK],
        )
        put(chunk, total[chunk % 2, pl.ds(pl.multiple_of(shift, 64), SHARD), :])
    reader.take()
    ends = jnp.zeros((ROWS, HEAD), F32)
    for source in range(DP):
        ends += factors[source * ROWS : (source + 1) * ROWS, SMALL:].astype(F32)
    lane = lax.broadcasted_iota(jnp.int32, (ROWS, HEAD), 1)

    def gain_piece(piece):
        held = (lane == piece + GAIN_HIGH) | (lane == piece + GAIN_LOW)
        return jnp.sum(jnp.where(held, ends, 0.0), axis=1, keepdims=True)

    first, second = gain_piece(base // HEAD), gain_piece(base // HEAD + 1)
    gain = jnp.where(
        shift == 0,
        jnp.concatenate([first, second[: SHARD - ROWS]], axis=0),
        jnp.concatenate([first[ROWS // 2 :], second], axis=0),
    )
    gain_high, gain_low = split(gain)
    total[0, :, :HEAD] = dot(turned[2], factors[:, SMALL:])
    router = total[0, pl.ds(pl.multiple_of(shift, 64), SHARD), :HEAD]
    lane = lax.broadcasted_iota(jnp.int32, (SHARD, HEAD), 1)
    router = jnp.where(lane < EXPERTS, router, 0.0)
    router = jnp.where(lane == EXPERTS, gain_high.astype(F32), router)
    router = jnp.where(lane == EXPERTS + 1, gain_low.astype(F32), router)
    put(CHUNKS - 2, jnp.concatenate([router, jnp.zeros_like(router)], axis=1))
    put(CHUNKS - 1, jnp.zeros((SHARD, CHUNK), F32))
    copies.finish()


def dense_grads(me, turned, factors, order):
    tokens = DP * ROWS

    def body(*refs):
        dense_grads_kernel(*refs[:3], *refs[3 + len(order) :])

    return pl.pallas_call(
        body,
        out_shape=jax.ShapeDtypeStruct((CHUNKS, SHARD, CHUNK), BF),
        in_specs=[pl.BlockSpec(memory_space=pltpu.SMEM)] + [ANY] * (2 + len(order)),
        out_specs=ANY,
        scratch_shapes=[
            pltpu.VMEM((3, TILE, tokens), BF),
            pltpu.VMEM((tokens, PACKED), BF),
            pltpu.VMEM((2, TILE, CHUNK), F32),
            pltpu.VMEM((CHUNKS, SHARD, CHUNK), BF),
            pltpu.SemaphoreType.DMA((1 + CHUNKS,)),
            pltpu.SemaphoreType.DMA((CHUNKS,)),
        ],
        compiler_params=pltpu.CompilerParams(vmem_limit_bytes=VMEM_BYTES),
        cost_estimate=pl.CostEstimate(
            flops=2 * tokens * TILE * PACKED, bytes_accessed=10 << 20, transcendentals=0
        ),
        name="dense_grads",
    )(me, turned, factors, *order)


def to_expert_peers(pieces):
    return lax.all_to_all(pieces, "expert", split_axis=0, concat_axis=0, tiled=True)


def sum_pieces_kernel(pieces_hbm, out_hbm, pieces, out, in_sems, out_sems):
    half = CHUNKS // 2
    pairs = []
    for at in (0, half):
        block = pl.ds(at, half)
        pairs += [(pieces_hbm.at[block, :, pl.ds(0, CHUNK)], pieces.at[block])]
    reader, writer = Reader(in_sems, pairs), Writer(out_sems)
    reader.take()
    total = pieces[0].astype(F32)
    for i in range(1, half):
        total += pieces[i].astype(F32)
    reader.take()
    for i in range(half, CHUNKS):
        total += pieces[i].astype(F32)
    out[...] = total.astype(BF)
    if len(out_hbm.shape) == 3:
        for i in range(CHUNKS):
            writer.send(out, out_hbm.at[i])
    else:
        writer.send(out, out_hbm)
    writer.finish()


def sum_pieces(pieces, copies):
    return pl.pallas_call(
        sum_pieces_kernel,
        out_shape=jax.ShapeDtypeStruct((copies,) * (copies > 1) + (SHARD, CHUNK), BF),
        in_specs=[ANY],
        out_specs=ANY,
        scratch_shapes=[
            pltpu.VMEM((CHUNKS, SHARD, CHUNK), BF),
            pltpu.VMEM((SHARD, CHUNK), BF),
            pltpu.SemaphoreType.DMA((2,)),
            pltpu.SemaphoreType.DMA((CHUNKS,)),
        ],
        compiler_params=pltpu.CompilerParams(vmem_limit_bytes=VMEM_BYTES),
        name="sum_pieces",
    )(pieces)


def finish_kernel(l, refs):
    (pieces, w_query, key_projection, value_projection, norm_attn), refs = refs[:5], refs[5:]
    if l == 0:
        ends_above, refs = refs[0], refs[5:]
        (query_hbm, key_hbm, value_hbm, out_hbm, gain_attn, gain_ffn, router) = refs[:7]
        query, key, value, out, sems = refs[7:]
    else:
        query_hbm, key_hbm, value_hbm, out_hbm, ends_out, query, key, value, out, sems = refs
    writer = Writer(sems)
    rows = jnp.zeros((SHARD, 1), F32)
    for chunk in range(SMALL // CHUNK):
        part = pieces[chunk].astype(F32)
        lanes = slice(chunk * CHUNK, (chunk + 1) * CHUNK)
        if chunk < Q_END // CHUNK:
            query[:, lanes] = part
            weight = w_query[l, :, lanes]
        elif chunk == Q_END // CHUNK:
            key[...] = part
            weight = key_projection[l]
            writer.send(query, query_hbm.at[l])
            writer.send(key, key_hbm.at[l])
        elif chunk < QKV // CHUNK:
            value[...] = part
            weight = value_projection[l]
            writer.send(value, value_hbm.at[l])
        else:
            out[:, lanes.start - QKV : lanes.stop - QKV] = part
            continue
        rows += jnp.sum(part * weight.astype(F32), axis=1, keepdims=True)
    writer.send(out, out_hbm.at[l])
    ends = pieces[CHUNKS - 2, :, :HEAD].astype(F32)
    ffn = ends[:, EXPERTS : EXPERTS + 1] + ends[:, EXPERTS + 1 : EXPERTS + 2]
    lane = lax.broadcasted_iota(jnp.int32, (SHARD, HEAD), 1)
    ends = jnp.where(lane == EXPERTS, rows, jnp.where(lane == EXPERTS + 1, ffn, ends))
    if l > 0:
        ends_out[...] = ends
    else:
        for layer, part in enumerate((ends, ends_above[...])):
            wide = jnp.concatenate([part, jnp.zeros((TILE - SHARD, HEAD), F32)], axis=0).T
            router[layer] = wide[:EXPERTS, :SHARD]
            gain = norm_attn[layer : layer + 1].astype(F32)
            gain_attn[layer : layer + 1] = wide[EXPERTS : EXPERTS + 1, :SHARD] / gain
            gain_ffn[layer : layer + 1] = wide[EXPERTS + 1 : EXPERTS + 2, :SHARD]
    writer.finish()


def finish(l, pieces, weights, norm_attn, above):
    sd = jax.ShapeDtypeStruct
    vmem = pl.BlockSpec(memory_space=pltpu.VMEM)
    keys = (SHARD, KEY_VALUE_HEADS * HEAD)
    slabs = [(SHARD, Q_END), keys, keys, (SHARD, WIDTH)]
    outs = [sd((LAYERS,) + shape, F32) for shape in slabs]
    if above is None:
        outs += [sd((SHARD, HEAD), F32)]
        ins, in_specs, aliases = [], [], {}
    else:
        outs += [sd((LAYERS, SHARD), F32)] * 2 + [sd((LAYERS, EXPERTS, SHARD), F32)]
        ins, in_specs = [above[4], *above[:4]], [vmem] + [ANY] * 4
        aliases = {6 + i: i for i in range(4)}
    return pl.pallas_call(
        lambda *refs: finish_kernel(l, refs),
        out_shape=outs,
        in_specs=[vmem] * 5 + in_specs,
        out_specs=[ANY] * 4 + [vmem] * (len(outs) - 4),
        input_output_aliases=aliases,
        scratch_shapes=[pltpu.VMEM(shape, F32) for shape in slabs]
        + [pltpu.SemaphoreType.DMA((4,))],
        compiler_params=pltpu.CompilerParams(vmem_limit_bytes=VMEM_BYTES),
        name="finish",
    )(pieces, *weights, norm_attn, *ins)


def finish_experts_kernel(shares0, shares1, gate, up, down):
    for l, shares in enumerate((shares0, shares1)):
        gate[l, 0] = shares[:SHARD, :FF].astype(F32)
        up[l, 0] = shares[:SHARD, FF:].astype(F32)
        down[l, 0] = shares[SHARD:].astype(F32)


def finish_experts(shares0, shares1):
    sd = jax.ShapeDtypeStruct
    vmem = pl.BlockSpec(memory_space=pltpu.VMEM)
    return pl.pallas_call(
        finish_experts_kernel,
        out_shape=[
            sd((LAYERS, 1, SHARD, FF), F32), sd((LAYERS, 1, SHARD, FF), F32),
            sd((LAYERS, 1, FF // DP, WIDTH), F32),
        ],
        in_specs=[vmem] * 2,
        out_specs=[vmem] * 3,
        compiler_params=pltpu.CompilerParams(vmem_limit_bytes=VMEM_BYTES),
        name="finish_experts",
    )(shares0, shares1)


def mixed_kernel(x_hbm, high, low, part0, part1, part2, out, x, gates, returned, sems):
    pairs = [(high, gates.at[:ROWS]), (low, gates.at[ROWS:]), (x_hbm, x)]
    for p, part in enumerate((part0, part1, part2)):
        pairs += [(part, returned.at[pl.ds(p * PART, PART)])]
    Reader(sems, pairs).take(len(pairs))
    for tile in tiles(WIDTH):
        both = dot(gates[...], returned[:, tile])
        out[:, tile] = (x[:, tile] + both[:ROWS] + both[ROWS:]).astype(BF)


def mixed_rows(x, high, low, parts):
    return pl.pallas_call(
        mixed_kernel,
        out_shape=jax.ShapeDtypeStruct(TOKENS, BF),
        in_specs=[ANY] * 6,
        out_specs=pl.BlockSpec(memory_space=pltpu.VMEM),
        scratch_shapes=[
            pltpu.VMEM(TOKENS, F32),
            pltpu.VMEM((2 * ROWS, SLOTS), BF),
            pltpu.VMEM(WIDE, BF),
            pltpu.SemaphoreType.DMA((6,)),
        ],
        compiler_params=pltpu.CompilerParams(vmem_limit_bytes=VMEM_BYTES),
        name="mixed",
    )(x, high, low, *parts)


def local(
    tokens, cotangent, lengths, routes, norm_attn, w_query, key_projection, value_projection,
    w_out, norm_ffn, w_router, w_gate, w_up, w_down,
):
    me_dp = lax.axis_index("dp").astype(jnp.int32).reshape(1)
    me_expert = lax.axis_index("expert").astype(jnp.int32).reshape(1)
    tables = seq_tables(lengths[0])
    give = [slot_matrix(routes[l]) for l in range(LAYERS)]
    take = [g.T for g in give]
    give_parts = slot_matrix(routes[1], True)
    experts = (w_gate, w_up, w_down)

    def gather(values):
        return lax.all_gather(values, "dp", axis=0, tiled=True)

    weights = (w_query, key_projection, value_projection, w_out, w_router, norm_attn, norm_ffn)
    shard0, out_shard0 = pack(0, *weights)
    w = [gather(shard0), gather(pack(1, *weights)[0])]
    out_ring = [me_dp, *ring(out_shard0)]

    dx_rows = exchange(dot(take[1], cotangent).astype(BF))

    kept0 = attn_forward(
        tokens, None, w[0], out_ring, tables, take[0], give[0],
        (dx_rows, give[1], give_parts, me_expert),
    )
    received0 = exchange(kept0["rows"])
    act0, slope0, hidden0, out0 = experts_forward(received0, experts, ())
    returned0 = exchange(out0)
    columns0 = gather(kept0["columns"])

    kept1 = attn_forward(
        kept0["after"], (kept0["high"], kept0["low"], returned0), w[1], None, tables, take[1],
        give_parts, (),
    )
    received1 = exchange(kept1["rows"])
    columns1 = gather(kept1["columns"])
    hidden1, *parts, dslot1, dgate1, dup1, back1 = experts_both(
        me_expert, received1, dx_rows, w[1], experts, ()
    )
    back1 = exchange(back1)
    grads1 = expert_grads(received1, dgate1, dup1, hidden1, dslot1)
    turned0, turned1 = turn_columns(me_dp, columns0), turn_columns(me_dp, columns1)
    parts[0] = exchange(after(parts[0], grads1, turned0, turned1))

    dx0, packed1, rows0 = attn_backward(
        cotangent, back1, kept1["x"], kept1, w[1], None, tables, give[1], (take[0], kept0["router"]),
        None, (),
    )
    packed1 = after(packed1, parts[0])
    dslot0 = exchange(rows0)
    factors1 = gather(packed1)
    shares1 = lax.psum_scatter(after(grads1, packed1), "dp", scatter_dimension=0, tiled=True)
    dgate0, dup0, back0 = experts_backward(dslot0, act0, slope0, experts, ())
    back0 = exchange(back0)
    grads0 = expert_grads(received0, dgate0, dup0, hidden0, dslot0)
    parts[1] = exchange(parts[1])
    pieces1 = dense_grads(me_dp, turned1, factors1, (parts[1],))
    parts[2] = exchange(after(parts[2], grads0, pieces1))
    grad_tokens, packed0 = attn_backward(
        dx0, back0, tokens, kept0, w[0], out_ring, tables, give[0], None, returned0,
        (shares1,),
    )
    factors0 = gather(after(packed0, parts[2]))
    summed1 = sum_pieces(to_expert_peers(pieces1), CHUNKS)
    shares0 = lax.psum_scatter(after(grads0, summed1), "dp", scatter_dimension=0, tiled=True)
    mixed = mixed_rows(kept1["after"], kept1["high"], kept1["low"], parts)
    pieces1 = to_expert_peers(summed1)
    pieces0 = dense_grads(me_dp, turned0, factors0, ())
    pieces0 = to_expert_peers(after(pieces0, pieces1))
    pieces0 = to_expert_peers(sum_pieces(pieces0, CHUNKS))

    dense = (w_query, key_projection, value_projection)
    above = finish(1, pieces1, dense, norm_attn, None)
    query, key, value, out, gain_attn, gain_ffn, router = finish(
        0, pieces0, dense, norm_attn, above
    )
    gate, up, down = finish_experts(shares0, shares1)
    return (
        mixed, grad_tokens, gain_attn, query, key, value, out, gain_ffn,
        router.transpose(0, 2, 1), gate, up, down,
    )


def solution(mesh):
    placed = (
        P(("dp", "expert"), None),
        P(("dp", "expert"), None),
        P(("dp", "expert"), None),
        P(None, ("dp", "expert"), None),
        P(None, "dp"),
        P(None, "dp", None),
        P(None, "dp", None),
        P(None, "dp", None),
        P(None, "dp", None),
        P(None, "dp"),
        P(None, "dp", None),
        P(None, "expert", None, None),
        P(None, "expert", None, None),
        P(None, "expert", None, None),
    )
    return jax.shard_map(
        local,
        mesh=mesh,
        in_specs=placed,
        out_specs=(
            P(("dp", "expert"), None),
            P(("dp", "expert"), None),
            P(None, "dp"),
            P(None, "dp", None),
            P(None, "dp", None),
            P(None, "dp", None),
            P(None, "dp", None),
            P(None, "dp"),
            P(None, "dp", None),
            P(None, "expert", "dp", None),
            P(None, "expert", "dp", None),
            P(None, "expert", "dp", None),
        ),
        check_vma=False,
    )
```

profile of v0, /device:TPU:0, one launch (start us, length us, event | category | flops | bytes accessed | tf_op | source)
XLA Modules:
  0.0 528.0 jit_solution(6840234664576738462)
XLA Ops:
  21.4 7.1 %all-to-all-start = ((bf16[16,48,1536]{2,1,0:T(8,128)(2,1)}), bf16[16,48,1536]{2,1,0:T(8,128)(2,1)S(1)}, u32[]{:S(2)}, u32[]{:S(2)}) async-start(bf16[16,48,1536]{2,1,0:T(8,128)(2,1)} %bitcast.9), calls=%async_computation | async-start | bytes 4718592 | tf_op jit(solution)/shard_map/all_to_all | solution.py:785
  49.7 7.2 %collective-permute-done.3.refs_12_.refs_19_ = bf16[96,1536]{1,0:T(8,128)(2,1)} collective-permute-done((bf16[96,1536]{1,0:T(8,128)(2,1)}, bf16[96,1536]{1,0:T(8,128)(2,1)}, u32[]{:S(2)}, u32[]{:S(2)}) %collective-permute-start.3) | collective-permute-done | bytes 294944 | tf_op jit(solution)/shard_map/ppermute | solution.py:739
  69.6 8.7 %attn_forward.2 = (bf16[128,4608]{1,0:T(8,128)(2,1)}, bf16[12,128,128]{2,1,0:T(8,128)(2,1)}, bf16[2,128,128]{2,1,0:T(8,128)(2,1)}, bf16[2,128,128]{2,1,0:T(8,128...) custom-call(bf16[128,1536]{1,0:T(8,128)(2,1)} %refs_8_.1, ...), custom_call_target="tpu_custom_call" | custom-call | flops 1459617792 | bytes 20971520 | tf_op jit(solution)/shard_map/attn_forward/pallas_call | solution.py:263
  78.3 39.0 %all_to_all.70 = bf16[16,48,1536]{2,1,0:T(8,128)(2,1)} all-to-all(bf16[16,48,1536]{2,1,0:T(8,128)(2,1)} %bitcast.72), channel_id=1, replica_groups=mesh['dp'=8,'expert'=16] {'expert'}, dimensions={0} | all-to-all | bytes 4718592 | tf_op jit(solution)/shard_map/all_to_all | solution.py:785
  117.3 10.8 %experts_forward.1 = (bf16[768,768]{1,0:T(8,128)(2,1)}, bf16[768,768]{1,0:T(8,128)(2,1)}, bf16[768,768]{1,0:T(8,128)(2,1)}, bf16[768,1536]{1,0:T(8,128)(2,1)}) custom-call(bf16[768,1536]{1,0:T(8,128)(2,1)} %bitcast.65, bf16[2,1,1536,768]{3,2,1,0:T(8,128)(2,1)} %refs_3_.9, bf16[2,1,1536,768]{3,2,1,0:T(8,128)(2,1)} %refs_4_.5, bf16[2,1,768,1536]{3,2,1,0:T(8,128)(2,1)} %refs_5_.7), custom_call_target="tpu_custom_call" | custom-call | flops 5435817984 | bytes 20971520 | tf_op jit(solution)/shard_map/experts_forward/pallas_call | solution.py:478
  132.9 33.6 %all-to-all-done.2 = bf16[16,48,1536]{2,1,0:T(8,128)(2,1)S(1)} async-done(((bf16[16,48,1536]{2,1,0:T(8,128)(2,1)}), bf16[16,48,1536]{2,1,0:T(8,128)(2,1)S(1)}, u32[]{:S(2)}, u32[]{:S(2)}) %all-to-all-start.2) | async-done | bytes 2359328 | tf_op jit(solution)/shard_map/all_to_all | solution.py:785
  167.8 11.7 %attn_forward.3 = (bf16[128,4608]{1,0:T(8,128)(2,1)}, bf16[12,128,128]{2,1,0:T(8,128)(2,1)}, bf16[2,128,128]{2,1,0:T(8,128)(2,1)}, bf16[2,128,128]{2,1,0:T(8,128...) custom-call(f32[128,1536]{1,0:T(8,128)} %get-tuple-element.72.refs_0, ...), custom_call_target="tpu_custom_call" | custom-call | flops 1459617792 | bytes 20971520 | tf_op jit(solution)/shard_map/attn_forward/pallas_call | solution.py:263
  179.6 35.6 %all_to_all.71 = bf16[16,48,1536]{2,1,0:T(8,128)(2,1)} all-to-all(bf16[16,48,1536]{2,1,0:T(8,128)(2,1)} %bitcast.71), channel_id=1, replica_groups=mesh['dp'=8,'expert'=16] {'expert'}, dimensions={0} | all-to-all | bytes 4718592 | tf_op jit(solution)/shard_map/all_to_all | solution.py:785
  215.2 17.8 %experts_both.1 = (bf16[768,768]{1,0:T(8,128)(2,1)}, bf16[16,16,1536]{2,1,0:T(8,128)(2,1)}, bf16[16,16,1536]{2,1,0:T(8,128)(2,1)}, bf16[16,16,1536]{2,1,0:T(8,12...) custom-call(s32[1]{0:T(128)} %bitcast.11.refs_21_.refs_0_, ...), custom_call_target="tpu_custom_call" | custom-call | flops 10871635968 | bytes 20971520 | tf_op jit(solution)/shard_map/experts_both/pallas_call | solution.py:478
  237.0 10.8 %expert_grads.2 = bf16[8,288,1536]{2,1,0:T(8,128)(2,1)} custom-call(bf16[768,1536]{1,0:T(8,128)(2,1)} %bitcast.74, bf16[768,768]{1,0:T(8,128)(2,1)} %get-tuple-element.82.dgate_pre, bf16[768,768]{1,0:T(8,128)(2,1)} %get-tuple-element.83.dup_pre, bf16[768,768]{1,0:T(8,128)(2,1)} %get-tuple-element.84.hidden, bf16[768,1536]{1,0:T(8,128)(2,1)} %get-tuple-element.85.dslot), custom_call_target="tpu_custom_call" | custom-call | flops 5435817984 | bytes 14680064 | tf_op jit(solution)/shard_map/expert_grads/pallas_call | solution.py:672
  252.8 17.6 %all-to-all-done.6 = bf16[16,48,1664]{2,1,0:T(8,128)(2,1)S(1)} async-done(((bf16[16,48,1664]{2,1,0:T(8,128)(2,1)}), bf16[16,48,1664]{2,1,0:T(8,128)(2,1)S(1)}, u32[]{:S(2)}, u32[]{:S(2)}) %all-to-all-start.6) | async-done | bytes 2555936 | tf_op jit(solution)/shard_map/all_to_all | solution.py:785
  274.1 14.6 %attn_backward.2 = (f32[128,1536]{1,0:T(8,128)}, bf16[128,3712]{1,0:T(8,128)(2,1)}, bf16[768,1536]{1,0:T(8,128)(2,1)}) custom-call(bf16[128,1536]{1,0:T(8,128)(2,1)} %refs_0_.7, bf16[768,1664]{1,0:T(8,128)(2,1)} %bitcast.53, bf16[1536,3712]{1,0:T(8,128)(2,1)} %all-gather.9.cloned.1.call-done.refs_1_.refs_3_.refs_2_, ...), custom_call_target="tpu_custom_call" | custom-call | flops 1459617792 | bytes 20971520 | tf_op jit(solution)/shard_map/attn_backward/pallas_call | solution.py:263
  291.3 37.5 %all_to_all.72 = bf16[16,48,1536]{2,1,0:T(8,128)(2,1)} all-to-all(bf16[16,48,1536]{2,1,0:T(8,128)(2,1)S(1)} %bitcast.67), channel_id=1, replica_groups=mesh['dp'=8,'expert'=16] {'expert'}, dimensions={0} | all-to-all | bytes 4718592 | tf_op jit(solution)/shard_map/all_to_all | solution.py:785
  332.6 11.2 %experts_backward.1 = (bf16[768,768]{1,0:T(8,128)(2,1)}, bf16[768,768]{1,0:T(8,128)(2,1)}, bf16[768,1536]{1,0:T(8,128)(2,1)}) custom-call(bf16[768,1536]{1,0:T(8,128)(2,1)} %bitcast.69, bf16[768,768]{1,0:T(8,128)(2,1)} %get-tuple-element.99.refs_1_, bf16[768,768]{1,0:T(8,128)(2,1)} %get-tuple-element.100.refs_2_, bf16[2,1,1536,768]{3,2,1,0:T(8,128)(2,1)} %refs_3_.9, ...), custom_call_target="tpu_custom_call" | custom-call | flops 5435817984 | bytes 20971520 | tf_op jit(solution)/shard_map/experts_backward/pallas_call | solution.py:478
  345.8 6.2 %all-to-all-start.9 = ((bf16[16,48,1536]{2,1,0:T(8,128)(2,1)}), bf16[16,48,1536]{2,1,0:T(8,128)(2,1)S(1)}, u32[]{:S(2)}, u32[]{:S(2)}) async-start(bf16[16,48,1536]{2,1,0:T(8,128)(2,1)} %bitcast.68), calls=%async_computation.9 | async-start | bytes 4718592 | tf_op jit(solution)/shard_map/all_to_all | solution.py:785
  352.0 10.8 %expert_grads.3 = bf16[8,288,1536]{2,1,0:T(8,128)(2,1)} custom-call(bf16[768,1536]{1,0:T(8,128)(2,1)} %bitcast.66, bf16[768,768]{1,0:T(8,128)(2,1)} %get-tuple-element.101.dgate_pre, bf16[768,768]{1,0:T(8,128)(2,1)} %get-tuple-element.102.dup_pre, bf16[768,768]{1,0:T(8,128)(2,1)} %get-tuple-element.103.hidden, bf16[768,1536]{1,0:T(8,128)(2,1)} %bitcast.70), custom_call_target="tpu_custom_call" | custom-call | flops 5435817984 | bytes 14680064 | tf_op jit(solution)/shard_map/expert_grads/pallas_call | solution.py:672
  362.8 8.9 %dense_grads.2.refs_2_ = bf16[16,192,256]{2,1,0:T(8,128)(2,1)} custom-call(s32[1]{0:T(128)} %bitcast.7.refs_7_.me.refs_0_.refs_14_, bf16[3,256,1024]{2,1,0:T(8,128)(2,1)} %turn_columns.3.refs_3_.refs_1_, bf16[1024,3712]{1,0:T(8,128)(2,1)} %all-gather.15.cloned.1.call-done.refs_2_, bf16[256,1536]{1,0:T(8,128)(2,1)} %bitcast.57), custom_call_target="tpu_custom_call" | custom-call | flops 1946157056 | bytes 10485760 | tf_op jit(solution)/shard_map/dense_grads/pallas_call | solution.py:893
  371.7 10.5 %all-to-all-done.9 = bf16[16,48,1536]{2,1,0:T(8,128)(2,1)S(1)} async-done(((bf16[16,48,1536]{2,1,0:T(8,128)(2,1)}), bf16[16,48,1536]{2,1,0:T(8,128)(2,1)S(1)}, u32[]{:S(2)}, u32[]{:S(2)}) %all-to-all-start.9) | async-done | bytes 2359328 | tf_op jit(solution)/shard_map/all_to_all | solution.py:785
  386.2 13.5 %attn_backward.3 = (f32[128,1536]{1,0:T(8,128)}, bf16[128,3712]{1,0:T(8,128)(2,1)}) custom-call(f32[128,1536]{1,0:T(8,128)} %get-tuple-element.105.refs_0_, bf16[768,1536]{1,0:T(8,128)(2,1)} %bitcast.54, bf16[1536,2176]{1,0:T(8,128)(2,1)} %all-gather.7.cloned.1.call-done.refs_1_.refs_2_, f32[128,128]{1,0:T(8,128)} %get-tuple-element.137.refs_2_.refs_3_, ...), custom_call_target="tpu_custom_call" | custom-call | flops 1459617792 | bytes 20971520 | tf_op jit(solution)/shard_map/attn_backward/pallas_call | solution.py:263
  401.4 29.3 %all_to_all.74.pieces_hbm = bf16[16,192,256]{2,1,0:T(8,128)(2,1)} all-to-all(bf16[16,192,256]{2,1,0:T(8,128)(2,1)S(1)} %copy-done.2), channel_id=1, replica_groups=mesh['dp'=8,'expert'=16] {'expert'}, dimensions={0} | all-to-all | bytes 3145728 | tf_op jit(solution)/shard_map/all_to_all | solution.py:915
  437.3 9.1 %all-gather.17.cloned.1.call-done.refs_2_ = bf16[1024,3712]{1,0:T(8,128)(2,1)} async-done(((bf16[128,3712]{1,0:T(8,128)(2,1)}), bf16[1024,3712]{1,0:T(8,128)(2,1)}) %all-gather.17.cloned.1.call-update) | async-done | bytes 7602192 | tf_op jit(solution)/shard_map/all_gather | solution.py:1093
  446.5 8.9 %dense_grads.3.refs_0_ = bf16[16,192,256]{2,1,0:T(8,128)(2,1)} custom-call(s32[1]{0:T(128)} %bitcast.7.refs_7_.me.refs_0_.refs_14_, bf16[3,256,1024]{2,1,0:T(8,128)(2,1)} %turn_columns.2.refs_2_.refs_1_, bf16[1024,3712]{1,0:T(8,128)(2,1)} %all-gather.17.cloned.1.call-done.refs_2_), custom_call_target="tpu_custom_call" | custom-call | flops 1946157056 | bytes 10485760 | tf_op jit(solution)/shard_map/dense_grads/pallas_call | solution.py:893
  460.1 26.6 %all_to_all.73.pieces_hbm = bf16[16,192,256]{2,1,0:T(8,128)(2,1)} all-to-all(bf16[16,192,256]{2,1,0:T(8,128)(2,1)} %after.12), channel_id=1, replica_groups=mesh['dp'=8,'expert'=16] {'expert'}, dimensions={0} | all-to-all | bytes 3145728 | tf_op jit(solution)/shard_map/all_to_all | solution.py:915
  504.6 10.7 %all-to-all-done.13.refs_0_ = bf16[16,192,256]{2,1,0:T(8,128)(2,1)S(1)} async-done(((bf16[16,192,256]{2,1,0:T(8,128)(2,1)}), bf16[16,192,256]{2,1,0:T(8,128)(2,1)S(1)}, u32[]{:S(2)}, u32[]{:S(2)}) %all-to-all-start.13) | async-done | bytes 1572896 | tf_op jit(solution)/shard_map/all_to_all | solution.py:915
  (141 shorter events, 115.3 us)
Async XLA Ops:
  7.2 62.4 %all-gather.7.cloned.1.call-start = ((), (), s32[]{:S(2)}) async-start(), calls=%async_computation.16 | async-start | bytes 7520256 | tf_op jit(solution)/shard_map/all_gather | solution.py:1093
  10.3 156.2 %all-gather.9.cloned.1.call-start = ((), (), s32[]{:S(2)}) async-start(), calls=%async_computation.17 | async-start | bytes 12828672 | tf_op jit(solution)/shard_map/all_gather | solution.py:1093
  13.6 51.0 %collective-permute-start.4 = (bf16[192,1536]{1,0:T(8,128)(2,1)}, bf16[192,1536]{1,0:T(8,128)(2,1)}, u32[]{:S(2)}, u32[]{:S(2)}) collective-permute-start(bf16[192,1536]{1,0:T(8,128)(2,1)} %get-tuple-element.71.refs_8_.refs_15_), channel_id=1, source_target_pairs={{0,16},{16,0},{32,48},{48,32},{64,80},{80,64},{96,112},{112,96},{1... | collective-permute-start | bytes 1769480 | tf_op jit(solution)/shard_map/ppermute | solution.py:746
  13.6 25.5 %collective-permute-start.1 = (bf16[192,1536]{1,0:T(8,128)(2,1)}, bf16[192,1536]{1,0:T(8,128)(2,1)S(1)}, u32[]{:S(2)}, u32[]{:S(2)}) collective-permute-start(bf16[192,1536]{1,0:T(8,128)(2,1)} %get-tuple-element.71.refs_8_.refs_15_), channel_id=1, source_target_pairs={{0,96},{16,112},{32,0},{48,16},{64,32},{80,48},{96,64},{112,80},{1... | collective-permute-start | bytes 1769480 | tf_op jit(solution)/shard_map/ppermute | solution.py:739
  17.8 25.6 %collective-permute-start = (bf16[192,1536]{1,0:T(8,128)(2,1)}, bf16[192,1536]{1,0:T(8,128)(2,1)S(1)}, u32[]{:S(2)}, u32[]{:S(2)}) collective-permute-start(bf16[192,1536]{1,0:T(8,128)(2,1)} %get-tuple-element.71.refs_8_.refs_15_), channel_id=1, source_target_pairs={{0,32},{16,48},{32,64},{48,80},{64,96},{80,112},{96,0},{112,16},{1... | collective-permute-start | bytes 1769480 | tf_op jit(solution)/shard_map/ppermute | solution.py:739
  21.4 44.5 %all-to-all-start = ((bf16[16,48,1536]{2,1,0:T(8,128)(2,1)}), bf16[16,48,1536]{2,1,0:T(8,128)(2,1)S(1)}, u32[]{:S(2)}, u32[]{:S(2)}) async-start(bf16[16,48,1536]{2,1,0:T(8,128)(2,1)} %bitcast.9), calls=%async_computation | async-start | bytes 4718592 | tf_op jit(solution)/shard_map/all_to_all | solution.py:785
  28.5 219.3 %all-gather.11.cloned.1.call-start = ((), (), s32[]{:S(2)}) async-start(), calls=%async_computation.18 | async-start | bytes 10616832 | tf_op jit(solution)/shard_map/all_gather | solution.py:1093
  40.0 16.9 %collective-permute-start.3 = (bf16[96,1536]{1,0:T(8,128)(2,1)}, bf16[96,1536]{1,0:T(8,128)(2,1)}, u32[]{:S(2)}, u32[]{:S(2)}) collective-permute-start(bf16[96,1536]{1,0:T(8,128)(2,1)} %slice.18), channel_id=1, source_target_pairs={{0,96},{16,112},{32,0},{48,16},{64,32},{80,48},{96,64},{112,80},{1... | collective-permute-start | bytes 884744 | tf_op jit(solution)/shard_map/ppermute | solution.py:739
  44.2 17.1 %collective-permute-start.2 = (bf16[96,1536]{1,0:T(8,128)(2,1)}, bf16[96,1536]{1,0:T(8,128)(2,1)}, u32[]{:S(2)}, u32[]{:S(2)}) collective-permute-start(bf16[96,1536]{1,0:T(8,128)(2,1)} %slice.17), channel_id=1, source_target_pairs={{0,32},{16,48},{32,64},{48,80},{64,96},{80,112},{96,0},{112,16},{1... | collective-permute-start | bytes 884744 | tf_op jit(solution)/shard_map/ppermute | solution.py:739
  44.2 20.4 %collective-permute-start.6 = (bf16[192,1536]{1,0:T(8,128)(2,1)S(1)}, bf16[192,1536]{1,0:T(8,128)(2,1)}, u32[]{:S(2)}, u32[]{:S(2)}) collective-permute-start(bf16[192,1536]{1,0:T(8,128)(2,1)S(1)} %collective-permute-done.1.refs_10_.refs_17_), channel_id=1, source_target_pairs={{0,16},{16,0},{32,48},{48,32},{64,80},{80,64},{96,112},{112,96},{1... | collective-permute-start | bytes 1769480 | tf_op jit(solution)/shard_map/ppermute | solution.py:746
  44.2 21.8 %collective-permute-start.5 = (bf16[192,1536]{1,0:T(8,128)(2,1)S(1)}, bf16[192,1536]{1,0:T(8,128)(2,1)}, u32[]{:S(2)}, u32[]{:S(2)}) collective-permute-start(bf16[192,1536]{1,0:T(8,128)(2,1)S(1)} %collective-permute-done.refs_9_.refs_16_), channel_id=1, source_target_pairs={{0,16},{16,0},{32,48},{48,32},{64,80},{80,64},{96,112},{112,96},{1... | collective-permute-start | bytes 1769480 | tf_op jit(solution)/shard_map/ppermute | solution.py:746
  128.1 38.3 %all-to-all-start.2 = ((bf16[16,48,1536]{2,1,0:T(8,128)(2,1)}), bf16[16,48,1536]{2,1,0:T(8,128)(2,1)S(1)}, u32[]{:S(2)}, u32[]{:S(2)}) async-start(bf16[16,48,1536]{2,1,0:T(8,128)(2,1)} %bitcast.75), calls=%async_computation.2 | async-start | bytes 4718592 | tf_op jit(solution)/shard_map/all_to_all | solution.py:785
  132.0 118.3 %all-gather.13.cloned.1.call-start = ((), (), s32[]{:S(2)}) async-start(), calls=%async_computation.19 | async-start | bytes 10616832 | tf_op jit(solution)/shard_map/all_gather | solution.py:1093
  233.0 37.4 %all-to-all-start.6 = ((bf16[16,48,1664]{2,1,0:T(8,128)(2,1)}), bf16[16,48,1664]{2,1,0:T(8,128)(2,1)S(1)}, u32[]{:S(2)}, u32[]{:S(2)}) async-start(bf16[16,48,1664]{2,1,0:T(8,128)(2,1)} %bitcast.64), calls=%async_computation.6 | async-start | bytes 5111808 | tf_op jit(solution)/shard_map/all_to_all | solution.py:785
  270.4 18.3 %all-to-all-start.4 = ((bf16[16,16,1536]{2,1,0:T(8,128)(2,1)}), bf16[16,16,1536]{2,1,0:T(8,128)(2,1)S(1)}, u32[]{:S(2)}, u32[]{:S(2)}) async-start(bf16[16,16,1536]{2,1,0:T(8,128)(2,1)} %after.7), calls=%async_computation.4 | async-start | bytes 1572864 | tf_op jit(solution)/shard_map/all_to_all | solution.py:785
  274.1 88.7 %all-gather.15.cloned.1.call-start = ((), (), s32[]{:S(2)}) async-start(), calls=%async_computation.20 | async-start | bytes 8552448 | tf_op jit(solution)/shard_map/all_gather | solution.py:1093
  289.6 96.6 %reduce-scatter.3.cloned.1.call-start = ((), (), s32[]{:S(2)}) async-start(), calls=%async_computation.21 | async-start | bytes 7962624 | tf_op jit(solution)/shard_map/reduce_scatter | solution.py:1132
  328.8 16.1 %all-to-all-start.5 = ((bf16[16,16,1536]{2,1,0:T(8,128)(2,1)}), bf16[16,16,1536]{2,1,0:T(8,128)(2,1)S(1)}, u32[]{:S(2)}, u32[]{:S(2)}) async-start(bf16[16,16,1536]{2,1,0:T(8,128)(2,1)} %get-tuple-element.88), calls=%async_computation.5 | async-start | bytes 1572864 | tf_op jit(solution)/shard_map/all_to_all | solution.py:785
  345.8 36.4 %all-to-all-start.9 = ((bf16[16,48,1536]{2,1,0:T(8,128)(2,1)}), bf16[16,48,1536]{2,1,0:T(8,128)(2,1)S(1)}, u32[]{:S(2)}, u32[]{:S(2)}) async-start(bf16[16,48,1536]{2,1,0:T(8,128)(2,1)} %bitcast.68), calls=%async_computation.9 | async-start | bytes 4718592 | tf_op jit(solution)/shard_map/all_to_all | solution.py:785
  382.2 17.5 %all-to-all-start.8 = ((bf16[16,16,1536]{2,1,0:T(8,128)(2,1)}), bf16[16,16,1536]{2,1,0:T(8,128)(2,1)S(1)}, u32[]{:S(2)}, u32[]{:S(2)}) async-start(bf16[16,16,1536]{2,1,0:T(8,128)(2,1)} %after.9), calls=%async_computation.8 | async-start | bytes 1572864 | tf_op jit(solution)/shard_map/all_to_all | solution.py:785
  385.8 60.6 %all-gather.17.cloned.1.call-start = ((), (), s32[]{:S(2)}) async-start(), calls=%async_computation.22 | async-start | bytes 8552448 | tf_op jit(solution)/shard_map/all_gather | solution.py:1093
  400.7 100.6 %reduce-scatter.5.cloned.1.call-start = ((), (), s32[]{:S(2)}) async-start(), calls=%async_computation.23 | async-start | bytes 7962624 | tf_op jit(solution)/shard_map/reduce_scatter | solution.py:1145
  433.6 25.4 %all-to-all-start.11 = ((bf16[16,192,256]{2,1,0:T(8,128)(2,1)}), bf16[16,192,256]{2,1,0:T(8,128)(2,1)S(1)}, u32[]{:S(2)}, u32[]{:S(2)}) async-start(bf16[16,192,256]{2,1,0:T(8,128)(2,1)} %sum_pieces.2.refs_1_), calls=%async_computation.12 | async-start | bytes 3145728 | tf_op jit(solution)/shard_map/all_to_all | solution.py:915
  489.6 25.7 %all-to-all-start.13 = ((bf16[16,192,256]{2,1,0:T(8,128)(2,1)}), bf16[16,192,256]{2,1,0:T(8,128)(2,1)S(1)}, u32[]{:S(2)}, u32[]{:S(2)}) async-start(bf16[16,192,256]{2,1,0:T(8,128)(2,1)} %sum_pieces.3), calls=%async_computation.14 | async-start | bytes 3145728 | tf_op jit(solution)/shard_map/all_to_all | solution.py:915
  (24 other events, 122.9 us)
Sparse Core Ops, SparseCore 0:
  10.4 59.1 all-gather.6
  71.3 61.4 all-gather.8
  135.1 54.5 all-gather.10
  191.2 54.4 all-gather.12
  289.7 45.6 all-gather.14
  337.7 46.3 reduce-scatter.2
  400.8 45.6 all-gather.16
  448.9 46.3 reduce-scatter.4
where the time goes:
time: 537 us; the launch traced here: 528 us
  blocking collectives  168 us (31%)
  Pallas kernels  160 us (30%)
  waiting for transfers between devices  102 us (19%)
  starting transfers between devices  48.4 us (9%)
  between operations  15.1 us (3%)
  local copies, waits for them, and re-layouts  14.3 us (3%)
  other arithmetic  10.3 us (2%)
  matrix products  9.81 us (2%)
    all_to_all x3, blocking collectives, exchange(): lax.all_to_all(rows.reshape(EXPERTS, -1, width), 'expert', split_axis=0,...  112 us
    all_to_all x7, waiting for transfers between devices, exchange(): lax.all_to_all(rows.reshape(EXPERTS, -1, width), 'expert', split_axis=0,...  62.7 us
    all_to_all x2, blocking collectives, to_expert_peers(): lax.all_to_all(pieces, 'expert', split_axis=0, concat_axis=0, tiled=True)  55.9 us
    pallas_call x4, Pallas kernels, run_attn(): pl.pallas_call(body, out_shape=[sd(shape, kind) for shape, kind in outs],...  48.5 us
    pallas_call x3, Pallas kernels, run_experts(): pl.pallas_call(body, out_shape=[sd(shape, BF) for shape in outs], in_spec...  39.7 us
    all_to_all x7, starting transfers between devices, exchange(): lax.all_to_all(rows.reshape(EXPERTS, -1, width), 'expert', split_axis=0,...  32.1 us
    pallas_call x2, Pallas kernels, expert_grads(): pl.pallas_call(expert_grads_kernel, grid=(2,), out_shape=jax.ShapeDtypeSt...  21.6 us
    pallas_call x2, Pallas kernels, dense_grads(): pl.pallas_call(body, out_shape=jax.ShapeDtypeStruct((CHUNKS, SHARD, CHUNK...  17.8 us
  transfers between devices with their start and end apart: 26, of which 10 were waited for; matrix products, arithmetic and copies ran while one was open for 5% of the time, Pallas kernels for 29%

commit v1 on v0

--- a/solution.py
+++ b/solution.py
@@ -318,23 +318,31 @@
      small_in, datt, dx_out, packed), scratch = scratch[:18], scratch[18:]
     if last:
         rows, scratch = scratch[0], scratch[1:]
+    else:
+        turned, scratch = scratch[0], scratch[1:]
     in_sems, out_sems = scratch
     pairs = [(give_hbm, give), (back_hbm, back), (router_hbm, router), (dx_hbm, dx_in)]
     if not last:
         pairs += [(ins[0], wide_in)]
     pairs += [small_block(w_hbm, w), (after_hbm, after)]
     if last:
+        out_pairs, qkv_pairs = [], []
         for at in range(0, WIDTH, TILE):
             block = (pl.ds(at, TILE), pl.ds(QKV, WIDTH))
-            pairs += [(w_hbm.at[block], w.at[block])]
+            out_pairs += [(w_hbm.at[block], w.at[block])]
+            block = (pl.ds(at, TILE), pl.ds(0, QKV))
+            qkv_pairs += [(w_hbm.at[block], w.at[block])]
     else:
-        pairs += ring_blocks(ins[1][0], ins[2:], w)
-    pairs += [(probs_hbm, probs), (value_hbm, value), (krot_hbm, krot), (qrot_hbm, qrot)]
-    pairs += [(cosine_hbm, cosine), (sine_hbm, sine)]
-    for at in range(0, WIDTH, TILE):
-        block = (pl.ds(at, TILE), pl.ds(0, QKV))
-        pairs += [(w_hbm.at[block], w.at[block])]
-    pairs += [(x_hbm, x_in)]
+        columns = [(slice(None), pl.ds(at, TILE)) for at in range(0, WIDTH, TILE)]
+        out_pairs = [
+            (ins[1].at[pl.ds(QKV, WIDTH)].at[c], turned.at[pl.ds(QKV, WIDTH)].at[c])
+            for c in columns
+        ]
+        qkv_pairs = [
+            (ins[1].at[pl.ds(0, QKV)].at[c], turned.at[pl.ds(0, QKV)].at[c]) for c in columns
+        ]
+    pairs += out_pairs + [(probs_hbm, probs), (value_hbm, value), (krot_hbm, krot), (qrot_hbm, qrot)]
+    pairs += [(cosine_hbm, cosine), (sine_hbm, sine)] + qkv_pairs + [(x_hbm, x_in)]
     if last:
         pairs += [(ins[0], wide_in), (ins[1], small_in)]
     reader, writer = Reader(in_sems, pairs), Writer(out_sems)
@@ -371,12 +379,12 @@
     pieces += [jnp.zeros((HEAD - 2 * GAIN_LOW + GAIN_HIGH, HEAD), F32)]
     packed[:, SMALL:] = (dlogits.astype(F32) + jnp.concatenate(pieces, axis=0).T).astype(BF)
     writer.send(packed.at[:, QKV:], outs[1].at[:, QKV:])
-    if not last:
-        reader.take(len(ins) - 2)
     for tile in tiles(WIDTH):
+        reader.take()
         if last:
-            reader.take()
-        wide = dot(packed[:, QKV:SMALL], w[tile, QKV:SMALL], 1, 1).astype(BF)
+            wide = dot(packed[:, QKV:SMALL], w[tile, QKV:SMALL], 1, 1).astype(BF)
+        else:
+            wide = dot(packed[:, QKV:SMALL], turned[QKV:SMALL, tile]).astype(BF)
         for half in range(TILE // HEAD):
             datt[tile.start // HEAD + half] = wide[:, half * HEAD : (half + 1) * HEAD]
     reader.take(6)
@@ -401,7 +409,10 @@
     parts = []
     for tile in tiles(WIDTH):
         reader.take()
-        parts += [dot(packed[:, :QKV], w[tile, :QKV], 1, 1)]
+        if last:
+            parts += [dot(packed[:, :QKV], w[tile, :QKV], 1, 1)]
+        else:
+            parts += [dot(packed[:, :QKV], turned[:QKV, tile])]
     dacts = jnp.concatenate(parts, axis=1)
     reader.take()
     dx = dx_out[...] + norm_back(dacts, gain_attn, x_in[...].astype(F32))
@@ -419,20 +430,23 @@
     writer.finish()
 
 
-def attn_backward(dx, back, x, kept, w, ring, tables, give, below, returned, order):
+def attn_backward(dx, back, x, kept, w, turned, tables, give, below, returned, order):
     last = below is not None
     outs = [(TOKENS, F32), ((ROWS, PACKED), BF)]
     if last:
         outs += [(WIDE, BF)]
     ins = [dx, back, w, tables[0], tables[1], give, kept["router"], kept["after"], x]
     ins += [kept[n] for n in ("probs", "qrot", "krot", "value")]
-    ins += list(below) if last else [returned, *ring]
+    ins += list(below) if last else [returned, turned]
     scratch = [
-        (TOKENS, dx.dtype), (back.shape, BF), ((WIDTH, PACKED), BF), (TABLE, F32), (TABLE, F32),
+        (TOKENS, dx.dtype), (back.shape, BF), ((WIDTH, PACKED), BF),
+        (TABLE, F32), (TABLE, F32),
         ((ROWS, SLOTS), BF), (TABLE, F32), (TOKENS, F32), (TOKENS, x.dtype),
         ((QUERY_HEADS, ROWS, ROWS), F32), (HEADS, BF), (KEYS, BF), (KEYS, BF),
         ((SLOTS, ROWS), BF) if last else (WIDE, BF), (TABLE, F32), (HEADS, BF),
     ] + outs
+    if not last:
+        scratch += [((SMALL, WIDTH), BF)]
     return run_attn(
         lambda *refs: attn_backward_kernel(last, *refs), "attn_backward", ins, order, outs, scratch,
         24 + WIDTH // TILE, 12, VMEM_BYTES,
@@ -458,14 +472,13 @@
     return 0.5 * gate * (1.0 + bend), slope
 
 
-def weight_pairs(l, gate_hbm, up_hbm, down_hbm, gate_w, up_w, down_w):
+def gate_up_pairs(l, gate_hbm, up_hbm, gate_w, up_w):
     gate_up = []
     for at in range(0, FF, TILE):
         block = (slice(None), pl.ds(at, TILE))
         gate_up += [(gate_hbm.at[l, 0].at[block], gate_w.at[block])]
         gate_up += [(up_hbm.at[l, 0].at[block], up_w.at[block])]
-    down = [(down_hbm.at[l, 0], down_w)]
-    return gate_up, down
+    return gate_up
 
 
 def run_experts(kernel, name, ins, order, outs, scratch, in_copies, flops):
@@ -494,8 +507,9 @@
     received_hbm, gate_hbm, up_hbm, down_hbm, act_hbm, slope_hbm, hidden_hbm, out_hbm,
     received, gate_w, up_w, down_w, act_s, slope_s, hidden, out, in_sems, out_sems,
 ):
-    gate_up, down = weight_pairs(0, gate_hbm, up_hbm, down_hbm, gate_w, up_w, down_w)
-    copies = start_all([(received_hbm, received)] + gate_up + down, in_sems)
+    gate_up = gate_up_pairs(0, gate_hbm, up_hbm, gate_w, up_w)
+    pairs = [(received_hbm, received)] + gate_up + [(down_hbm.at[0, 0], down_w)]
+    copies = start_all(pairs, in_sems)
     writer = Writer(out_sems)
     copies.pop(0).wait()
     for tile in tiles(FF):
@@ -539,74 +553,105 @@
         writer.send(back.at[:, tile], back_hbm.at[:, tile])
 
 
+def expert_gate(me, received, small):
+    shares = router_probs(received, small)
+    lane = lax.broadcasted_iota(jnp.int32, shares.shape, 1)
+    return jnp.sum(jnp.where(lane == me, shares, 0.0), axis=-1, keepdims=True)
+
+
 def experts_both_kernel(
-    me, received_hbm, dx_hbm, w_hbm, gate_hbm, up_hbm, down_hbm,
-    hidden_hbm, part0_hbm, part1_hbm, part2_hbm, dslot_hbm, dgate_hbm, dup_hbm, back_hbm,
-    received, dx, small, gate_w, up_w, down_w, act_s, slope_s, hidden, part0, part1, part2, dslot, dgate, dup,
-    back, in_sems, out_sems,
+    me, received_hbm, product_hbm, w_hbm, gate_hbm, up_hbm,
+    hidden_hbm, dgate_hbm, dup_hbm, back_hbm,
+    received, product, small, gate_w, up_w, act_s, slope_s, hidden, dgate, dup, back,
+    in_sems, out_sems,
 ):
-    gate_up, down = weight_pairs(1, gate_hbm, up_hbm, down_hbm, gate_w, up_w, down_w)
-    pairs = [(received_hbm, received)] + gate_up
-    pairs += [(w_hbm.at[:, pl.ds(SMALL, HEAD)], small), (dx_hbm, dx)] + down
-    copies = start_all(pairs, in_sems)
-    writer = Writer(out_sems)
-    copies.pop(0).wait()
+    pairs = [(received_hbm, received)] + gate_up_pairs(1, gate_hbm, up_hbm, gate_w, up_w)
+    pairs += [small_source(w_hbm, small), (product_hbm, product)]
+    reader, writer = Reader(in_sems, pairs), Writer(out_sems)
+    reader.take()
     for tile in tiles(FF):
-        copies.pop(0).wait()
-        copies.pop(0).wait()
+        reader.take(2)
         gate = dot(received[...], gate_w[:, tile])
         up = dot(received[...], up_w[:, tile])
         act, slope = gelu_both(gate)
         act_s[:, tile] = act
         slope_s[:, tile] = slope * up
         hidden[:, tile] = (act * up).astype(BF)
-    for copy in copies:
-        copy.wait()
+    reader.take(2)
     writer.send(hidden, hidden_hbm)
-    shares = router_probs(received[...], small[...])
-    lane = lax.broadcasted_iota(jnp.int32, shares.shape, 1)
-    weight = jnp.sum(jnp.where(lane == me[0], shares, 0.0), axis=-1, keepdims=True)
+    weight = expert_gate(me[0], received[...], small[...])
     total = jnp.zeros((SLOTS, 1), F32)
-    for tile in tiles(WIDTH):
-        part = dot(hidden[...], down_w[:, tile]).astype(BF)
-        for expert in range(EXPERTS):
-            for p, target in enumerate((part0, part1, part2)):
-                at = expert * CAP + p * PART_ROWS
-                target[expert, :, tile] = part[at : at + PART_ROWS]
-        wide = dx[:, tile].astype(F32)
-        total += jnp.sum(wide * part.astype(F32), axis=-1, keepdims=True)
-        dslot[:, tile] = (weight * wide).astype(BF)
-    writer.send(part0, part0_hbm)
-    writer.send(part1, part1_hbm)
-    writer.send(part2, part2_hbm)
-    writer.send(dslot, dslot_hbm)
+    for tile in tiles(FF):
+        dhidden = product[:, tile]
+        total += jnp.sum(dhidden * hidden[:, tile].astype(F32), axis=-1, keepdims=True)
+        dhidden = weight * dhidden
+        dgate[:, tile] = (dhidden * slope_s[:, tile]).astype(BF)
+        dup[:, tile] = (dhidden * act_s[:, tile]).astype(BF)
+    writer.send(dgate, dgate_hbm)
+    writer.send(dup, dup_hbm)
     high, low = split(total)
+    lane = lax.broadcasted_iota(jnp.int32, (SLOTS, HEAD), 1)
     back[:, WIDTH:] = jnp.where(
         lane == 0, high.astype(F32), jnp.where(lane == 1, low.astype(F32), 0.0)
     ).astype(BF)
     writer.send(back.at[:, WIDTH:], back_hbm.at[:, WIDTH:])
-    for tile in tiles(FF):
-        dhidden = dot(dslot[...], down_w[tile], 1, 1)
-        dgate[:, tile] = (dhidden * slope_s[:, tile]).astype(BF)
-        dup[:, tile] = (dhidden * act_s[:, tile]).astype(BF)
-    writer.send(dgate, dgate_hbm)
-    writer.send(dup, dup_hbm)
     back_tiles(dgate, dup, gate_w, up_w, back, back_hbm, writer)
     writer.finish()
 
 
-def experts_both(me, received, dx, w, weights, order):
+def small_source(w_hbm, small):
+    return (w_hbm.at[:, pl.ds(SMALL, HEAD)], small)
+
+
+def experts_both(me, received, product, w, weights, order):
+    small = (SLOTS, FF)
+    wide = (SLOTS, WIDTH)
+    back = (SLOTS, WIDTH + HEAD)
+    return run_experts(
+        experts_both_kernel, "experts_both", [me, received, product, w, *weights[:2]], order,
+        [small, small, small, back],
+        [(wide, BF), (small, F32), ((WIDTH, HEAD), BF)] + EXPERT_SCRATCH[:2]
+        + [(small, F32), (small, F32), (small, BF), (small, BF), (small, BF), (back, BF)],
+        10, 8 * SLOTS * WIDTH * FF,
+    )
+
+
+def experts_out_kernel(
+    me, hidden_hbm, received_hbm, dx_hbm, w_hbm, down_hbm,
+    part0_hbm, part1_hbm, part2_hbm, dslot_hbm,
+    hidden, received, dx, small, down_w, part0, part1, part2, dslot, in_sems, out_sems,
+):
+    pairs = [(hidden_hbm, hidden), (down_hbm.at[1, 0], down_w), (received_hbm, received)]
+    pairs += [small_source(w_hbm, small), (dx_hbm, dx)]
+    reader, writer = Reader(in_sems, pairs), Writer(out_sems)
+    reader.take(2)
+    for tile in tiles(WIDTH):
+        out = dot(hidden[...], down_w[:, tile]).astype(BF)
+        for expert in range(EXPERTS):
+            for p, target in enumerate((part0, part1, part2)):
+                at = expert * CAP + p * PART_ROWS
+                target[expert, :, tile] = out[at : at + PART_ROWS]
+    writer.send(part0, part0_hbm)
+    writer.send(part1, part1_hbm)
+    writer.send(part2, part2_hbm)
+    reader.take(3)
+    weight = expert_gate(me[0], received[...], small[...])
+    for tile in tiles(WIDTH):
+        dslot[:, tile] = (weight * dx[:, tile].astype(F32)).astype(BF)
+    writer.send(dslot, dslot_hbm)
+    writer.finish()
+
+
+def experts_out(me, hidden, received, dx, w, down, order):
     small = (SLOTS, FF)
     wide = (SLOTS, WIDTH)
     part = (EXPERTS, PART_ROWS, WIDTH)
-    back = (SLOTS, WIDTH + HEAD)
     return run_experts(
-        experts_both_kernel, "experts_both", [me, received, dx, w, *weights], order,
-        [small, part, part, part, wide, small, small, back],
-        [(wide, BF), (wide, BF), ((WIDTH, HEAD), BF)] + EXPERT_SCRATCH
-        + [(small, F32), (small, F32), (small, BF), (part, BF), (part, BF), (part, BF),
-           (wide, BF), (small, BF), (small, BF), (back, BF)],
-        10, 12 * SLOTS * WIDTH * FF,
+        experts_out_kernel, "experts_out", [me, hidden, received, dx, w, down], order,
+        [part, part, part, wide],
+        [(small, BF), (wide, BF), (wide, BF), ((WIDTH, HEAD), BF), ((FF, WIDTH), BF)]
+        + [(part, BF)] * 3 + [(wide, BF)],
+        5, 2 * SLOTS * WIDTH * FF,
     )
 
 
@@ -652,6 +697,78 @@
         [(wide, BF), (small, BF), (small, BF)] + EXPERT_SCRATCH
         + [(small, BF), (small, BF), (wide, BF)],
         6 + 2 * WIDTH // TILE, 6 * SLOTS * WIDTH * FF,
+    )
+
+
+def on_core(core, me, ins, outs, scratch, kernel, name, above, order):
+    sd = jax.ShapeDtypeStruct
+    held = [] if above is None else list(above)
+    first_out = 1 + len(ins) + len(held) + len(order)
+
+    def body(*refs):
+        @pl.when(refs[0][0] % 2 == core)
+        def _():
+            kernel(refs[0][0], refs[1 : 1 + len(ins)], refs[first_out : first_out + len(outs)],
+                   refs[first_out + len(outs) :])
+
+    return pl.pallas_call(
+        body,
+        out_shape=[sd(shape, kind) for shape, kind in outs],
+        in_specs=[pl.BlockSpec(memory_space=pltpu.SMEM)]
+        + [ANY] * (len(ins) + len(held) + len(order)),
+        out_specs=[ANY] * len(outs),
+        input_output_aliases={1 + len(ins) + i: i for i in range(len(held))},
+        scratch_shapes=[pltpu.VMEM(shape, kind) for shape, kind in scratch]
+        + [pltpu.SemaphoreType.DMA((24,)), pltpu.SemaphoreType.DMA((24,))],
+        compiler_params=pltpu.CompilerParams(vmem_limit_bytes=VMEM_BYTES),
+        name=name,
+    )(me, *ins, *held, *order)
+
+
+def upper_product_kernel(me, ins, outs, scratch):
+    rows, down, product, in_sems, out_sems = scratch
+    pairs = [(ins[0], rows)]
+    for tile in tiles(FF):
+        block = pl.ds(tile.start, TILE)
+        pairs += [(ins[1].at[1, 0].at[block], down.at[block])]
+    reader, writer = Reader(in_sems, pairs), Writer(out_sems)
+    reader.take()
+    for tile in tiles(FF):
+        reader.take()
+        product[:, tile] = dot(rows[...], down[tile], 1, 1)
+        writer.send(product.at[:, tile], outs[0].at[:, tile])
+    writer.finish()
+
+
+def upper_product(core, me, dx_rows, w_down, above, order):
+    small = (SLOTS, FF)
+    return on_core(
+        core, me, [dx_rows, w_down], [(small, F32)], [(WIDE, BF), ((FF, WIDTH), BF), (small, F32)],
+        upper_product_kernel, "upper_product", above, order,
+    )
+
+
+def turn_weights_kernel(me, ins, outs, scratch):
+    w, turned, in_sems, out_sems = scratch
+    pairs = [column_block(ins[0], w, at) for at in range(0, QKV, TILE)] + ring_blocks(me, ins[1:], w)
+    reader, writer = Reader(in_sems, pairs), Writer(out_sems)
+    for tile in tiles(QKV):
+        reader.take()
+        turned[tile] = w[:, tile].T
+        writer.send(turned.at[tile], outs[0].at[tile])
+    reader.take(len(ins) - 1)
+    for tile in tiles(WIDTH):
+        at = slice(QKV + tile.start, QKV + tile.stop)
+        turned[at] = w[:, at].T
+        writer.send(turned.at[at], outs[0].at[at])
+    writer.finish()
+
+
+def turn_weights(core, me, w, blocks, above, order):
+    turned = ((SMALL, WIDTH), BF)
+    return on_core(
+        core, me, [w, *blocks], [turned], [((WIDTH, SMALL), BF), turned], turn_weights_kernel,
+        "turn_weights", above, order,
     )
 
 
@@ -1099,32 +1216,37 @@
 
     dx_rows = exchange(dot(take[1], cotangent).astype(BF))
 
+    product = upper_product(0, me_dp, dx_rows, w_down, None, ())
+    turned_w = turn_weights(1, me_dp, w[0], out_ring[1:], None, ())
+    product = upper_product(1, me_dp, dx_rows, w_down, product, turned_w)
     kept0 = attn_forward(
         tokens, None, w[0], out_ring, tables, take[0], give[0],
-        (dx_rows, give[1], give_parts, me_expert),
+        (*product, give[1], give_parts, me_expert),
     )
     received0 = exchange(kept0["rows"])
     act0, slope0, hidden0, out0 = experts_forward(received0, experts, ())
     returned0 = exchange(out0)
+    turned_w = turn_weights(0, me_dp, w[0], out_ring[1:], turned_w, (out0,))
     columns0 = gather(kept0["columns"])
 
     kept1 = attn_forward(
         kept0["after"], (kept0["high"], kept0["low"], returned0), w[1], None, tables, take[1],
-        give_parts, (),
+        give_parts, tuple(turned_w),
     )
     received1 = exchange(kept1["rows"])
     columns1 = gather(kept1["columns"])
-    hidden1, *parts, dslot1, dgate1, dup1, back1 = experts_both(
-        me_expert, received1, dx_rows, w[1], experts, ()
+    hidden1, dgate1, dup1, back1 = experts_both(
+        me_expert, received1, product[0], w[1], experts, ()
     )
     back1 = exchange(back1)
+    *parts, dslot1 = experts_out(me_expert, hidden1, received1, dx_rows, w[1], w_down, ())
     grads1 = expert_grads(received1, dgate1, dup1, hidden1, dslot1)
-    turned0, turned1 = turn_columns(me_dp, columns0), turn_columns(me_dp, columns1)
-    parts[0] = exchange(after(parts[0], grads1, turned0, turned1))
+    turned0 = turn_columns(me_dp, columns0)
+    parts[0] = exchange(after(parts[0], grads1, turned0))
 
     dx0, packed1, rows0 = attn_backward(
-        cotangent, back1, kept1["x"], kept1, w[1], None, tables, give[1], (take[0], kept0["router"]),
-        None, (),
+        cotangent, back1, kept1["x"], kept1, w[1], None, tables, give[1],
+        (take[0], kept0["router"]), None, (),
     )
     packed1 = after(packed1, parts[0])
     dslot0 = exchange(rows0)
@@ -1134,13 +1256,13 @@
     back0 = exchange(back0)
     grads0 = expert_grads(received0, dgate0, dup0, hidden0, dslot0)
     parts[1] = exchange(parts[1])
+    turned1 = turn_columns(me_dp, columns1)
     pieces1 = dense_grads(me_dp, turned1, factors1, (parts[1],))
     parts[2] = exchange(after(parts[2], grads0, pieces1))
     grad_tokens, packed0 = attn_backward(
-        dx0, back0, tokens, kept0, w[0], out_ring, tables, give[0], None, returned0,
-        (shares1,),
-    )
-    factors0 = gather(after(packed0, parts[2]))
+        dx0, back0, tokens, kept0, w[0], turned_w[0], tables, give[0], None, returned0, ()
+    )
+    factors0 = gather(after(packed0, parts[2], shares1))
     summed1 = sum_pieces(to_expert_peers(pieces1), CHUNKS)
     shares0 = lax.psum_scatter(after(grads0, summed1), "dp", scatter_dimension=0, tiled=True)
     mixed = mixed_rows(kept1["after"], kept1["high"], kept1["low"], parts)

time: 537 us -> 526 us (0.980)
  Pallas kernels: 160 us -> 192 us
  waiting for transfers between devices: 102 us -> 72 us
  blocking collectives: 168 us -> 153 us
    pallas_call x0 -> x4, Pallas kernels: none -> 28 us  [on_core(): pl.pallas_call(body, out_shape=[sd(shape, kind) for shape, kind in outs],...]
    all_to_all x7, waiting for transfers between devices: 62.7 us -> 36.1 us  [exchange(): lax.all_to_all(rows.reshape(EXPERTS, -1, width), 'expert', split_axis=0,...]
    all_to_all x3, blocking collectives: 112 us -> 98.3 us  [exchange(): lax.all_to_all(rows.reshape(EXPERTS, -1, width), 'expert', split_axis=0,...]
    pallas_call x3 -> x4, Pallas kernels: 39.7 us -> 45 us  [run_experts(): pl.pallas_call(body, out_shape=[sd(shape, BF) for shape in outs], in_spec...]
  transfers between devices with their start and end apart: 26 -> 26, of which waited for: 10 -> 11; matrix products, arithmetic and copies ran while one was open for 5% -> 5% of each run, Pallas kernels for 29% -> 36%
where the time goes in v1:
time: 526 us; the launch traced here: 516 us
  Pallas kernels  192 us (37%)
  blocking collectives  153 us (29%)
  waiting for transfers between devices  72 us (14%)
  starting transfers between devices  49.7 us (9%)
  between operations  14.9 us (3%)
  local copies, waits for them, and re-layouts  13.7 us (3%)
  other arithmetic  10.3 us (2%)
  matrix products  9.81 us (2%)
    all_to_all x3, blocking collectives, exchange(): lax.all_to_all(rows.reshape(EXPERTS, -1, width), 'expert', split_axis=0,...  98.3 us
    all_to_all x2, blocking collectives, to_expert_peers(): lax.all_to_all(pieces, 'expert', split_axis=0, concat_axis=0, tiled=True)  54.5 us
    pallas_call x4, Pallas kernels, run_attn(): pl.pallas_call(body, out_shape=[sd(shape, kind) for shape, kind in outs],...  47.8 us
    pallas_call x4, Pallas kernels, run_experts(): pl.pallas_call(body, out_shape=[sd(shape, BF) for shape in outs], in_spec...  45 us
    all_to_all x7, waiting for transfers between devices, exchange(): lax.all_to_all(rows.reshape(EXPERTS, -1, width), 'expert', split_axis=0,...  36.1 us
    all_to_all x7, starting transfers between devices, exchange(): lax.all_to_all(rows.reshape(EXPERTS, -1, width), 'expert', split_axis=0,...  33.5 us
    pallas_call x4, Pallas kernels, on_core(): pl.pallas_call(body, out_shape=[sd(shape, kind) for shape, kind in outs],...  28 us
    pallas_call x2, Pallas kernels, expert_grads(): pl.pallas_call(expert_grads_kernel, grid=(2,), out_shape=jax.ShapeDtypeSt...  21.5 us
  transfers between devices with their start and end apart: 26, of which 11 were waited for; matrix products, arithmetic and copies ran while one was open for 5% of the time, Pallas kernels for 36%

profile of v1, /device:TPU:0, one launch (start us, length us, event | category | flops | bytes accessed | tf_op | source)
XLA Modules:
  0.0 515.6 jit_solution(3267673803711063529)
XLA Ops:
  49.7 7.2 %collective-permute-done.3.refs_6_.refs_12_ = bf16[96,1536]{1,0:T(8,128)(2,1)} collective-permute-done((bf16[96,1536]{1,0:T(8,128)(2,1)}, bf16[96,1536]{1,0:T(8,128)(2,1)}, u32[]{:S(2)}, u32[]{:S(2)}) %collective-permute-start.3) | collective-permute-done | bytes 294944 | tf_op jit(solution)/shard_map/ppermute | solution.py:856
  74.8 9.0 %attn_forward.2 = (bf16[128,4608]{1,0:T(8,128)(2,1)}, bf16[12,128,128]{2,1,0:T(8,128)(2,1)}, bf16[2,128,128]{2,1,0:T(8,128)(2,1)}, bf16[2,128,128]{2,1,0:T(8,128...) custom-call(bf16[128,1536]{1,0:T(8,128)(2,1)} %refs_8_.1, ...), custom_call_target="tpu_custom_call" | custom-call | flops 1459617792 | bytes 20971520 | tf_op jit(solution)/shard_map/attn_forward/pallas_call | solution.py:263
  83.8 28.0 %all_to_all.70 = bf16[16,48,1536]{2,1,0:T(8,128)(2,1)} all-to-all(bf16[16,48,1536]{2,1,0:T(8,128)(2,1)} %bitcast.78), channel_id=1, replica_groups=mesh['dp'=8,'expert'=16] {'expert'}, dimensions={0} | all-to-all | bytes 4718592 | tf_op jit(solution)/shard_map/all_to_all | solution.py:902
  111.8 11.0 %experts_forward.1 = (bf16[768,768]{1,0:T(8,128)(2,1)}, bf16[768,768]{1,0:T(8,128)(2,1)}, bf16[768,768]{1,0:T(8,128)(2,1)}, bf16[768,1536]{1,0:T(8,128)(2,1)}) custom-call(bf16[768,1536]{1,0:T(8,128)(2,1)} %bitcast.71, bf16[2,1,1536,768]{3,2,1,0:T(8,128)(2,1)} %refs_3_.9, bf16[2,1,1536,768]{3,2,1,0:T(8,128)(2,1)} %refs_4_.5, bf16[2,1,768,1536]{3,2,1,0:T(8,128)(2,1)} %refs_5_.9), custom_call_target="tpu_custom_call" | custom-call | flops 5435817984 | bytes 20971520 | tf_op jit(solution)/shard_map/experts_forward/pallas_call | solution.py:491
  127.5 20.1 %turn_weights.3.refs_10_.refs_14_ = bf16[3584,1536]{1,0:T(8,128)(2,1)} custom-call(s32[1]{0:T(128)} %bitcast.7.refs_0_.refs_7_.me, bf16[1536,2176]{1,0:T(8,128)(2,1)} %all-gather.7.cloned.1.call-done.refs_1_.refs_2_, bf16[192,1536]{1,0:T(8,128)(2,1)} %get-tuple-element.71.refs_2_.refs_8_, ...), custom_call_target="tpu_custom_call", output_to_operand_aliasing={{}: (12, {})} | custom-call | tf_op jit(solution)/shard_map/turn_weights/pallas_call | solution.py:714
  153.2 11.9 %attn_forward.3 = (bf16[128,4608]{1,0:T(8,128)(2,1)}, bf16[12,128,128]{2,1,0:T(8,128)(2,1)}, bf16[2,128,128]{2,1,0:T(8,128)(2,1)}, bf16[2,128,128]{2,1,0:T(8,128...) custom-call(f32[128,1536]{1,0:T(8,128)} %get-tuple-element.72.refs_0, ...), custom_call_target="tpu_custom_call" | custom-call | flops 1459617792 | bytes 20971520 | tf_op jit(solution)/shard_map/attn_forward/pallas_call | solution.py:263
  165.1 32.5 %all_to_all.71 = bf16[16,48,1536]{2,1,0:T(8,128)(2,1)} all-to-all(bf16[16,48,1536]{2,1,0:T(8,128)(2,1)} %bitcast.77), channel_id=1, replica_groups=mesh['dp'=8,'expert'=16] {'expert'}, dimensions={0} | all-to-all | bytes 4718592 | tf_op jit(solution)/shard_map/all_to_all | solution.py:902
  197.6 14.5 %experts_both.1 = (bf16[768,768]{1,0:T(8,128)(2,1)}, bf16[768,768]{1,0:T(8,128)(2,1)}, bf16[768,768]{1,0:T(8,128)(2,1)}, bf16[768,1664]{1,0:T(8,128)(2,1)}) custom-call(s32[1]{0:T(128)} %bitcast.11.refs_21_.refs_0_, bf16[768,1536]{1,0:T(8,128)(2,1)} %bitcast.59, f32[768,768]{1,0:T(8,128)} %upper_product.3.refs_18_.refs_2_, ...), custom_call_target="tpu_custom_call" | custom-call | flops 7247757312 | bytes 20971520 | tf_op jit(solution)/shard_map/experts_both/pallas_call | solution.py:491
  216.3 8.3 %experts_out.1 = (bf16[16,16,1536]{2,1,0:T(8,128)(2,1)}, bf16[16,16,1536]{2,1,0:T(8,128)(2,1)}, bf16[16,16,1536]{2,1,0:T(8,128)(2,1)}, bf16[768,1536]{1,0:T(8,128)(2,1)}) custom-call(s32[1]{0:T(128)} %bitcast.11.refs_21_.refs_0_, bf16[768,768]{1,0:T(8,128)(2,1)} %get-tuple-element.81.refs_1_.hidden, bf16[768,1536]{1,0:T(8,128)(2,1)} %bitcast.60, ...), custom_call_target="tpu_custom_call" | custom-call | flops 1811939328 | bytes 20971520 | tf_op jit(solution)/shard_map/experts_out/pallas_call | solution.py:491
  224.6 10.8 %expert_grads.2 = bf16[8,288,1536]{2,1,0:T(8,128)(2,1)} custom-call(bf16[768,1536]{1,0:T(8,128)(2,1)} %bitcast.61, bf16[768,768]{1,0:T(8,128)(2,1)} %get-tuple-element.83.dgate_pre, bf16[768,768]{1,0:T(8,128)(2,1)} %get-tuple-element.84.dup_pre, bf16[768,768]{1,0:T(8,128)(2,1)} %get-tuple-element.81.refs_1_.hidden, bf16[768,1536]{1,0:T(8,128)(2,1)} %get-tuple-element.85.dslot), custom_call_target="tpu_custom_call" | custom-call | flops 5435817984 | bytes 14680064 | tf_op jit(solution)/shard_map/expert_grads/pallas_call | solution.py:789
  237.9 8.9 %all-to-all-done.6 = bf16[16,48,1664]{2,1,0:T(8,128)(2,1)S(1)} async-done(((bf16[16,48,1664]{2,1,0:T(8,128)(2,1)}), bf16[16,48,1664]{2,1,0:T(8,128)(2,1)S(1)}, u32[]{:S(2)}, u32[]{:S(2)}) %all-to-all-start.6) | async-done | bytes 2555936 | tf_op jit(solution)/shard_map/all_to_all | solution.py:902
  246.8 7.1 %all-to-all-start.4 = ((bf16[16,16,1536]{2,1,0:T(8,128)(2,1)}), bf16[16,16,1536]{2,1,0:T(8,128)(2,1)S(1)}, u32[]{:S(2)}, u32[]{:S(2)}) async-start(bf16[16,16,1536]{2,1,0:T(8,128)(2,1)} %after.7), calls=%async_computation.4 | async-start | bytes 1572864 | tf_op jit(solution)/shard_map/all_to_all | solution.py:902
  254.0 14.6 %attn_backward.2 = (f32[128,1536]{1,0:T(8,128)}, bf16[128,3712]{1,0:T(8,128)(2,1)}, bf16[768,1536]{1,0:T(8,128)(2,1)}) custom-call(bf16[128,1536]{1,0:T(8,128)(2,1)} %refs_0_.7, bf16[768,1664]{1,0:T(8,128)(2,1)} %bitcast.56, bf16[1536,3712]{1,0:T(8,128)(2,1)} %all-gather.9.cloned.1.call-done.refs_1_.refs_3_.refs_4_.refs_2_, ...), custom_call_target="tpu_custom_call" | custom-call | flops 1459617792 | bytes 20971520 | tf_op jit(solution)/shard_map/attn_backward/pallas_call | solution.py:263
  271.3 37.9 %all_to_all.72 = bf16[16,48,1536]{2,1,0:T(8,128)(2,1)} all-to-all(bf16[16,48,1536]{2,1,0:T(8,128)(2,1)S(1)} %bitcast.73), channel_id=1, replica_groups=mesh['dp'=8,'expert'=16] {'expert'}, dimensions={0} | all-to-all | bytes 4718592 | tf_op jit(solution)/shard_map/all_to_all | solution.py:902
  312.9 11.2 %experts_backward.1 = (bf16[768,768]{1,0:T(8,128)(2,1)}, bf16[768,768]{1,0:T(8,128)(2,1)}, bf16[768,1536]{1,0:T(8,128)(2,1)}) custom-call(bf16[768,1536]{1,0:T(8,128)(2,1)} %bitcast.75, bf16[768,768]{1,0:T(8,128)(2,1)} %get-tuple-element.98.refs_1_, bf16[768,768]{1,0:T(8,128)(2,1)} %get-tuple-element.99.refs_2_, bf16[2,1,1536,768]{3,2,1,0:T(8,128)(2,1)} %refs_3_.9, ...), custom_call_target="tpu_custom_call" | custom-call | flops 5435817984 | bytes 20971520 | tf_op jit(solution)/shard_map/experts_backward/pallas_call | solution.py:491
  332.8 10.8 %expert_grads.3 = bf16[8,288,1536]{2,1,0:T(8,128)(2,1)} custom-call(bf16[768,1536]{1,0:T(8,128)(2,1)} %bitcast.72, bf16[768,768]{1,0:T(8,128)(2,1)} %get-tuple-element.100.dgate_pre, bf16[768,768]{1,0:T(8,128)(2,1)} %get-tuple-element.101.dup_pre, bf16[768,768]{1,0:T(8,128)(2,1)} %get-tuple-element.102.hidden, bf16[768,1536]{1,0:T(8,128)(2,1)} %bitcast.76), custom_call_target="tpu_custom_call" | custom-call | flops 5435817984 | bytes 14680064 | tf_op jit(solution)/shard_map/expert_grads/pallas_call | solution.py:789
  346.1 8.9 %dense_grads.2.refs_2_ = bf16[16,192,256]{2,1,0:T(8,128)(2,1)} custom-call(s32[1]{0:T(128)} %bitcast.7.refs_0_.refs_7_.me, bf16[3,256,1024]{2,1,0:T(8,128)(2,1)} %turn_columns.3.refs_1_, bf16[1024,3712]{1,0:T(8,128)(2,1)} %all-gather.15.cloned.1.call-done.refs_2_, bf16[256,1536]{1,0:T(8,128)(2,1)} %bitcast.63), custom_call_target="tpu_custom_call" | custom-call | flops 1946157056 | bytes 10485760 | tf_op jit(solution)/shard_map/dense_grads/pallas_call | solution.py:1010
  355.1 16.3 %all-to-all-done.9 = bf16[16,48,1536]{2,1,0:T(8,128)(2,1)S(1)} async-done(((bf16[16,48,1536]{2,1,0:T(8,128)(2,1)}), bf16[16,48,1536]{2,1,0:T(8,128)(2,1)S(1)}, u32[]{:S(2)}, u32[]{:S(2)}) %all-to-all-start.9) | async-done | bytes 2359328 | tf_op jit(solution)/shard_map/all_to_all | solution.py:902
  375.3 12.3 %attn_backward.3 = (f32[128,1536]{1,0:T(8,128)}, bf16[128,3712]{1,0:T(8,128)(2,1)}) custom-call(f32[128,1536]{1,0:T(8,128)} %get-tuple-element.105.refs_0_, bf16[768,1536]{1,0:T(8,128)(2,1)} %bitcast.57, bf16[1536,2176]{1,0:T(8,128)(2,1)} %all-gather.7.cloned.1.call-done.refs_1_.refs_2_, f32[128,128]{1,0:T(8,128)} %get-tuple-element.137.refs_2_.refs_3_, ...), custom_call_target="tpu_custom_call" | custom-call | flops 1459617792 | bytes 20971520 | tf_op jit(solution)/shard_map/attn_backward/pallas_call | solution.py:263
  390.5 28.1 %all_to_all.74.pieces_hbm = bf16[16,192,256]{2,1,0:T(8,128)(2,1)} all-to-all(bf16[16,192,256]{2,1,0:T(8,128)(2,1)S(1)} %copy-done.3), channel_id=1, replica_groups=mesh['dp'=8,'expert'=16] {'expert'}, dimensions={0} | all-to-all | bytes 3145728 | tf_op jit(solution)/shard_map/all_to_all | solution.py:1032
  425.2 9.2 %all-gather.17.cloned.1.call-done.refs_2_ = bf16[1024,3712]{1,0:T(8,128)(2,1)} async-done(((bf16[128,3712]{1,0:T(8,128)(2,1)}), bf16[1024,3712]{1,0:T(8,128)(2,1)}) %all-gather.17.cloned.1.call-update) | async-done | bytes 7602192 | tf_op jit(solution)/shard_map/all_gather | solution.py:1210
  434.4 8.9 %dense_grads.3.refs_0_ = bf16[16,192,256]{2,1,0:T(8,128)(2,1)} custom-call(s32[1]{0:T(128)} %bitcast.7.refs_0_.refs_7_.me, bf16[3,256,1024]{2,1,0:T(8,128)(2,1)} %turn_columns.2.refs_2_.refs_1_, bf16[1024,3712]{1,0:T(8,128)(2,1)} %all-gather.17.cloned.1.call-done.refs_2_), custom_call_target="tpu_custom_call" | custom-call | flops 1946157056 | bytes 10485760 | tf_op jit(solution)/shard_map/dense_grads/pallas_call | solution.py:1010
  448.4 26.4 %all_to_all.73.pieces_hbm = bf16[16,192,256]{2,1,0:T(8,128)(2,1)} all-to-all(bf16[16,192,256]{2,1,0:T(8,128)(2,1)} %after.12), channel_id=1, replica_groups=mesh['dp'=8,'expert'=16] {'expert'}, dimensions={0} | all-to-all | bytes 3145728 | tf_op jit(solution)/shard_map/all_to_all | solution.py:1032
  492.6 10.5 %all-to-all-done.13.refs_0_ = bf16[16,192,256]{2,1,0:T(8,128)(2,1)S(1)} async-done(((bf16[16,192,256]{2,1,0:T(8,128)(2,1)}), bf16[16,192,256]{2,1,0:T(8,128)(2,1)S(1)}, u32[]{:S(2)}, u32[]{:S(2)}) %all-to-all-start.13) | async-done | bytes 1572896 | tf_op jit(solution)/shard_map/all_to_all | solution.py:1032
  (142 shorter events, 136.4 us)
Async XLA Ops:
  7.2 66.4 %all-gather.7.cloned.1.call-start = ((), (), s32[]{:S(2)}) async-start(), calls=%async_computation.16 | async-start | bytes 7520256 | tf_op jit(solution)/shard_map/all_gather | solution.py:1210
  10.2 141.6 %all-gather.9.cloned.1.call-start = ((), (), s32[]{:S(2)}) async-start(), calls=%async_computation.17 | async-start | bytes 12828672 | tf_op jit(solution)/shard_map/all_gather | solution.py:1210
  13.5 60.0 %collective-permute-start.4 = (bf16[192,1536]{1,0:T(8,128)(2,1)}, bf16[192,1536]{1,0:T(8,128)(2,1)}, u32[]{:S(2)}, u32[]{:S(2)}) collective-permute-start(bf16[192,1536]{1,0:T(8,128)(2,1)} %get-tuple-element.71.refs_2_.refs_8_), channel_id=1, source_target_pairs={{0,16},{16,0},{32,48},{48,32},{64,80},{80,64},{96,112},{112,96},{1... | collective-permute-start | bytes 1769480 | tf_op jit(solution)/shard_map/ppermute | solution.py:863
  13.6 25.5 %collective-permute-start.1 = (bf16[192,1536]{1,0:T(8,128)(2,1)}, bf16[192,1536]{1,0:T(8,128)(2,1)S(1)}, u32[]{:S(2)}, u32[]{:S(2)}) collective-permute-start(bf16[192,1536]{1,0:T(8,128)(2,1)} %get-tuple-element.71.refs_2_.refs_8_), channel_id=1, source_target_pairs={{0,96},{16,112},{32,0},{48,16},{64,32},{80,48},{96,64},{112,80},{1... | collective-permute-start | bytes 1769480 | tf_op jit(solution)/shard_map/ppermute | solution.py:856
  17.8 25.6 %collective-permute-start = (bf16[192,1536]{1,0:T(8,128)(2,1)}, bf16[192,1536]{1,0:T(8,128)(2,1)S(1)}, u32[]{:S(2)}, u32[]{:S(2)}) collective-permute-start(bf16[192,1536]{1,0:T(8,128)(2,1)} %get-tuple-element.71.refs_2_.refs_8_), channel_id=1, source_target_pairs={{0,32},{16,48},{32,64},{48,80},{64,96},{80,112},{96,0},{112,16},{1... | collective-permute-start | bytes 1769480 | tf_op jit(solution)/shard_map/ppermute | solution.py:856
  21.4 44.0 %all-to-all-start = ((bf16[16,48,1536]{2,1,0:T(8,128)(2,1)}), bf16[16,48,1536]{2,1,0:T(8,128)(2,1)S(1)}, u32[]{:S(2)}, u32[]{:S(2)}) async-start(bf16[16,48,1536]{2,1,0:T(8,128)(2,1)} %bitcast.62), calls=%async_computation | async-start | bytes 4718592 | tf_op jit(solution)/shard_map/all_to_all | solution.py:902
  28.5 206.9 %all-gather.11.cloned.1.call-start = ((), (), s32[]{:S(2)}) async-start(), calls=%async_computation.18 | async-start | bytes 10616832 | tf_op jit(solution)/shard_map/all_gather | solution.py:1210
  39.9 16.9 %collective-permute-start.3 = (bf16[96,1536]{1,0:T(8,128)(2,1)}, bf16[96,1536]{1,0:T(8,128)(2,1)}, u32[]{:S(2)}, u32[]{:S(2)}) collective-permute-start(bf16[96,1536]{1,0:T(8,128)(2,1)} %slice.18), channel_id=1, source_target_pairs={{0,96},{16,112},{32,0},{48,16},{64,32},{80,48},{96,64},{112,80},{1... | collective-permute-start | bytes 884744 | tf_op jit(solution)/shard_map/ppermute | solution.py:856
  44.1 17.1 %collective-permute-start.2 = (bf16[96,1536]{1,0:T(8,128)(2,1)}, bf16[96,1536]{1,0:T(8,128)(2,1)}, u32[]{:S(2)}, u32[]{:S(2)}) collective-permute-start(bf16[96,1536]{1,0:T(8,128)(2,1)} %slice.17), channel_id=1, source_target_pairs={{0,32},{16,48},{32,64},{48,80},{64,96},{80,112},{96,0},{112,16},{1... | collective-permute-start | bytes 884744 | tf_op jit(solution)/shard_map/ppermute | solution.py:856
  44.1 29.4 %collective-permute-start.6 = (bf16[192,1536]{1,0:T(8,128)(2,1)S(1)}, bf16[192,1536]{1,0:T(8,128)(2,1)}, u32[]{:S(2)}, u32[]{:S(2)}) collective-permute-start(bf16[192,1536]{1,0:T(8,128)(2,1)S(1)} %collective-permute-done.1.refs_4_.refs_10_), channel_id=1, source_target_pairs={{0,16},{16,0},{32,48},{48,32},{64,80},{80,64},{96,112},{112,96},{1... | collective-permute-start | bytes 1769480 | tf_op jit(solution)/shard_map/ppermute | solution.py:863
  44.1 29.4 %collective-permute-start.5 = (bf16[192,1536]{1,0:T(8,128)(2,1)S(1)}, bf16[192,1536]{1,0:T(8,128)(2,1)}, u32[]{:S(2)}, u32[]{:S(2)}) collective-permute-start(bf16[192,1536]{1,0:T(8,128)(2,1)S(1)} %collective-permute-done.refs_3_.refs_9_), channel_id=1, source_target_pairs={{0,16},{16,0},{32,48},{48,32},{64,80},{80,64},{96,112},{112,96},{1... | collective-permute-start | bytes 1769480 | tf_op jit(solution)/shard_map/ppermute | solution.py:863
  122.8 29.0 %all-to-all-start.2 = ((bf16[16,48,1536]{2,1,0:T(8,128)(2,1)}), bf16[16,48,1536]{2,1,0:T(8,128)(2,1)S(1)}, u32[]{:S(2)}, u32[]{:S(2)}) async-start(bf16[16,48,1536]{2,1,0:T(8,128)(2,1)} %bitcast.58), calls=%async_computation.2 | async-start | bytes 4718592 | tf_op jit(solution)/shard_map/all_to_all | solution.py:902
  126.7 216.9 %all-gather.13.cloned.1.call-start = ((), (), s32[]{:S(2)}) async-start(), calls=%async_computation.19 | async-start | bytes 10616832 | tf_op jit(solution)/shard_map/all_gather | solution.py:1210
  212.1 34.7 %all-to-all-start.6 = ((bf16[16,48,1664]{2,1,0:T(8,128)(2,1)}), bf16[16,48,1664]{2,1,0:T(8,128)(2,1)S(1)}, u32[]{:S(2)}, u32[]{:S(2)}) async-start(bf16[16,48,1664]{2,1,0:T(8,128)(2,1)} %bitcast.70), calls=%async_computation.6 | async-start | bytes 5111808 | tf_op jit(solution)/shard_map/all_to_all | solution.py:902
  246.8 21.8 %all-to-all-start.4 = ((bf16[16,16,1536]{2,1,0:T(8,128)(2,1)}), bf16[16,16,1536]{2,1,0:T(8,128)(2,1)S(1)}, u32[]{:S(2)}, u32[]{:S(2)}) async-start(bf16[16,16,1536]{2,1,0:T(8,128)(2,1)} %after.7), calls=%async_computation.4 | async-start | bytes 1572864 | tf_op jit(solution)/shard_map/all_to_all | solution.py:902
  253.9 92.2 %all-gather.15.cloned.1.call-start = ((), (), s32[]{:S(2)}) async-start(), calls=%async_computation.20 | async-start | bytes 8552448 | tf_op jit(solution)/shard_map/all_gather | solution.py:1210
  269.5 120.0 %reduce-scatter.3.cloned.1.call-start = ((), (), s32[]{:S(2)}) async-start(), calls=%async_computation.21 | async-start | bytes 7962624 | tf_op jit(solution)/shard_map/reduce_scatter | solution.py:1254
  309.1 18.9 %all-to-all-start.5 = ((bf16[16,16,1536]{2,1,0:T(8,128)(2,1)}), bf16[16,16,1536]{2,1,0:T(8,128)(2,1)S(1)}, u32[]{:S(2)}, u32[]{:S(2)}) async-start(bf16[16,16,1536]{2,1,0:T(8,128)(2,1)} %get-tuple-element.87), calls=%async_computation.5 | async-start | bytes 1572864 | tf_op jit(solution)/shard_map/all_to_all | solution.py:902
  328.9 42.4 %all-to-all-start.9 = ((bf16[16,48,1536]{2,1,0:T(8,128)(2,1)}), bf16[16,48,1536]{2,1,0:T(8,128)(2,1)S(1)}, u32[]{:S(2)}, u32[]{:S(2)}) async-start(bf16[16,48,1536]{2,1,0:T(8,128)(2,1)} %bitcast.74), calls=%async_computation.9 | async-start | bytes 4718592 | tf_op jit(solution)/shard_map/all_to_all | solution.py:902
  371.3 18.2 %all-to-all-start.8 = ((bf16[16,16,1536]{2,1,0:T(8,128)(2,1)}), bf16[16,16,1536]{2,1,0:T(8,128)(2,1)S(1)}, u32[]{:S(2)}, u32[]{:S(2)}) async-start(bf16[16,16,1536]{2,1,0:T(8,128)(2,1)} %after.9), calls=%async_computation.8 | async-start | bytes 1572864 | tf_op jit(solution)/shard_map/all_to_all | solution.py:902
  375.0 59.4 %all-gather.17.cloned.1.call-start = ((), (), s32[]{:S(2)}) async-start(), calls=%async_computation.22 | async-start | bytes 8552448 | tf_op jit(solution)/shard_map/all_gather | solution.py:1210
  390.4 98.9 %reduce-scatter.5.cloned.1.call-start = ((), (), s32[]{:S(2)}) async-start(), calls=%async_computation.23 | async-start | bytes 7962624 | tf_op jit(solution)/shard_map/reduce_scatter | solution.py:1267
  421.5 25.8 %all-to-all-start.11 = ((bf16[16,192,256]{2,1,0:T(8,128)(2,1)}), bf16[16,192,256]{2,1,0:T(8,128)(2,1)S(1)}, u32[]{:S(2)}, u32[]{:S(2)}) async-start(bf16[16,192,256]{2,1,0:T(8,128)(2,1)} %sum_pieces.2.refs_1_), calls=%async_computation.12 | async-start | bytes 3145728 | tf_op jit(solution)/shard_map/all_to_all | solution.py:1032
  477.6 25.5 %all-to-all-start.13 = ((bf16[16,192,256]{2,1,0:T(8,128)(2,1)}), bf16[16,192,256]{2,1,0:T(8,128)(2,1)S(1)}, u32[]{:S(2)}, u32[]{:S(2)}) async-start(bf16[16,192,256]{2,1,0:T(8,128)(2,1)} %sum_pieces.3), calls=%async_computation.14 | async-start | bytes 3145728 | tf_op jit(solution)/shard_map/all_to_all | solution.py:1032
  (22 other events, 150.0 us)
Sparse Core Ops, SparseCore 0:
  10.3 59.1 all-gather.6
  71.2 61.5 all-gather.8
  135.1 54.5 all-gather.10
  191.2 54.4 all-gather.12
  269.7 48.4 all-gather.14
  320.4 46.3 reduce-scatter.2
  390.6 43.8 all-gather.16
  436.9 46.3 reduce-scatter.4

commit v2 on v1

--- a/solution.py
+++ b/solution.py
@@ -312,35 +312,23 @@
 
 
 def attn_backward_kernel(last, ins, outs, scratch):
-    (dx_hbm, back_hbm, w_hbm, cosine_hbm, sine_hbm, give_hbm, router_hbm, after_hbm, x_hbm, probs_hbm,
-     qrot_hbm, krot_hbm, value_hbm), ins = ins[:13], ins[13:]
-    (dx_in, back, w, cosine, sine, give, router, after, x_in, probs, qrot, krot, value, wide_in,
-     small_in, datt, dx_out, packed), scratch = scratch[:18], scratch[18:]
+    (dx_hbm, back_hbm, w_hbm, turned_hbm, cosine_hbm, sine_hbm, give_hbm, router_hbm, after_hbm,
+     x_hbm, probs_hbm, qrot_hbm, krot_hbm, value_hbm), ins = ins[:14], ins[14:]
+    (dx_in, back, small_ref, turned, cosine, sine, give, router, after, x_in, probs, qrot, krot, value, wide_in,
+     small_in, datt, dx_out, packed), scratch = scratch[:19], scratch[19:]
     if last:
         rows, scratch = scratch[0], scratch[1:]
-    else:
-        turned, scratch = scratch[0], scratch[1:]
     in_sems, out_sems = scratch
     pairs = [(give_hbm, give), (back_hbm, back), (router_hbm, router), (dx_hbm, dx_in)]
     if not last:
         pairs += [(ins[0], wide_in)]
-    pairs += [small_block(w_hbm, w), (after_hbm, after)]
-    if last:
-        out_pairs, qkv_pairs = [], []
-        for at in range(0, WIDTH, TILE):
-            block = (pl.ds(at, TILE), pl.ds(QKV, WIDTH))
-            out_pairs += [(w_hbm.at[block], w.at[block])]
-            block = (pl.ds(at, TILE), pl.ds(0, QKV))
-            qkv_pairs += [(w_hbm.at[block], w.at[block])]
-    else:
-        columns = [(slice(None), pl.ds(at, TILE)) for at in range(0, WIDTH, TILE)]
-        out_pairs = [
-            (ins[1].at[pl.ds(QKV, WIDTH)].at[c], turned.at[pl.ds(QKV, WIDTH)].at[c])
-            for c in columns
-        ]
-        qkv_pairs = [
-            (ins[1].at[pl.ds(0, QKV)].at[c], turned.at[pl.ds(0, QKV)].at[c]) for c in columns
-        ]
+    last_block = pl.ds(w_hbm.shape[1] - HEAD, HEAD)
+    pairs += [(w_hbm.at[:, last_block], small_ref), (after_hbm, after)]
+    columns = [(slice(None), pl.ds(at, TILE)) for at in range(0, WIDTH, TILE)]
+    out_pairs, qkv_pairs = (
+        [(turned_hbm.at[rows].at[c], turned.at[rows].at[c]) for c in columns]
+        for rows in (pl.ds(QKV, WIDTH), pl.ds(0, QKV))
+    )
     pairs += out_pairs + [(probs_hbm, probs), (value_hbm, value), (krot_hbm, krot), (qrot_hbm, qrot)]
     pairs += [(cosine_hbm, cosine), (sine_hbm, sine)] + qkv_pairs + [(x_hbm, x_in)]
     if last:
@@ -359,7 +347,7 @@
         both = dot(jnp.concatenate(split(dgate), axis=0), spread)
         drouter = both[:ROWS] + both[ROWS:]
     reader.take(2)
-    small = w[:, SMALL:]
+    small = small_ref[...]
     gain_attn, gain_ffn = gain_rows(small)
     shares = router[...]
     dlogits = shares * (drouter - jnp.sum(drouter * shares, axis=-1, keepdims=True))
@@ -381,10 +369,7 @@
     writer.send(packed.at[:, QKV:], outs[1].at[:, QKV:])
     for tile in tiles(WIDTH):
         reader.take()
-        if last:
-            wide = dot(packed[:, QKV:SMALL], w[tile, QKV:SMALL], 1, 1).astype(BF)
-        else:
-            wide = dot(packed[:, QKV:SMALL], turned[QKV:SMALL, tile]).astype(BF)
+        wide = dot(packed[:, QKV:SMALL], turned[QKV:SMALL, tile]).astype(BF)
         for half in range(TILE // HEAD):
             datt[tile.start // HEAD + half] = wide[:, half * HEAD : (half + 1) * HEAD]
     reader.take(6)
@@ -409,10 +394,7 @@
     parts = []
     for tile in tiles(WIDTH):
         reader.take()
-        if last:
-            parts += [dot(packed[:, :QKV], w[tile, :QKV], 1, 1)]
-        else:
-            parts += [dot(packed[:, :QKV], turned[:QKV, tile])]
+        parts += [dot(packed[:, :QKV], turned[:QKV, tile])]
     dacts = jnp.concatenate(parts, axis=1)
     reader.take()
     dx = dx_out[...] + norm_back(dacts, gain_attn, x_in[...].astype(F32))
@@ -435,18 +417,16 @@
     outs = [(TOKENS, F32), ((ROWS, PACKED), BF)]
     if last:
         outs += [(WIDE, BF)]
-    ins = [dx, back, w, tables[0], tables[1], give, kept["router"], kept["after"], x]
+    ins = [dx, back, w, turned, tables[0], tables[1], give, kept["router"], kept["after"], x]
     ins += [kept[n] for n in ("probs", "qrot", "krot", "value")]
-    ins += list(below) if last else [returned, turned]
+    ins += list(below) if last else [returned]
     scratch = [
-        (TOKENS, dx.dtype), (back.shape, BF), ((WIDTH, PACKED), BF),
+        (TOKENS, dx.dtype), (back.shape, BF), ((WIDTH, HEAD), BF), ((SMALL, WIDTH), BF),
         (TABLE, F32), (TABLE, F32),
         ((ROWS, SLOTS), BF), (TABLE, F32), (TOKENS, F32), (TOKENS, x.dtype),
         ((QUERY_HEADS, ROWS, ROWS), F32), (HEADS, BF), (KEYS, BF), (KEYS, BF),
         ((SLOTS, ROWS), BF) if last else (WIDE, BF), (TABLE, F32), (HEADS, BF),
     ] + outs
-    if not last:
-        scratch += [((SMALL, WIDTH), BF)]
     return run_attn(
         lambda *refs: attn_backward_kernel(last, *refs), "attn_backward", ins, order, outs, scratch,
         24 + WIDTH // TILE, 12, VMEM_BYTES,
@@ -750,17 +730,18 @@
 
 def turn_weights_kernel(me, ins, outs, scratch):
     w, turned, in_sems, out_sems = scratch
-    pairs = [column_block(ins[0], w, at) for at in range(0, QKV, TILE)] + ring_blocks(me, ins[1:], w)
+    ring_out = len(ins) > 1
+    pairs = [column_block(ins[0], w, at) for at in range(0, QKV if ring_out else SMALL, TILE)]
+    if ring_out:
+        pairs += ring_blocks(me, ins[1:], w)
     reader, writer = Reader(in_sems, pairs), Writer(out_sems)
-    for tile in tiles(QKV):
-        reader.take()
+    for tile in tiles(SMALL):
+        if ring_out and tile.start == QKV:
+            reader.take(len(ins) - 1)
+        elif not ring_out or tile.start < QKV:
+            reader.take()
         turned[tile] = w[:, tile].T
         writer.send(turned.at[tile], outs[0].at[tile])
-    reader.take(len(ins) - 1)
-    for tile in tiles(WIDTH):
-        at = slice(QKV + tile.start, QKV + tile.stop)
-        turned[at] = w[:, at].T
-        writer.send(turned.at[at], outs[0].at[at])
     writer.finish()
 
 
@@ -956,24 +937,16 @@
     base = start - shift
     copies = Writer(out_sems)
     pairs = [(turned_hbm, turned)]
-    for at in range(0, PACKED, CHUNK):
-        block = (slice(None), pl.ds(at, min(CHUNK, PACKED - at)))
+    for at, width in [(SMALL, HEAD)] + [(at, 2 * CHUNK) for at in range(0, SMALL, 2 * CHUNK)]:
+        block = (slice(None), pl.ds(at, width))
         pairs += [(factors_hbm.at[block], factors.at[block])]
     reader = Reader(in_sems, pairs)
-    reader.take()
+    reader.take(2)
 
     def put(chunk, values):
         pieces[chunk] = values.astype(BF)
         copies.send(pieces.at[chunk], pieces_hbm.at[chunk])
 
-    for chunk in range(SMALL // CHUNK):
-        reader.take()
-        total[chunk % 2] = dot(
-            turned[0 if chunk < QKV // CHUNK else 1],
-            factors[:, chunk * CHUNK : (chunk + 1) * CHUNK],
-        )
-        put(chunk, total[chunk % 2, pl.ds(pl.multiple_of(shift, 64), SHARD), :])
-    reader.take()
     ends = jnp.zeros((ROWS, HEAD), F32)
     for source in range(DP):
         ends += factors[source * ROWS : (source + 1) * ROWS, SMALL:].astype(F32)
@@ -990,14 +963,21 @@
         jnp.concatenate([first[ROWS // 2 :], second], axis=0),
     )
     gain_high, gain_low = split(gain)
-    total[0, :, :HEAD] = dot(turned[2], factors[:, SMALL:])
-    router = total[0, pl.ds(pl.multiple_of(shift, 64), SHARD), :HEAD]
+    rows = pl.ds(pl.multiple_of(shift, 64), SHARD)
+    total[1, :, :HEAD] = dot(turned[2], factors[:, SMALL:])
+    router = total[1, rows, :HEAD]
     lane = lax.broadcasted_iota(jnp.int32, (SHARD, HEAD), 1)
     router = jnp.where(lane < EXPERTS, router, 0.0)
     router = jnp.where(lane == EXPERTS, gain_high.astype(F32), router)
     router = jnp.where(lane == EXPERTS + 1, gain_low.astype(F32), router)
     put(CHUNKS - 2, jnp.concatenate([router, jnp.zeros_like(router)], axis=1))
     put(CHUNKS - 1, jnp.zeros((SHARD, CHUNK), F32))
+    for pair in range(SMALL // CHUNK // 2):
+        reader.take()
+        at = pair * 2 * CHUNK
+        total[pair % 2] = dot(turned[0 if at < QKV else 1], factors[:, at : at + 2 * CHUNK])
+        put(2 * pair, total[pair % 2, rows, :CHUNK])
+        put(2 * pair + 1, total[pair % 2, rows, CHUNK:])
     copies.finish()
 
 
@@ -1015,7 +995,7 @@
         scratch_shapes=[
             pltpu.VMEM((3, TILE, tokens), BF),
             pltpu.VMEM((tokens, PACKED), BF),
-            pltpu.VMEM((2, TILE, CHUNK), F32),
+            pltpu.VMEM((2, TILE, 2 * CHUNK), F32),
             pltpu.VMEM((CHUNKS, SHARD, CHUNK), BF),
             pltpu.SemaphoreType.DMA((1 + CHUNKS,)),
             pltpu.SemaphoreType.DMA((CHUNKS,)),
@@ -1216,9 +1196,8 @@
 
     dx_rows = exchange(dot(take[1], cotangent).astype(BF))
 
-    product = upper_product(0, me_dp, dx_rows, w_down, None, ())
     turned_w = turn_weights(1, me_dp, w[0], out_ring[1:], None, ())
-    product = upper_product(1, me_dp, dx_rows, w_down, product, turned_w)
+    product = upper_product(1, me_dp, dx_rows, w_down, None, turned_w)
     kept0 = attn_forward(
         tokens, None, w[0], out_ring, tables, take[0], give[0],
         (*product, give[1], give_parts, me_expert),
@@ -1227,16 +1206,19 @@
     act0, slope0, hidden0, out0 = experts_forward(received0, experts, ())
     returned0 = exchange(out0)
     turned_w = turn_weights(0, me_dp, w[0], out_ring[1:], turned_w, (out0,))
+    product = upper_product(0, me_dp, dx_rows, w_down, product, turned_w)
+    turned_w1 = turn_weights(0, me_dp, w[1], [], None, product)
     columns0 = gather(kept0["columns"])
 
     kept1 = attn_forward(
         kept0["after"], (kept0["high"], kept0["low"], returned0), w[1], None, tables, take[1],
-        give_parts, tuple(turned_w),
+        give_parts, tuple(turned_w1),
     )
     received1 = exchange(kept1["rows"])
     columns1 = gather(kept1["columns"])
+    turned_w1 = turn_weights(1, me_dp, w[1], [], turned_w1, (received1,))
     hidden1, dgate1, dup1, back1 = experts_both(
-        me_expert, received1, product[0], w[1], experts, ()
+        me_expert, received1, product[0], w[1], experts, tuple(turned_w1)
     )
     back1 = exchange(back1)
     *parts, dslot1 = experts_out(me_expert, hidden1, received1, dx_rows, w[1], w_down, ())
@@ -1245,7 +1227,7 @@
     parts[0] = exchange(after(parts[0], grads1, turned0))
 
     dx0, packed1, rows0 = attn_backward(
-        cotangent, back1, kept1["x"], kept1, w[1], None, tables, give[1],
+        cotangent, back1, kept1["x"], kept1, w[1], turned_w1[0], tables, give[1],
         (take[0], kept0["router"]), None, (),
     )
     packed1 = after(packed1, parts[0])
@@ -1262,9 +1244,9 @@
     grad_tokens, packed0 = attn_backward(
         dx0, back0, tokens, kept0, w[0], turned_w[0], tables, give[0], None, returned0, ()
     )
-    factors0 = gather(after(packed0, parts[2], shares1))
+    factors0 = gather(after(packed0, parts[2]))
     summed1 = sum_pieces(to_expert_peers(pieces1), CHUNKS)
-    shares0 = lax.psum_scatter(after(grads0, summed1), "dp", scatter_dimension=0, tiled=True)
+    shares0 = lax.psum_scatter(after(grads0, summed1, shares1), "dp", scatter_dimension=0, tiled=True)
     mixed = mixed_rows(kept1["after"], kept1["high"], kept1["low"], parts)
     pieces1 = to_expert_peers(summed1)
     pieces0 = dense_grads(me_dp, turned0, factors0, ())

time: 526 us -> 504 us (0.958)
  blocking collectives: 153 us -> 143 us
  Pallas kernels: 192 us -> 183 us
  waiting for transfers between devices: 72 us -> 65.2 us
    all_to_all x7, waiting for transfers between devices: 36.1 us -> 11.8 us  [exchange(): lax.all_to_all(rows.reshape(EXPERTS, -1, width), 'expert', split_axis=0,...]
    all_gather x6, waiting for transfers between devices: 9.24 us -> 32.7 us  [gather(): return lax.all_gather(values, 'dp', axis=0, tiled=True)]
    all_to_all x3, blocking collectives: 98.3 us -> 88.6 us  [exchange(): lax.all_to_all(rows.reshape(EXPERTS, -1, width), 'expert', split_axis=0,...]
    pallas_call x2, Pallas kernels: 17.8 us -> 12 us  [dense_grads(): pl.pallas_call(body, out_shape=jax.ShapeDtypeStruct((CHUNKS, SHARD, CHUNK...]
    unnamed x40 -> x44, local copies, waits for them, and re-layouts: 8.98 us -> 10.5 us
    pallas_call x4 -> x6, Pallas kernels: 28 us -> 27.4 us  [on_core(): pl.pallas_call(body, out_shape=[sd(shape, kind) for shape, kind in outs],...]
  transfers between devices with their start and end apart: 26 -> 26, of which waited for: 11 -> 10; matrix products, arithmetic and copies ran while one was open for 5% -> 5% of each run, Pallas kernels for 36% -> 36%
where the time goes in v2:
time: 504 us; the launch traced here: 495 us
  Pallas kernels  183 us (36%)
  blocking collectives  143 us (28%)
  waiting for transfers between devices  65.2 us (13%)
  starting transfers between devices  53.2 us (11%)
  local copies, waits for them, and re-layouts  15.2 us (3%)
  between operations  15.2 us (3%)
  other arithmetic  10.3 us (2%)
  matrix products  9.82 us (2%)
    all_to_all x3, blocking collectives, exchange(): lax.all_to_all(rows.reshape(EXPERTS, -1, width), 'expert', split_axis=0,...  88.6 us
    all_to_all x2, blocking collectives, to_expert_peers(): lax.all_to_all(pieces, 'expert', split_axis=0, concat_axis=0, tiled=True)  54.2 us
    pallas_call x4, Pallas kernels, run_experts(): pl.pallas_call(body, out_shape=[sd(shape, BF) for shape in outs], in_spec...  45 us
    pallas_call x4, Pallas kernels, run_attn(): pl.pallas_call(body, out_shape=[sd(shape, kind) for shape, kind in outs],...  44.4 us
    all_to_all x7, starting transfers between devices, exchange(): lax.all_to_all(rows.reshape(EXPERTS, -1, width), 'expert', split_axis=0,...  36.9 us
    all_gather x6, waiting for transfers between devices, gather(): return lax.all_gather(values, 'dp', axis=0, tiled=True)  32.7 us
    pallas_call x6, Pallas kernels, on_core(): pl.pallas_call(body, out_shape=[sd(shape, kind) for shape, kind in outs],...  27.4 us
    pallas_call x2, Pallas kernels, expert_grads(): pl.pallas_call(expert_grads_kernel, grid=(2,), out_shape=jax.ShapeDtypeSt...  21.6 us
  transfers between devices with their start and end apart: 26, of which 10 were waited for; matrix products, arithmetic and copies ran while one was open for 5% of the time, Pallas kernels for 36%

profile of v2, /device:TPU:0, one launch (start us, length us, event | category | flops | bytes accessed | tf_op | source)
XLA Modules:
  0.0 494.6 jit_solution(4661719577274327975)
XLA Ops:
  21.4 7.0 %all-to-all-start = ((bf16[16,48,1536]{2,1,0:T(8,128)(2,1)}), bf16[16,48,1536]{2,1,0:T(8,128)(2,1)S(1)}, u32[]{:S(2)}, u32[]{:S(2)}) async-start(bf16[16,48,1536]{2,1,0:T(8,128)(2,1)} %bitcast.63), calls=%async_computation | async-start | bytes 4718592 | tf_op jit(solution)/shard_map/all_to_all | solution.py:883
  49.4 7.9 %collective-permute-done.2.refs_5_.refs_11_ = bf16[96,1536]{1,0:T(8,128)(2,1)} collective-permute-done((bf16[96,1536]{1,0:T(8,128)(2,1)}, bf16[96,1536]{1,0:T(8,128)(2,1)}, u32[]{:S(2)}, u32[]{:S(2)}) %collective-permute-start.2) | collective-permute-done | bytes 294944 | tf_op jit(solution)/shard_map/ppermute | solution.py:837
  68.6 8.7 %attn_forward.2 = (bf16[128,4608]{1,0:T(8,128)(2,1)}, bf16[12,128,128]{2,1,0:T(8,128)(2,1)}, bf16[2,128,128]{2,1,0:T(8,128)(2,1)}, bf16[2,128,128]{2,1,0:T(8,128...) custom-call(bf16[128,1536]{1,0:T(8,128)(2,1)} %refs_9_.1, ...), custom_call_target="tpu_custom_call" | custom-call | flops 1459617792 | bytes 20971520 | tf_op jit(solution)/shard_map/attn_forward/pallas_call | solution.py:263
  77.4 27.3 %all_to_all.70 = bf16[16,48,1536]{2,1,0:T(8,128)(2,1)} all-to-all(bf16[16,48,1536]{2,1,0:T(8,128)(2,1)} %bitcast.79), channel_id=1, replica_groups=mesh['dp'=8,'expert'=16] {'expert'}, dimensions={0} | all-to-all | bytes 4718592 | tf_op jit(solution)/shard_map/all_to_all | solution.py:883
  104.7 10.9 %experts_forward.1 = (bf16[768,768]{1,0:T(8,128)(2,1)}, bf16[768,768]{1,0:T(8,128)(2,1)}, bf16[768,768]{1,0:T(8,128)(2,1)}, bf16[768,1536]{1,0:T(8,128)(2,1)}) custom-call(bf16[768,1536]{1,0:T(8,128)(2,1)} %bitcast.72, bf16[2,1,1536,768]{3,2,1,0:T(8,128)(2,1)} %refs_3_.9, bf16[2,1,1536,768]{3,2,1,0:T(8,128)(2,1)} %refs_4_.5, bf16[2,1,768,1536]{3,2,1,0:T(8,128)(2,1)} %refs_5_.9), custom_call_target="tpu_custom_call" | custom-call | flops 5435817984 | bytes 20971520 | tf_op jit(solution)/shard_map/experts_forward/pallas_call | solution.py:471
  120.3 9.5 %turn_weights.5.refs_4_.refs_3_ = bf16[3584,1536]{1,0:T(8,128)(2,1)} custom-call(s32[1]{0:T(128)} %bitcast.7.refs_0_.refs_7_.me, bf16[1536,2176]{1,0:T(8,128)(2,1)} %all-gather.7.cloned.1.call-done.refs_1_.refs_2_, bf16[192,1536]{1,0:T(8,128)(2,1)} %get-tuple-element.71.refs_2_.refs_8_, ...), custom_call_target="tpu_custom_call", output_to_operand_aliasing={{}: (12, {})} | custom-call | tf_op jit(solution)/shard_map/turn_weights/pallas_call | solution.py:694
  129.8 6.9 %upper_product.3.refs_2_ = f32[768,768]{1,0:T(8,128)} custom-call(s32[1]{0:T(128)} %bitcast.7.refs_0_.refs_7_.me, bf16[768,1536]{1,0:T(8,128)(2,1)} %bitcast.52, bf16[2,1,768,1536]{3,2,1,0:T(8,128)(2,1)} %refs_5_.9, f32[768,768]{1,0:T(8,128)} %upper_product.2.refs_18_.refs_3_, ...), custom_call_target="tpu_custom_call", output_to_operand_aliasing={{}: (3, {})} | custom-call | tf_op jit(solution)/shard_map/upper_product/pallas_call | solution.py:694
  136.7 9.2 %turn_weights.6.refs_10_.refs_2_ = bf16[3584,1536]{1,0:T(8,128)(2,1)} custom-call(s32[1]{0:T(128)} %bitcast.7.refs_0_.refs_7_.me, bf16[1536,3712]{1,0:T(8,128)(2,1)} %all-gather.9.cloned.1.call-done.refs_1_.refs_3_.refs_4_.refs_2_, f32[768,768]{1,0:T(8,128)} %upper_product.3.refs_2_), custom_call_target="tpu_custom_call" | custom-call | tf_op jit(solution)/shard_map/turn_weights/pallas_call | solution.py:694
  147.3 11.7 %attn_forward.3 = (bf16[128,4608]{1,0:T(8,128)(2,1)}, bf16[12,128,128]{2,1,0:T(8,128)(2,1)}, bf16[2,128,128]{2,1,0:T(8,128)(2,1)}, bf16[2,128,128]{2,1,0:T(8,128...) custom-call(f32[128,1536]{1,0:T(8,128)} %get-tuple-element.72.refs_0, ...), custom_call_target="tpu_custom_call" | custom-call | flops 1459617792 | bytes 20971520 | tf_op jit(solution)/shard_map/attn_forward/pallas_call | solution.py:263
  159.1 33.4 %all_to_all.71 = bf16[16,48,1536]{2,1,0:T(8,128)(2,1)} all-to-all(bf16[16,48,1536]{2,1,0:T(8,128)(2,1)} %bitcast.78), channel_id=1, replica_groups=mesh['dp'=8,'expert'=16] {'expert'}, dimensions={0} | all-to-all | bytes 4718592 | tf_op jit(solution)/shard_map/all_to_all | solution.py:883
  193.4 14.5 %experts_both.1 = (bf16[768,768]{1,0:T(8,128)(2,1)}, bf16[768,768]{1,0:T(8,128)(2,1)}, bf16[768,768]{1,0:T(8,128)(2,1)}, bf16[768,1664]{1,0:T(8,128)(2,1)}) custom-call(s32[1]{0:T(128)} %bitcast.11.refs_21_.refs_0_, bf16[768,1536]{1,0:T(8,128)(2,1)} %bitcast.55, f32[768,768]{1,0:T(8,128)} %upper_product.3.refs_2_, ...), custom_call_target="tpu_custom_call" | custom-call | flops 7247757312 | bytes 20971520 | tf_op jit(solution)/shard_map/experts_both/pallas_call | solution.py:471
  211.9 8.3 %experts_out.1 = (bf16[16,16,1536]{2,1,0:T(8,128)(2,1)}, bf16[16,16,1536]{2,1,0:T(8,128)(2,1)}, bf16[16,16,1536]{2,1,0:T(8,128)(2,1)}, bf16[768,1536]{1,0:T(8,128)(2,1)}) custom-call(s32[1]{0:T(128)} %bitcast.11.refs_21_.refs_0_, bf16[768,768]{1,0:T(8,128)(2,1)} %get-tuple-element.81.refs_1_.hidden, bf16[768,1536]{1,0:T(8,128)(2,1)} %bitcast.56, ...), custom_call_target="tpu_custom_call" | custom-call | flops 1811939328 | bytes 20971520 | tf_op jit(solution)/shard_map/experts_out/pallas_call | solution.py:471
  220.2 10.8 %expert_grads.2 = bf16[8,288,1536]{2,1,0:T(8,128)(2,1)} custom-call(bf16[768,1536]{1,0:T(8,128)(2,1)} %bitcast.57, bf16[768,768]{1,0:T(8,128)(2,1)} %get-tuple-element.83.dgate_pre, bf16[768,768]{1,0:T(8,128)(2,1)} %get-tuple-element.84.dup_pre, bf16[768,768]{1,0:T(8,128)(2,1)} %get-tuple-element.81.refs_1_.hidden, bf16[768,1536]{1,0:T(8,128)(2,1)} %get-tuple-element.85.dslot), custom_call_target="tpu_custom_call" | custom-call | flops 5435817984 | bytes 14680064 | tf_op jit(solution)/shard_map/expert_grads/pallas_call | solution.py:770
  244.2 11.6 %attn_backward.2 = (f32[128,1536]{1,0:T(8,128)}, bf16[128,3712]{1,0:T(8,128)(2,1)}, bf16[768,1536]{1,0:T(8,128)(2,1)}) custom-call(bf16[128,1536]{1,0:T(8,128)(2,1)} %refs_0_.7, bf16[768,1664]{1,0:T(8,128)(2,1)} %bitcast.60, bf16[1536,3712]{1,0:T(8,128)(2,1)} %all-gather.9.cloned.1.call-done.refs_1_.refs_3_.refs_4_.refs_2_, ...), custom_call_target="tpu_custom_call" | custom-call | flops 1459617792 | bytes 20971520 | tf_op jit(solution)/shard_map/attn_backward/pallas_call | solution.py:263
  259.1 27.9 %all_to_all.72 = bf16[16,48,1536]{2,1,0:T(8,128)(2,1)} all-to-all(bf16[16,48,1536]{2,1,0:T(8,128)(2,1)S(1)} %bitcast.74), channel_id=1, replica_groups=mesh['dp'=8,'expert'=16] {'expert'}, dimensions={0} | all-to-all | bytes 4718592 | tf_op jit(solution)/shard_map/all_to_all | solution.py:883
  290.8 11.3 %experts_backward.1 = (bf16[768,768]{1,0:T(8,128)(2,1)}, bf16[768,768]{1,0:T(8,128)(2,1)}, bf16[768,1536]{1,0:T(8,128)(2,1)}) custom-call(bf16[768,1536]{1,0:T(8,128)(2,1)} %bitcast.76, bf16[768,768]{1,0:T(8,128)(2,1)} %get-tuple-element.98.refs_1_, bf16[768,768]{1,0:T(8,128)(2,1)} %get-tuple-element.99.refs_2_, bf16[2,1,1536,768]{3,2,1,0:T(8,128)(2,1)} %refs_3_.9, ...), custom_call_target="tpu_custom_call" | custom-call | flops 5435817984 | bytes 20971520 | tf_op jit(solution)/shard_map/experts_backward/pallas_call | solution.py:471
  303.5 6.6 %all-to-all-start.9 = ((bf16[16,48,1536]{2,1,0:T(8,128)(2,1)}), bf16[16,48,1536]{2,1,0:T(8,128)(2,1)S(1)}, u32[]{:S(2)}, u32[]{:S(2)}) async-start(bf16[16,48,1536]{2,1,0:T(8,128)(2,1)} %bitcast.75), calls=%async_computation.9 | async-start | bytes 4718592 | tf_op jit(solution)/shard_map/all_to_all | solution.py:883
  310.1 10.8 %expert_grads.3 = bf16[8,288,1536]{2,1,0:T(8,128)(2,1)} custom-call(bf16[768,1536]{1,0:T(8,128)(2,1)} %bitcast.73, bf16[768,768]{1,0:T(8,128)(2,1)} %get-tuple-element.100.dgate_pre, bf16[768,768]{1,0:T(8,128)(2,1)} %get-tuple-element.101.dup_pre, bf16[768,768]{1,0:T(8,128)(2,1)} %get-tuple-element.102.hidden, bf16[768,1536]{1,0:T(8,128)(2,1)} %bitcast.77), custom_call_target="tpu_custom_call" | custom-call | flops 5435817984 | bytes 14680064 | tf_op jit(solution)/shard_map/expert_grads/pallas_call | solution.py:770
  323.5 6.0 %dense_grads.2.refs_2_ = bf16[16,192,256]{2,1,0:T(8,128)(2,1)} custom-call(s32[1]{0:T(128)} %bitcast.7.refs_0_.refs_7_.me, bf16[3,256,1024]{2,1,0:T(8,128)(2,1)} %turn_columns.3.refs_1_, bf16[1024,3712]{1,0:T(8,128)(2,1)} %all-gather.15.cloned.1.call-done.refs_2_, bf16[256,1536]{1,0:T(8,128)(2,1)} %bitcast.64), custom_call_target="tpu_custom_call" | custom-call | flops 1946157056 | bytes 10485760 | tf_op jit(solution)/shard_map/dense_grads/pallas_call | solution.py:990
  341.5 12.4 %attn_backward.3 = (f32[128,1536]{1,0:T(8,128)}, bf16[128,3712]{1,0:T(8,128)(2,1)}) custom-call(f32[128,1536]{1,0:T(8,128)} %get-tuple-element.105.refs_0_, bf16[768,1536]{1,0:T(8,128)(2,1)} %bitcast.61, bf16[1536,2176]{1,0:T(8,128)(2,1)} %all-gather.7.cloned.1.call-done.refs_1_.refs_2_, bf16[3584,1536]{1,0:T(8,128)(2,1)} %turn_weights.5.refs_4_.refs_3_, ...), custom_call_target="tpu_custom_call" | custom-call | flops 1459617792 | bytes 20971520 | tf_op jit(solution)/shard_map/attn_backward/pallas_call | solution.py:263
  355.6 24.1 %all_to_all.74.pieces_hbm = bf16[16,192,256]{2,1,0:T(8,128)(2,1)} all-to-all(bf16[16,192,256]{2,1,0:T(8,128)(2,1)S(1)} %copy-done.3), channel_id=1, replica_groups=mesh['dp'=8,'expert'=16] {'expert'}, dimensions={0} | all-to-all | bytes 3145728 | tf_op jit(solution)/shard_map/all_to_all | solution.py:1012
  386.5 28.5 %all-gather.17.cloned.1.call-done.refs_2_ = bf16[1024,3712]{1,0:T(8,128)(2,1)} async-done(((bf16[128,3712]{1,0:T(8,128)(2,1)}), bf16[1024,3712]{1,0:T(8,128)(2,1)}) %all-gather.17.cloned.1.call-update) | async-done | bytes 7602192 | tf_op jit(solution)/shard_map/all_gather | solution.py:1190
  422.2 30.1 %all_to_all.73.pieces_hbm = bf16[16,192,256]{2,1,0:T(8,128)(2,1)} all-to-all(bf16[16,192,256]{2,1,0:T(8,128)(2,1)} %after.11), channel_id=1, replica_groups=mesh['dp'=8,'expert'=16] {'expert'}, dimensions={0} | all-to-all | bytes 3145728 | tf_op jit(solution)/shard_map/all_to_all | solution.py:1012
  470.1 11.7 %all-to-all-done.13.refs_0_ = bf16[16,192,256]{2,1,0:T(8,128)(2,1)S(1)} async-done(((bf16[16,192,256]{2,1,0:T(8,128)(2,1)}), bf16[16,192,256]{2,1,0:T(8,128)(2,1)S(1)}, u32[]{:S(2)}, u32[]{:S(2)}) %all-to-all-start.13) | async-done | bytes 1572896 | tf_op jit(solution)/shard_map/all_to_all | solution.py:1012
  (148 shorter events, 132.1 us)
Async XLA Ops:
  7.2 59.0 %all-gather.7.cloned.1.call-start = ((), (), s32[]{:S(2)}) async-start(), calls=%async_computation.16 | async-start | bytes 7520256 | tf_op jit(solution)/shard_map/all_gather | solution.py:1190
  10.2 126.5 %all-gather.9.cloned.1.call-start = ((), (), s32[]{:S(2)}) async-start(), calls=%async_computation.17 | async-start | bytes 12828672 | tf_op jit(solution)/shard_map/all_gather | solution.py:1190
  13.5 25.6 %collective-permute-start = (bf16[192,1536]{1,0:T(8,128)(2,1)}, bf16[192,1536]{1,0:T(8,128)(2,1)S(1)}, u32[]{:S(2)}, u32[]{:S(2)}) collective-permute-start(bf16[192,1536]{1,0:T(8,128)(2,1)} %get-tuple-element.71.refs_2_.refs_8_), channel_id=1, source_target_pairs={{0,32},{16,48},{32,64},{48,80},{64,96},{80,112},{96,0},{112,16},{1... | collective-permute-start | bytes 1769480 | tf_op jit(solution)/shard_map/ppermute | solution.py:837
  15.6 24.3 %collective-permute-start.1 = (bf16[192,1536]{1,0:T(8,128)(2,1)}, bf16[192,1536]{1,0:T(8,128)(2,1)S(1)}, u32[]{:S(2)}, u32[]{:S(2)}) collective-permute-start(bf16[192,1536]{1,0:T(8,128)(2,1)} %get-tuple-element.71.refs_2_.refs_8_), channel_id=1, source_target_pairs={{0,96},{16,112},{32,0},{48,16},{64,32},{80,48},{96,64},{112,80},{1... | collective-permute-start | bytes 1769480 | tf_op jit(solution)/shard_map/ppermute | solution.py:837
  17.8 43.4 %collective-permute-start.4 = (bf16[192,1536]{1,0:T(8,128)(2,1)}, bf16[192,1536]{1,0:T(8,128)(2,1)}, u32[]{:S(2)}, u32[]{:S(2)}) collective-permute-start(bf16[192,1536]{1,0:T(8,128)(2,1)} %get-tuple-element.71.refs_2_.refs_8_), channel_id=1, source_target_pairs={{0,16},{16,0},{32,48},{48,32},{64,80},{80,64},{96,112},{112,96},{1... | collective-permute-start | bytes 1769480 | tf_op jit(solution)/shard_map/ppermute | solution.py:844
  21.4 45.3 %all-to-all-start = ((bf16[16,48,1536]{2,1,0:T(8,128)(2,1)}), bf16[16,48,1536]{2,1,0:T(8,128)(2,1)S(1)}, u32[]{:S(2)}, u32[]{:S(2)}) async-start(bf16[16,48,1536]{2,1,0:T(8,128)(2,1)} %bitcast.63), calls=%async_computation | async-start | bytes 4718592 | tf_op jit(solution)/shard_map/all_to_all | solution.py:883
  28.4 202.6 %all-gather.11.cloned.1.call-start = ((), (), s32[]{:S(2)}) async-start(), calls=%async_computation.18 | async-start | bytes 10616832 | tf_op jit(solution)/shard_map/all_gather | solution.py:1190
  39.9 17.5 %collective-permute-start.2 = (bf16[96,1536]{1,0:T(8,128)(2,1)}, bf16[96,1536]{1,0:T(8,128)(2,1)}, u32[]{:S(2)}, u32[]{:S(2)}) collective-permute-start(bf16[96,1536]{1,0:T(8,128)(2,1)} %slice.17), channel_id=1, source_target_pairs={{0,32},{16,48},{32,64},{48,80},{64,96},{80,112},{96,0},{112,16},{1... | collective-permute-start | bytes 884744 | tf_op jit(solution)/shard_map/ppermute | solution.py:837
  40.7 16.9 %collective-permute-start.3 = (bf16[96,1536]{1,0:T(8,128)(2,1)}, bf16[96,1536]{1,0:T(8,128)(2,1)}, u32[]{:S(2)}, u32[]{:S(2)}) collective-permute-start(bf16[96,1536]{1,0:T(8,128)(2,1)} %slice.18), channel_id=1, source_target_pairs={{0,96},{16,112},{32,0},{48,16},{64,32},{80,48},{96,64},{112,80},{1... | collective-permute-start | bytes 884744 | tf_op jit(solution)/shard_map/ppermute | solution.py:837
  43.9 17.3 %collective-permute-start.5 = (bf16[192,1536]{1,0:T(8,128)(2,1)S(1)}, bf16[192,1536]{1,0:T(8,128)(2,1)}, u32[]{:S(2)}, u32[]{:S(2)}) collective-permute-start(bf16[192,1536]{1,0:T(8,128)(2,1)S(1)} %collective-permute-done.refs_3_.refs_9_), channel_id=1, source_target_pairs={{0,16},{16,0},{32,48},{48,32},{64,80},{80,64},{96,112},{112,96},{1... | collective-permute-start | bytes 1769480 | tf_op jit(solution)/shard_map/ppermute | solution.py:844
  43.9 18.1 %collective-permute-start.6 = (bf16[192,1536]{1,0:T(8,128)(2,1)S(1)}, bf16[192,1536]{1,0:T(8,128)(2,1)}, u32[]{:S(2)}, u32[]{:S(2)}) collective-permute-start(bf16[192,1536]{1,0:T(8,128)(2,1)S(1)} %collective-permute-done.1.refs_4_.refs_10_), channel_id=1, source_target_pairs={{0,16},{16,0},{32,48},{48,32},{64,80},{80,64},{96,112},{112,96},{1... | collective-permute-start | bytes 1769480 | tf_op jit(solution)/shard_map/ppermute | solution.py:844
  115.6 30.4 %all-to-all-start.2 = ((bf16[16,48,1536]{2,1,0:T(8,128)(2,1)}), bf16[16,48,1536]{2,1,0:T(8,128)(2,1)S(1)}, u32[]{:S(2)}, u32[]{:S(2)}) async-start(bf16[16,48,1536]{2,1,0:T(8,128)(2,1)} %bitcast.62), calls=%async_computation.2 | async-start | bytes 4718592 | tf_op jit(solution)/shard_map/all_to_all | solution.py:883
  119.4 201.6 %all-gather.13.cloned.1.call-start = ((), (), s32[]{:S(2)}) async-start(), calls=%async_computation.19 | async-start | bytes 10616832 | tf_op jit(solution)/shard_map/all_gather | solution.py:1190
  207.9 30.3 %all-to-all-start.6 = ((bf16[16,48,1664]{2,1,0:T(8,128)(2,1)}), bf16[16,48,1664]{2,1,0:T(8,128)(2,1)S(1)}, u32[]{:S(2)}, u32[]{:S(2)}) async-start(bf16[16,48,1664]{2,1,0:T(8,128)(2,1)} %bitcast.71), calls=%async_computation.6 | async-start | bytes 5111808 | tf_op jit(solution)/shard_map/all_to_all | solution.py:883
  238.2 18.3 %all-to-all-start.4 = ((bf16[16,16,1536]{2,1,0:T(8,128)(2,1)}), bf16[16,16,1536]{2,1,0:T(8,128)(2,1)S(1)}, u32[]{:S(2)}, u32[]{:S(2)}) async-start(bf16[16,16,1536]{2,1,0:T(8,128)(2,1)} %after.7), calls=%async_computation.4 | async-start | bytes 1572864 | tf_op jit(solution)/shard_map/all_to_all | solution.py:883
  244.1 79.4 %all-gather.15.cloned.1.call-start = ((), (), s32[]{:S(2)}) async-start(), calls=%async_computation.20 | async-start | bytes 8552448 | tf_op jit(solution)/shard_map/all_gather | solution.py:1190
  257.4 125.3 %reduce-scatter.3.cloned.1.call-start = ((), (), s32[]{:S(2)}) async-start(), calls=%async_computation.22 | async-start | bytes 7962624 | tf_op jit(solution)/shard_map/reduce_scatter | solution.py:1236
  287.0 15.6 %all-to-all-start.5 = ((bf16[16,16,1536]{2,1,0:T(8,128)(2,1)}), bf16[16,16,1536]{2,1,0:T(8,128)(2,1)S(1)}, u32[]{:S(2)}, u32[]{:S(2)}) async-start(bf16[16,16,1536]{2,1,0:T(8,128)(2,1)} %get-tuple-element.87), calls=%async_computation.5 | async-start | bytes 1572864 | tf_op jit(solution)/shard_map/all_to_all | solution.py:883
  303.5 32.0 %all-to-all-start.9 = ((bf16[16,48,1536]{2,1,0:T(8,128)(2,1)}), bf16[16,48,1536]{2,1,0:T(8,128)(2,1)S(1)}, u32[]{:S(2)}, u32[]{:S(2)}) async-start(bf16[16,48,1536]{2,1,0:T(8,128)(2,1)} %bitcast.75), calls=%async_computation.9 | async-start | bytes 4718592 | tf_op jit(solution)/shard_map/all_to_all | solution.py:883
  335.5 18.4 %all-to-all-start.8 = ((bf16[16,16,1536]{2,1,0:T(8,128)(2,1)}), bf16[16,16,1536]{2,1,0:T(8,128)(2,1)S(1)}, u32[]{:S(2)}, u32[]{:S(2)}) async-start(bf16[16,16,1536]{2,1,0:T(8,128)(2,1)} %after.9), calls=%async_computation.8 | async-start | bytes 1572864 | tf_op jit(solution)/shard_map/all_to_all | solution.py:883
  341.1 73.9 %all-gather.17.cloned.1.call-start = ((), (), s32[]{:S(2)}) async-start(), calls=%async_computation.21 | async-start | bytes 8552448 | tf_op jit(solution)/shard_map/all_gather | solution.py:1190
  354.8 112.0 %reduce-scatter.5.cloned.1.call-start = ((), (), s32[]{:S(2)}) async-start(), calls=%async_computation.23 | async-start | bytes 7962624 | tf_op jit(solution)/shard_map/reduce_scatter | solution.py:1249
  382.8 38.2 %all-to-all-start.11 = ((bf16[16,192,256]{2,1,0:T(8,128)(2,1)}), bf16[16,192,256]{2,1,0:T(8,128)(2,1)S(1)}, u32[]{:S(2)}, u32[]{:S(2)}) async-start(bf16[16,192,256]{2,1,0:T(8,128)(2,1)} %sum_pieces.2.refs_1_), calls=%async_computation.11 | async-start | bytes 3145728 | tf_op jit(solution)/shard_map/all_to_all | solution.py:1012
  455.1 26.8 %all-to-all-start.13 = ((bf16[16,192,256]{2,1,0:T(8,128)(2,1)}), bf16[16,192,256]{2,1,0:T(8,128)(2,1)S(1)}, u32[]{:S(2)}, u32[]{:S(2)}) async-start(bf16[16,192,256]{2,1,0:T(8,128)(2,1)} %sum_pieces.3), calls=%async_computation.13 | async-start | bytes 3145728 | tf_op jit(solution)/shard_map/all_to_all | solution.py:1012
  (24 other events, 118.1 us)
Sparse Core Ops, SparseCore 0:
  10.3 55.7 all-gather.6
  67.8 63.8 all-gather.8
  134.0 54.5 all-gather.10
  190.1 54.4 all-gather.12
  257.5 60.0 all-gather.14
  319.9 46.3 reduce-scatter.2
  368.6 46.3 all-gather.16
  417.5 46.3 reduce-scatter.4

commit v3 on v2

--- a/solution.py
+++ b/solution.py
@@ -542,31 +542,35 @@
 def experts_both_kernel(
     me, received_hbm, product_hbm, w_hbm, gate_hbm, up_hbm,
     hidden_hbm, dgate_hbm, dup_hbm, back_hbm,
-    received, product, small, gate_w, up_w, act_s, slope_s, hidden, dgate, dup, back,
+    received, product, small, gate_w, up_w, hidden, dgate, dup, back,
     in_sems, out_sems,
 ):
-    pairs = [(received_hbm, received)] + gate_up_pairs(1, gate_hbm, up_hbm, gate_w, up_w)
-    pairs += [small_source(w_hbm, small), (product_hbm, product)]
+    pairs = [(received_hbm, received), small_source(w_hbm, small)]
+    gate_up = gate_up_pairs(1, gate_hbm, up_hbm, gate_w, up_w)
+    for i, tile in enumerate(tiles(FF)):
+        block = (slice(None), pl.ds(tile.start, TILE))
+        pairs += gate_up[2 * i : 2 * i + 2] + [(product_hbm.at[block], product.at[block])]
     reader, writer = Reader(in_sems, pairs), Writer(out_sems)
-    reader.take()
-    for tile in tiles(FF):
-        reader.take(2)
-        gate = dot(received[...], gate_w[:, tile])
-        up = dot(received[...], up_w[:, tile])
-        act, slope = gelu_both(gate)
-        act_s[:, tile] = act
-        slope_s[:, tile] = slope * up
-        hidden[:, tile] = (act * up).astype(BF)
     reader.take(2)
-    writer.send(hidden, hidden_hbm)
     weight = expert_gate(me[0], received[...], small[...])
     total = jnp.zeros((SLOTS, 1), F32)
-    for tile in tiles(FF):
-        dhidden = product[:, tile]
-        total += jnp.sum(dhidden * hidden[:, tile].astype(F32), axis=-1, keepdims=True)
-        dhidden = weight * dhidden
-        dgate[:, tile] = (dhidden * slope_s[:, tile]).astype(BF)
-        dup[:, tile] = (dhidden * act_s[:, tile]).astype(BF)
+    ahead = None
+    for tile in tiles(FF) + [None]:
+        if tile is not None:
+            reader.take(3)
+            coming = (tile, dot(received[...], gate_w[:, tile]), dot(received[...], up_w[:, tile]))
+        if ahead is not None:
+            at, gate, up = ahead
+            act, slope = gelu_both(gate)
+            low = (act * up).astype(BF)
+            hidden[:, at] = low
+            dhidden = product[:, at]
+            total += jnp.sum(dhidden * low.astype(F32), axis=-1, keepdims=True)
+            dhidden = weight * dhidden
+            dgate[:, at] = (dhidden * (slope * up)).astype(BF)
+            dup[:, at] = (dhidden * act).astype(BF)
+        ahead = coming
+    writer.send(hidden, hidden_hbm)
     writer.send(dgate, dgate_hbm)
     writer.send(dup, dup_hbm)
     high, low = split(total)
@@ -591,8 +595,8 @@
         experts_both_kernel, "experts_both", [me, received, product, w, *weights[:2]], order,
         [small, small, small, back],
         [(wide, BF), (small, F32), ((WIDTH, HEAD), BF)] + EXPERT_SCRATCH[:2]
-        + [(small, F32), (small, F32), (small, BF), (small, BF), (small, BF), (back, BF)],
-        10, 8 * SLOTS * WIDTH * FF,
+        + [(small, BF), (small, BF), (small, BF), (back, BF)],
+        11, 8 * SLOTS * WIDTH * FF,
     )
 
 
@@ -753,32 +757,44 @@
     )
 
 
-def expert_grads_kernel(received, dgate_pre, dup_pre, hidden, dslot, packed):
+def expert_grads_kernel(received, dgate_pre, dup_pre, hidden, dslot, *rest):
+    above = None
+    if rest[0].shape[1] == SHARD:
+        packed, down_out = rest
+    else:
+        above, packed = rest
+        down_out = packed.at[:, SHARD : SHARD + FF // DP]
     gate = dot(received[...], dgate_pre[...], 0, 0).astype(BF)
     up = dot(received[...], dup_pre[...], 0, 0).astype(BF)
     down = dot(hidden[...], dslot[...], 0, 0).astype(BF)
     for part in range(DP // 2):
         packed[part, :SHARD, :FF] = gate[part * SHARD : (part + 1) * SHARD]
         packed[part, :SHARD, FF:] = up[part * SHARD : (part + 1) * SHARD]
-        packed[part, SHARD:] = down[part * FF // DP : (part + 1) * FF // DP]
-
-
-def expert_grads(received, dgate_pre, dup_pre, hidden, dslot):
-    rows = SHARD + FF // DP
+        down_out[part] = down[part * FF // DP : (part + 1) * FF // DP]
+    if above is not None:
+        packed[:, SHARD + FF // DP :] = above[...]
+
+
+def expert_grads(received, dgate_pre, dup_pre, hidden, dslot, above):
+    down = FF // DP
+    shapes = [(SHARD,), (down,)] if above is None else [(SHARD + 2 * down,)]
     whole = lambda width: pl.BlockSpec((SLOTS, width), lambda i: (0, 0))
     part = lambda width: pl.BlockSpec((SLOTS, width), lambda i: (0, i))
+    rows = lambda count: pl.BlockSpec((DP // 2, count, WIDTH), lambda i: (i, 0, 0))
+    held = [] if above is None else [above]
     return pl.pallas_call(
         expert_grads_kernel,
         grid=(2,),
-        out_shape=jax.ShapeDtypeStruct((DP, rows, WIDTH), BF),
-        in_specs=[part(WIDTH // 2), whole(FF), whole(FF), part(FF // 2), whole(WIDTH)],
-        out_specs=pl.BlockSpec((DP // 2, rows, WIDTH), lambda i: (i, 0, 0)),
+        out_shape=[jax.ShapeDtypeStruct((DP, count, WIDTH), BF) for count, in shapes],
+        in_specs=[part(WIDTH // 2), whole(FF), whole(FF), part(FF // 2), whole(WIDTH)]
+        + [rows(down)] * len(held),
+        out_specs=[rows(count) for count, in shapes],
         compiler_params=pltpu.CompilerParams(vmem_limit_bytes=VMEM_BYTES),
         cost_estimate=pl.CostEstimate(
             flops=6 * SLOTS * WIDTH * FF, bytes_accessed=14 << 20, transcendentals=0
         ),
         name="expert_grads",
-    )(received, dgate_pre, dup_pre, hidden, dslot).reshape(DP * rows, WIDTH)
+    )(received, dgate_pre, dup_pre, hidden, dslot, *held)
 
 
 def pack_kernel(
@@ -1053,35 +1069,40 @@
 
 
 def finish_kernel(l, refs):
-    (pieces, w_query, key_projection, value_projection, norm_attn), refs = refs[:5], refs[5:]
+    (pieces_hbm, query_w, key_w, value_w, norm_attn), refs = refs[:5], refs[5:]
     if l == 0:
         ends_above, refs = refs[0], refs[5:]
-        (query_hbm, key_hbm, value_hbm, out_hbm, gain_attn, gain_ffn, router) = refs[:7]
-        query, key, value, out, sems = refs[7:]
+        (query_hbm, key_hbm, value_hbm, out_hbm, gain_attn, gain_ffn, router), refs = refs[:7], refs[7:]
     else:
-        query_hbm, key_hbm, value_hbm, out_hbm, ends_out, query, key, value, out, sems = refs
-    writer = Writer(sems)
+        (query_hbm, key_hbm, value_hbm, out_hbm, ends_out), refs = refs[:5], refs[5:]
+    query, key, value, out, pieces, w_query, w_key, w_value, in_sems, sems = refs
+    pairs = [(query_w.at[l], w_query), (key_w.at[l], w_key), (value_w.at[l], w_value)]
+    pairs += [(pieces_hbm.at[chunk], pieces.at[chunk]) for chunk in range(CHUNKS - 1)]
+    reader, writer = Reader(in_sems, pairs), Writer(sems)
     rows = jnp.zeros((SHARD, 1), F32)
+    reader.take(3)
     for chunk in range(SMALL // CHUNK):
+        reader.take()
         part = pieces[chunk].astype(F32)
         lanes = slice(chunk * CHUNK, (chunk + 1) * CHUNK)
         if chunk < Q_END // CHUNK:
             query[:, lanes] = part
-            weight = w_query[l, :, lanes]
+            weight = w_query[:, lanes]
         elif chunk == Q_END // CHUNK:
             key[...] = part
-            weight = key_projection[l]
+            weight = w_key[...]
             writer.send(query, query_hbm.at[l])
             writer.send(key, key_hbm.at[l])
         elif chunk < QKV // CHUNK:
             value[...] = part
-            weight = value_projection[l]
+            weight = w_value[...]
             writer.send(value, value_hbm.at[l])
         else:
             out[:, lanes.start - QKV : lanes.stop - QKV] = part
             continue
         rows += jnp.sum(part * weight.astype(F32), axis=1, keepdims=True)
     writer.send(out, out_hbm.at[l])
+    reader.take()
     ends = pieces[CHUNKS - 2, :, :HEAD].astype(F32)
     ffn = ends[:, EXPERTS : EXPERTS + 1] + ends[:, EXPERTS + 1 : EXPERTS + 2]
     lane = lax.broadcasted_iota(jnp.int32, (SHARD, HEAD), 1)
@@ -1114,21 +1135,24 @@
     return pl.pallas_call(
         lambda *refs: finish_kernel(l, refs),
         out_shape=outs,
-        in_specs=[vmem] * 5 + in_specs,
+        in_specs=[ANY] * 4 + [vmem] + in_specs,
         out_specs=[ANY] * 4 + [vmem] * (len(outs) - 4),
         input_output_aliases=aliases,
         scratch_shapes=[pltpu.VMEM(shape, F32) for shape in slabs]
-        + [pltpu.SemaphoreType.DMA((4,))],
+        + [pltpu.VMEM((CHUNKS, SHARD, CHUNK), BF)]
+        + [pltpu.VMEM(shape, BF) for shape in slabs[:3]]
+        + [pltpu.SemaphoreType.DMA((2 + CHUNKS,)), pltpu.SemaphoreType.DMA((4,))],
         compiler_params=pltpu.CompilerParams(vmem_limit_bytes=VMEM_BYTES),
         name="finish",
     )(pieces, *weights, norm_attn, *ins)
 
 
 def finish_experts_kernel(shares0, shares1, gate, up, down):
+    rows = FF // DP
     for l, shares in enumerate((shares0, shares1)):
         gate[l, 0] = shares[:SHARD, :FF].astype(F32)
         up[l, 0] = shares[:SHARD, FF:].astype(F32)
-        down[l, 0] = shares[SHARD:].astype(F32)
+        down[l, 0] = shares0[SHARD + l * rows : SHARD + (l + 1) * rows].astype(F32)
 
 
 def finish_experts(shares0, shares1):
@@ -1222,7 +1246,7 @@
     )
     back1 = exchange(back1)
     *parts, dslot1 = experts_out(me_expert, hidden1, received1, dx_rows, w[1], w_down, ())
-    grads1 = expert_grads(received1, dgate1, dup1, hidden1, dslot1)
+    grads1, down1 = expert_grads(received1, dgate1, dup1, hidden1, dslot1, None)
     turned0 = turn_columns(me_dp, columns0)
     parts[0] = exchange(after(parts[0], grads1, turned0))
 
@@ -1233,10 +1257,12 @@
     packed1 = after(packed1, parts[0])
     dslot0 = exchange(rows0)
     factors1 = gather(packed1)
-    shares1 = lax.psum_scatter(after(grads1, packed1), "dp", scatter_dimension=0, tiled=True)
+    shares1 = lax.psum_scatter(
+        after(grads1, packed1).reshape(-1, WIDTH), "dp", scatter_dimension=0, tiled=True
+    )
     dgate0, dup0, back0 = experts_backward(dslot0, act0, slope0, experts, ())
     back0 = exchange(back0)
-    grads0 = expert_grads(received0, dgate0, dup0, hidden0, dslot0)
+    (grads0,) = expert_grads(received0, dgate0, dup0, hidden0, dslot0, down1)
     parts[1] = exchange(parts[1])
     turned1 = turn_columns(me_dp, columns1)
     pieces1 = dense_grads(me_dp, turned1, factors1, (parts[1],))
@@ -1246,7 +1272,9 @@
     )
     factors0 = gather(after(packed0, parts[2]))
     summed1 = sum_pieces(to_expert_peers(pieces1), CHUNKS)
-    shares0 = lax.psum_scatter(after(grads0, summed1, shares1), "dp", scatter_dimension=0, tiled=True)
+    shares0 = lax.psum_scatter(
+        after(grads0, summed1, shares1).reshape(-1, WIDTH), "dp", scatter_dimension=0, tiled=True
+    )
     mixed = mixed_rows(kept1["after"], kept1["high"], kept1["low"], parts)
     pieces1 = to_expert_peers(summed1)
     pieces0 = dense_grads(me_dp, turned0, factors0, ())
@@ -1255,10 +1283,11 @@
 
     dense = (w_query, key_projection, value_projection)
     above = finish(1, pieces1, dense, norm_attn, None)
+    gate, up, down = finish_experts(shares0, shares1)
+    above = (after(above[0], gate), *above[1:])
     query, key, value, out, gain_attn, gain_ffn, router = finish(
         0, pieces0, dense, norm_attn, above
     )
-    gate, up, down = finish_experts(shares0, shares1)
     return (
         mixed, grad_tokens, gain_attn, query, key, value, out, gain_ffn,
         router.transpose(0, 2, 1), gate, up, down,

time: 504 us -> 500 us (level)
    all_to_all x2, waiting for transfers between devices: 11.7 us -> 3.56 us  [to_expert_peers(): lax.all_to_all(pieces, 'expert', split_axis=0, concat_axis=0, tiled=True)]
    reduce_scatter x2, waiting for transfers between devices: 0.04 us -> 7.67 us  [the longest x1 7.65 us: local(): lax.psum_scatter(after(grads0, summed1, shares1).reshape(-1, WIDTH), 'dp'...]
where the time goes in v3:
time: 500 us; the launch traced here: 491 us
  Pallas kernels  183 us (37%)
  blocking collectives  143 us (29%)
  waiting for transfers between devices  61.7 us (12%)
  starting transfers between devices  52.9 us (11%)
  local copies, waits for them, and re-layouts  15.3 us (3%)
  between operations  15.2 us (3%)
  other arithmetic  10.3 us (2%)
  matrix products  9.79 us (2%)
    all_to_all x3, blocking collectives, exchange(): lax.all_to_all(rows.reshape(EXPERTS, -1, width), 'expert', split_axis=0,...  88.6 us
    all_to_all x2, blocking collectives, to_expert_peers(): lax.all_to_all(pieces, 'expert', split_axis=0, concat_axis=0, tiled=True)  54.3 us
    pallas_call x4, Pallas kernels, run_attn(): pl.pallas_call(body, out_shape=[sd(shape, kind) for shape, kind in outs],...  44.4 us
    pallas_call x4, Pallas kernels, run_experts(): pl.pallas_call(body, out_shape=[sd(shape, BF) for shape in outs], in_spec...  44.1 us
    all_to_all x7, starting transfers between devices, exchange(): lax.all_to_all(rows.reshape(EXPERTS, -1, width), 'expert', split_axis=0,...  36.6 us
    all_gather x6, waiting for transfers between devices, gather(): return lax.all_gather(values, 'dp', axis=0, tiled=True)  29.6 us
    pallas_call x6, Pallas kernels, on_core(): pl.pallas_call(body, out_shape=[sd(shape, kind) for shape, kind in outs],...  27.3 us
    pallas_call x2, Pallas kernels, expert_grads(): pl.pallas_call(expert_grads_kernel, grid=(2,), out_shape=[jax.ShapeDtypeS...  21.6 us
  transfers between devices with their start and end apart: 26, of which 10 were waited for; matrix products, arithmetic and copies ran while one was open for 5% of the time, Pallas kernels for 36%

profile of v3, /device:TPU:0, one launch (start us, length us, event | category | flops | bytes accessed | tf_op | source)
XLA Modules:
  0.0 491.0 jit_solution(15332942371099018016)
XLA Ops:
  21.4 7.0 %all-to-all-start = ((bf16[16,48,1536]{2,1,0:T(8,128)(2,1)}), bf16[16,48,1536]{2,1,0:T(8,128)(2,1)S(1)}, u32[]{:S(2)}, u32[]{:S(2)}) async-start(bf16[16,48,1536]{2,1,0:T(8,128)(2,1)} %bitcast.61), calls=%async_computation | async-start | bytes 4718592 | tf_op jit(solution)/shard_map/all_to_all | solution.py:899
  49.5 7.9 %collective-permute-done.2.refs_5_.refs_11_ = bf16[96,1536]{1,0:T(8,128)(2,1)} collective-permute-done((bf16[96,1536]{1,0:T(8,128)(2,1)}, bf16[96,1536]{1,0:T(8,128)(2,1)}, u32[]{:S(2)}, u32[]{:S(2)}) %collective-permute-start.2) | collective-permute-done | bytes 294944 | tf_op jit(solution)/shard_map/ppermute | solution.py:853
  68.6 8.7 %attn_forward.2 = (bf16[128,4608]{1,0:T(8,128)(2,1)}, bf16[12,128,128]{2,1,0:T(8,128)(2,1)}, bf16[2,128,128]{2,1,0:T(8,128)(2,1)}, bf16[2,128,128]{2,1,0:T(8,128...) custom-call(bf16[128,1536]{1,0:T(8,128)(2,1)} %refs_9_.1, ...), custom_call_target="tpu_custom_call" | custom-call | flops 1459617792 | bytes 20971520 | tf_op jit(solution)/shard_map/attn_forward/pallas_call | solution.py:263
  77.3 27.3 %all_to_all.70 = bf16[16,48,1536]{2,1,0:T(8,128)(2,1)} all-to-all(bf16[16,48,1536]{2,1,0:T(8,128)(2,1)} %bitcast.77), channel_id=1, replica_groups=mesh['dp'=8,'expert'=16] {'expert'}, dimensions={0} | all-to-all | bytes 4718592 | tf_op jit(solution)/shard_map/all_to_all | solution.py:899
  104.6 10.8 %experts_forward.1 = (bf16[768,768]{1,0:T(8,128)(2,1)}, bf16[768,768]{1,0:T(8,128)(2,1)}, bf16[768,768]{1,0:T(8,128)(2,1)}, bf16[768,1536]{1,0:T(8,128)(2,1)}) custom-call(bf16[768,1536]{1,0:T(8,128)(2,1)} %bitcast.70, bf16[2,1,1536,768]{3,2,1,0:T(8,128)(2,1)} %refs_3_.9, bf16[2,1,1536,768]{3,2,1,0:T(8,128)(2,1)} %refs_4_.5, bf16[2,1,768,1536]{3,2,1,0:T(8,128)(2,1)} %refs_5_.9), custom_call_target="tpu_custom_call" | custom-call | flops 5435817984 | bytes 20971520 | tf_op jit(solution)/shard_map/experts_forward/pallas_call | solution.py:471
  120.2 9.5 %turn_weights.5.refs_4_.refs_3_ = bf16[3584,1536]{1,0:T(8,128)(2,1)} custom-call(s32[1]{0:T(128)} %bitcast.7.refs_0_.refs_7_.me, bf16[1536,2176]{1,0:T(8,128)(2,1)} %all-gather.7.cloned.1.call-done.refs_1_.refs_2_, bf16[192,1536]{1,0:T(8,128)(2,1)} %get-tuple-element.73.refs_2_.refs_8_, ...), custom_call_target="tpu_custom_call", output_to_operand_aliasing={{}: (12, {})} | custom-call | tf_op jit(solution)/shard_map/turn_weights/pallas_call | solution.py:698
  129.7 6.9 %upper_product.3.refs_2_ = f32[768,768]{1,0:T(8,128)} custom-call(s32[1]{0:T(128)} %bitcast.7.refs_0_.refs_7_.me, bf16[768,1536]{1,0:T(8,128)(2,1)} %bitcast.50, bf16[2,1,768,1536]{3,2,1,0:T(8,128)(2,1)} %refs_5_.9, f32[768,768]{1,0:T(8,128)} %upper_product.2.refs_18_.refs_3_, ...), custom_call_target="tpu_custom_call", output_to_operand_aliasing={{}: (3, {})} | custom-call | tf_op jit(solution)/shard_map/upper_product/pallas_call | solution.py:698
  136.6 9.1 %turn_weights.6.refs_10_.refs_2_ = bf16[3584,1536]{1,0:T(8,128)(2,1)} custom-call(s32[1]{0:T(128)} %bitcast.7.refs_0_.refs_7_.me, bf16[1536,3712]{1,0:T(8,128)(2,1)} %all-gather.9.cloned.1.call-done.refs_1_.refs_3_.refs_4_.refs_2_, f32[768,768]{1,0:T(8,128)} %upper_product.3.refs_2_), custom_call_target="tpu_custom_call" | custom-call | tf_op jit(solution)/shard_map/turn_weights/pallas_call | solution.py:698
  147.2 11.7 %attn_forward.3 = (bf16[128,4608]{1,0:T(8,128)(2,1)}, bf16[12,128,128]{2,1,0:T(8,128)(2,1)}, bf16[2,128,128]{2,1,0:T(8,128)(2,1)}, bf16[2,128,128]{2,1,0:T(8,128...) custom-call(f32[128,1536]{1,0:T(8,128)} %get-tuple-element.74.refs_0, ...), custom_call_target="tpu_custom_call" | custom-call | flops 1459617792 | bytes 20971520 | tf_op jit(solution)/shard_map/attn_forward/pallas_call | solution.py:263
  158.9 33.5 %all_to_all.71 = bf16[16,48,1536]{2,1,0:T(8,128)(2,1)} all-to-all(bf16[16,48,1536]{2,1,0:T(8,128)(2,1)} %bitcast.76), channel_id=1, replica_groups=mesh['dp'=8,'expert'=16] {'expert'}, dimensions={0} | all-to-all | bytes 4718592 | tf_op jit(solution)/shard_map/all_to_all | solution.py:899
  193.3 13.7 %experts_both.1 = (bf16[768,768]{1,0:T(8,128)(2,1)}, bf16[768,768]{1,0:T(8,128)(2,1)}, bf16[768,768]{1,0:T(8,128)(2,1)}, bf16[768,1664]{1,0:T(8,128)(2,1)}) custom-call(s32[1]{0:T(128)} %bitcast.11.refs_21_.refs_0_, bf16[768,1536]{1,0:T(8,128)(2,1)} %bitcast.53, f32[768,768]{1,0:T(8,128)} %upper_product.3.refs_2_, ...), custom_call_target="tpu_custom_call" | custom-call | flops 7247757312 | bytes 20971520 | tf_op jit(solution)/shard_map/experts_both/pallas_call | solution.py:471
  210.9 8.4 %experts_out.1 = (bf16[16,16,1536]{2,1,0:T(8,128)(2,1)}, bf16[16,16,1536]{2,1,0:T(8,128)(2,1)}, bf16[16,16,1536]{2,1,0:T(8,128)(2,1)}, bf16[768,1536]{1,0:T(8,128)(2,1)}) custom-call(s32[1]{0:T(128)} %bitcast.11.refs_21_.refs_0_, bf16[768,768]{1,0:T(8,128)(2,1)} %get-tuple-element.83.refs_1_.hidden, bf16[768,1536]{1,0:T(8,128)(2,1)} %bitcast.54, ...), custom_call_target="tpu_custom_call" | custom-call | flops 1811939328 | bytes 20971520 | tf_op jit(solution)/shard_map/experts_out/pallas_call | solution.py:471
  219.3 10.0 %expert_grads.2 = (bf16[8,192,1536]{2,1,0:T(8,128)(2,1)}, bf16[8,96,1536]{2,1,0:T(8,128)(2,1)}) custom-call(bf16[768,1536]{1,0:T(8,128)(2,1)} %bitcast.55, bf16[768,768]{1,0:T(8,128)(2,1)} %get-tuple-element.85.dgate_pre, bf16[768,768]{1,0:T(8,128)(2,1)} %get-tuple-element.86.dup_pre, bf16[768,768]{1,0:T(8,128)(2,1)} %get-tuple-element.83.refs_1_.hidden, ...), custom_call_target="tpu_custom_call" | custom-call | flops 5435817984 | bytes 14680064 | tf_op jit(solution)/shard_map/expert_grads/pallas_call | solution.py:785
  243.2 11.6 %attn_backward.2 = (f32[128,1536]{1,0:T(8,128)}, bf16[128,3712]{1,0:T(8,128)(2,1)}, bf16[768,1536]{1,0:T(8,128)(2,1)}) custom-call(bf16[128,1536]{1,0:T(8,128)(2,1)} %refs_0_.7, bf16[768,1664]{1,0:T(8,128)(2,1)} %bitcast.58, bf16[1536,3712]{1,0:T(8,128)(2,1)} %all-gather.9.cloned.1.call-done.refs_1_.refs_3_.refs_4_.refs_2_, ...), custom_call_target="tpu_custom_call" | custom-call | flops 1459617792 | bytes 20971520 | tf_op jit(solution)/shard_map/attn_backward/pallas_call | solution.py:263
  258.1 27.8 %all_to_all.72 = bf16[16,48,1536]{2,1,0:T(8,128)(2,1)} all-to-all(bf16[16,48,1536]{2,1,0:T(8,128)(2,1)S(1)} %bitcast.72), channel_id=1, replica_groups=mesh['dp'=8,'expert'=16] {'expert'}, dimensions={0} | all-to-all | bytes 4718592 | tf_op jit(solution)/shard_map/all_to_all | solution.py:899
  289.7 11.3 %experts_backward.1 = (bf16[768,768]{1,0:T(8,128)(2,1)}, bf16[768,768]{1,0:T(8,128)(2,1)}, bf16[768,1536]{1,0:T(8,128)(2,1)}) custom-call(bf16[768,1536]{1,0:T(8,128)(2,1)} %bitcast.74, bf16[768,768]{1,0:T(8,128)(2,1)} %get-tuple-element.101.refs_1_, bf16[768,768]{1,0:T(8,128)(2,1)} %get-tuple-element.102.refs_2_, bf16[2,1,1536,768]{3,2,1,0:T(8,128)(2,1)} %refs_3_.9, ...), custom_call_target="tpu_custom_call" | custom-call | flops 5435817984 | bytes 20971520 | tf_op jit(solution)/shard_map/experts_backward/pallas_call | solution.py:471
  302.5 6.6 %all-to-all-start.9 = ((bf16[16,48,1536]{2,1,0:T(8,128)(2,1)}), bf16[16,48,1536]{2,1,0:T(8,128)(2,1)S(1)}, u32[]{:S(2)}, u32[]{:S(2)}) async-start(bf16[16,48,1536]{2,1,0:T(8,128)(2,1)} %bitcast.73), calls=%async_computation.9 | async-start | bytes 4718592 | tf_op jit(solution)/shard_map/all_to_all | solution.py:899
  309.1 11.6 %expert_grads.3.refs_1_.refs_0_ = bf16[8,384,1536]{2,1,0:T(8,128)(2,1)} custom-call(bf16[768,1536]{1,0:T(8,128)(2,1)} %bitcast.71, bf16[768,768]{1,0:T(8,128)(2,1)} %get-tuple-element.103.dgate_pre, bf16[768,768]{1,0:T(8,128)(2,1)} %get-tuple-element.104.dup_pre, bf16[768,768]{1,0:T(8,128)(2,1)} %get-tuple-element.105.hidden, bf16[768,1536]{1,0:T(8,128)(2,1)} %bitcast.75, ...), custom_call_target="tpu_custom_call" | custom-call | flops 5435817984 | bytes 14680064 | tf_op jit(solution)/shard_map/expert_grads/pallas_call | solution.py:785
  323.2 6.0 %dense_grads.2.refs_2_ = bf16[16,192,256]{2,1,0:T(8,128)(2,1)} custom-call(s32[1]{0:T(128)} %bitcast.7.refs_0_.refs_7_.me, bf16[3,256,1024]{2,1,0:T(8,128)(2,1)} %turn_columns.3.refs_1_, bf16[1024,3712]{1,0:T(8,128)(2,1)} %all-gather.15.cloned.1.call-done.refs_2_, bf16[256,1536]{1,0:T(8,128)(2,1)} %bitcast.62), custom_call_target="tpu_custom_call" | custom-call | flops 1946157056 | bytes 10485760 | tf_op jit(solution)/shard_map/dense_grads/pallas_call | solution.py:1006
  340.4 12.4 %attn_backward.3 = (f32[128,1536]{1,0:T(8,128)}, bf16[128,3712]{1,0:T(8,128)(2,1)}) custom-call(f32[128,1536]{1,0:T(8,128)} %get-tuple-element.109.refs_0_, bf16[768,1536]{1,0:T(8,128)(2,1)} %bitcast.59, bf16[1536,2176]{1,0:T(8,128)(2,1)} %all-gather.7.cloned.1.call-done.refs_1_.refs_2_, bf16[3584,1536]{1,0:T(8,128)(2,1)} %turn_weights.5.refs_4_.refs_3_, ...), custom_call_target="tpu_custom_call" | custom-call | flops 1459617792 | bytes 20971520 | tf_op jit(solution)/shard_map/attn_backward/pallas_call | solution.py:263
  354.5 24.2 %all_to_all.74.pieces_hbm = bf16[16,192,256]{2,1,0:T(8,128)(2,1)} all-to-all(bf16[16,192,256]{2,1,0:T(8,128)(2,1)S(1)} %copy-done.3), channel_id=1, replica_groups=mesh['dp'=8,'expert'=16] {'expert'}, dimensions={0} | all-to-all | bytes 3145728 | tf_op jit(solution)/shard_map/all_to_all | solution.py:1028
  385.3 25.3 %all-gather.17.cloned.1.call-done.refs_2_ = bf16[1024,3712]{1,0:T(8,128)(2,1)} async-done(((bf16[128,3712]{1,0:T(8,128)(2,1)}), bf16[1024,3712]{1,0:T(8,128)(2,1)}) %all-gather.17.cloned.1.call-update) | async-done | bytes 7602192 | tf_op jit(solution)/shard_map/all_gather | solution.py:1214
  417.8 30.1 %all_to_all.73.pieces_hbm = bf16[16,192,256]{2,1,0:T(8,128)(2,1)} all-to-all(bf16[16,192,256]{2,1,0:T(8,128)(2,1)} %after.12), channel_id=1, replica_groups=mesh['dp'=8,'expert'=16] {'expert'}, dimensions={0} | all-to-all | bytes 3145728 | tf_op jit(solution)/shard_map/all_to_all | solution.py:1028
  463.0 7.6 %reduce-scatter.5.cloned.1.call-done.shares0 = bf16[384,1536]{1,0:T(8,128)(2,1)} async-done(((bf16[3072,1536]{1,0:T(8,128)(2,1)}), bf16[384,1536]{1,0:T(8,128)(2,1)}) %reduce-scatter.5.cloned.1.call-update) | async-done | bytes 1179664 | tf_op jit(solution)/shard_map/reduce_scatter | solution.py:1275
  (149 shorter events, 137.0 us)
Async XLA Ops:
  7.2 59.0 %all-gather.7.cloned.1.call-start = ((), (), s32[]{:S(2)}) async-start(), calls=%async_computation.16 | async-start | bytes 7520256 | tf_op jit(solution)/shard_map/all_gather | solution.py:1214
  10.2 126.4 %all-gather.9.cloned.1.call-start = ((), (), s32[]{:S(2)}) async-start(), calls=%async_computation.17 | async-start | bytes 12828672 | tf_op jit(solution)/shard_map/all_gather | solution.py:1214
  13.5 25.6 %collective-permute-start = (bf16[192,1536]{1,0:T(8,128)(2,1)}, bf16[192,1536]{1,0:T(8,128)(2,1)S(1)}, u32[]{:S(2)}, u32[]{:S(2)}) collective-permute-start(bf16[192,1536]{1,0:T(8,128)(2,1)} %get-tuple-element.73.refs_2_.refs_8_), channel_id=1, source_target_pairs={{0,32},{16,48},{32,64},{48,80},{64,96},{80,112},{96,0},{112,16},{1... | collective-permute-start | bytes 1769480 | tf_op jit(solution)/shard_map/ppermute | solution.py:853
  15.6 24.3 %collective-permute-start.1 = (bf16[192,1536]{1,0:T(8,128)(2,1)}, bf16[192,1536]{1,0:T(8,128)(2,1)S(1)}, u32[]{:S(2)}, u32[]{:S(2)}) collective-permute-start(bf16[192,1536]{1,0:T(8,128)(2,1)} %get-tuple-element.73.refs_2_.refs_8_), channel_id=1, source_target_pairs={{0,96},{16,112},{32,0},{48,16},{64,32},{80,48},{96,64},{112,80},{1... | collective-permute-start | bytes 1769480 | tf_op jit(solution)/shard_map/ppermute | solution.py:853
  17.8 43.3 %collective-permute-start.4 = (bf16[192,1536]{1,0:T(8,128)(2,1)}, bf16[192,1536]{1,0:T(8,128)(2,1)}, u32[]{:S(2)}, u32[]{:S(2)}) collective-permute-start(bf16[192,1536]{1,0:T(8,128)(2,1)} %get-tuple-element.73.refs_2_.refs_8_), channel_id=1, source_target_pairs={{0,16},{16,0},{32,48},{48,32},{64,80},{80,64},{96,112},{112,96},{1... | collective-permute-start | bytes 1769480 | tf_op jit(solution)/shard_map/ppermute | solution.py:860
  21.4 45.2 %all-to-all-start = ((bf16[16,48,1536]{2,1,0:T(8,128)(2,1)}), bf16[16,48,1536]{2,1,0:T(8,128)(2,1)S(1)}, u32[]{:S(2)}, u32[]{:S(2)}) async-start(bf16[16,48,1536]{2,1,0:T(8,128)(2,1)} %bitcast.61), calls=%async_computation | async-start | bytes 4718592 | tf_op jit(solution)/shard_map/all_to_all | solution.py:899
  28.5 200.8 %all-gather.11.cloned.1.call-start = ((), (), s32[]{:S(2)}) async-start(), calls=%async_computation.18 | async-start | bytes 10616832 | tf_op jit(solution)/shard_map/all_gather | solution.py:1214
  39.9 17.4 %collective-permute-start.2 = (bf16[96,1536]{1,0:T(8,128)(2,1)}, bf16[96,1536]{1,0:T(8,128)(2,1)}, u32[]{:S(2)}, u32[]{:S(2)}) collective-permute-start(bf16[96,1536]{1,0:T(8,128)(2,1)} %slice.17), channel_id=1, source_target_pairs={{0,32},{16,48},{32,64},{48,80},{64,96},{80,112},{96,0},{112,16},{1... | collective-permute-start | bytes 884744 | tf_op jit(solution)/shard_map/ppermute | solution.py:853
  40.7 16.9 %collective-permute-start.3 = (bf16[96,1536]{1,0:T(8,128)(2,1)}, bf16[96,1536]{1,0:T(8,128)(2,1)}, u32[]{:S(2)}, u32[]{:S(2)}) collective-permute-start(bf16[96,1536]{1,0:T(8,128)(2,1)} %slice.18), channel_id=1, source_target_pairs={{0,96},{16,112},{32,0},{48,16},{64,32},{80,48},{96,64},{112,80},{1... | collective-permute-start | bytes 884744 | tf_op jit(solution)/shard_map/ppermute | solution.py:853
  43.9 17.2 %collective-permute-start.5 = (bf16[192,1536]{1,0:T(8,128)(2,1)S(1)}, bf16[192,1536]{1,0:T(8,128)(2,1)}, u32[]{:S(2)}, u32[]{:S(2)}) collective-permute-start(bf16[192,1536]{1,0:T(8,128)(2,1)S(1)} %collective-permute-done.refs_3_.refs_9_), channel_id=1, source_target_pairs={{0,16},{16,0},{32,48},{48,32},{64,80},{80,64},{96,112},{112,96},{1... | collective-permute-start | bytes 1769480 | tf_op jit(solution)/shard_map/ppermute | solution.py:860
  43.9 18.0 %collective-permute-start.6 = (bf16[192,1536]{1,0:T(8,128)(2,1)S(1)}, bf16[192,1536]{1,0:T(8,128)(2,1)}, u32[]{:S(2)}, u32[]{:S(2)}) collective-permute-start(bf16[192,1536]{1,0:T(8,128)(2,1)S(1)} %collective-permute-done.1.refs_4_.refs_10_), channel_id=1, source_target_pairs={{0,16},{16,0},{32,48},{48,32},{64,80},{80,64},{96,112},{112,96},{1... | collective-permute-start | bytes 1769480 | tf_op jit(solution)/shard_map/ppermute | solution.py:860
  115.5 30.3 %all-to-all-start.2 = ((bf16[16,48,1536]{2,1,0:T(8,128)(2,1)}), bf16[16,48,1536]{2,1,0:T(8,128)(2,1)S(1)}, u32[]{:S(2)}, u32[]{:S(2)}) async-start(bf16[16,48,1536]{2,1,0:T(8,128)(2,1)} %bitcast.60), calls=%async_computation.2 | async-start | bytes 4718592 | tf_op jit(solution)/shard_map/all_to_all | solution.py:899
  119.3 201.4 %all-gather.13.cloned.1.call-start = ((), (), s32[]{:S(2)}) async-start(), calls=%async_computation.19 | async-start | bytes 10616832 | tf_op jit(solution)/shard_map/all_gather | solution.py:1214
  207.0 30.2 %all-to-all-start.6 = ((bf16[16,48,1664]{2,1,0:T(8,128)(2,1)}), bf16[16,48,1664]{2,1,0:T(8,128)(2,1)S(1)}, u32[]{:S(2)}, u32[]{:S(2)}) async-start(bf16[16,48,1664]{2,1,0:T(8,128)(2,1)} %bitcast.69), calls=%async_computation.6 | async-start | bytes 5111808 | tf_op jit(solution)/shard_map/all_to_all | solution.py:899
  237.2 18.3 %all-to-all-start.4 = ((bf16[16,16,1536]{2,1,0:T(8,128)(2,1)}), bf16[16,16,1536]{2,1,0:T(8,128)(2,1)S(1)}, u32[]{:S(2)}, u32[]{:S(2)}) async-start(bf16[16,16,1536]{2,1,0:T(8,128)(2,1)} %after.8), calls=%async_computation.4 | async-start | bytes 1572864 | tf_op jit(solution)/shard_map/all_to_all | solution.py:899
  243.1 80.1 %all-gather.15.cloned.1.call-start = ((), (), s32[]{:S(2)}) async-start(), calls=%async_computation.20 | async-start | bytes 8552448 | tf_op jit(solution)/shard_map/all_gather | solution.py:1214
  256.4 125.1 %reduce-scatter.3.cloned.1.call-start = ((), (), s32[]{:S(2)}) async-start(), calls=%async_computation.22 | async-start | bytes 5308416 | tf_op jit(solution)/shard_map/reduce_scatter | solution.py:1260
  285.9 15.7 %all-to-all-start.5 = ((bf16[16,16,1536]{2,1,0:T(8,128)(2,1)}), bf16[16,16,1536]{2,1,0:T(8,128)(2,1)S(1)}, u32[]{:S(2)}, u32[]{:S(2)}) async-start(bf16[16,16,1536]{2,1,0:T(8,128)(2,1)} %get-tuple-element.90), calls=%async_computation.5 | async-start | bytes 1572864 | tf_op jit(solution)/shard_map/all_to_all | solution.py:899
  302.5 32.2 %all-to-all-start.9 = ((bf16[16,48,1536]{2,1,0:T(8,128)(2,1)}), bf16[16,48,1536]{2,1,0:T(8,128)(2,1)S(1)}, u32[]{:S(2)}, u32[]{:S(2)}) async-start(bf16[16,48,1536]{2,1,0:T(8,128)(2,1)} %bitcast.73), calls=%async_computation.9 | async-start | bytes 4718592 | tf_op jit(solution)/shard_map/all_to_all | solution.py:899
  334.7 18.1 %all-to-all-start.8 = ((bf16[16,16,1536]{2,1,0:T(8,128)(2,1)}), bf16[16,16,1536]{2,1,0:T(8,128)(2,1)S(1)}, u32[]{:S(2)}, u32[]{:S(2)}) async-start(bf16[16,16,1536]{2,1,0:T(8,128)(2,1)} %after.10), calls=%async_computation.8 | async-start | bytes 1572864 | tf_op jit(solution)/shard_map/all_to_all | solution.py:899
  340.1 70.5 %all-gather.17.cloned.1.call-start = ((), (), s32[]{:S(2)}) async-start(), calls=%async_computation.21 | async-start | bytes 8552448 | tf_op jit(solution)/shard_map/all_gather | solution.py:1214
  353.8 116.9 %reduce-scatter.5.cloned.1.call-start = ((), (), s32[]{:S(2)}) async-start(), calls=%async_computation.23 | async-start | bytes 10616832 | tf_op jit(solution)/shard_map/reduce_scatter | solution.py:1275
  381.5 35.1 %all-to-all-start.11 = ((bf16[16,192,256]{2,1,0:T(8,128)(2,1)}), bf16[16,192,256]{2,1,0:T(8,128)(2,1)S(1)}, u32[]{:S(2)}, u32[]{:S(2)}) async-start(bf16[16,192,256]{2,1,0:T(8,128)(2,1)} %sum_pieces.2.refs_1_), calls=%async_computation.11 | async-start | bytes 3145728 | tf_op jit(solution)/shard_map/all_to_all | solution.py:1028
  450.8 26.8 %all-to-all-start.13 = ((bf16[16,192,256]{2,1,0:T(8,128)(2,1)}), bf16[16,192,256]{2,1,0:T(8,128)(2,1)S(1)}, u32[]{:S(2)}, u32[]{:S(2)}) async-start(bf16[16,192,256]{2,1,0:T(8,128)(2,1)} %sum_pieces.3), calls=%async_computation.13 | async-start | bytes 3145728 | tf_op jit(solution)/shard_map/all_to_all | solution.py:1028
  (24 other events, 118.1 us)
Sparse Core Ops, SparseCore 0:
  10.3 55.7 all-gather.6
  67.8 63.8 all-gather.8
  134.0 54.5 all-gather.10
  190.1 54.4 all-gather.12
  256.5 60.3 all-gather.14
  319.2 39.3 reduce-scatter.2
  360.9 49.6 all-gather.16
  413.0 57.6 reduce-scatter.4

commit v4 on v3

--- a/solution.py
+++ b/solution.py
@@ -1069,40 +1069,35 @@
 
 
 def finish_kernel(l, refs):
-    (pieces_hbm, query_w, key_w, value_w, norm_attn), refs = refs[:5], refs[5:]
+    (pieces, w_query, key_projection, value_projection, norm_attn), refs = refs[:5], refs[5:]
     if l == 0:
         ends_above, refs = refs[0], refs[5:]
-        (query_hbm, key_hbm, value_hbm, out_hbm, gain_attn, gain_ffn, router), refs = refs[:7], refs[7:]
+        (query_hbm, key_hbm, value_hbm, out_hbm, gain_attn, gain_ffn, router) = refs[:7]
+        query, key, value, out, sems = refs[7:]
     else:
-        (query_hbm, key_hbm, value_hbm, out_hbm, ends_out), refs = refs[:5], refs[5:]
-    query, key, value, out, pieces, w_query, w_key, w_value, in_sems, sems = refs
-    pairs = [(query_w.at[l], w_query), (key_w.at[l], w_key), (value_w.at[l], w_value)]
-    pairs += [(pieces_hbm.at[chunk], pieces.at[chunk]) for chunk in range(CHUNKS - 1)]
-    reader, writer = Reader(in_sems, pairs), Writer(sems)
+        query_hbm, key_hbm, value_hbm, out_hbm, ends_out, query, key, value, out, sems = refs
+    writer = Writer(sems)
     rows = jnp.zeros((SHARD, 1), F32)
-    reader.take(3)
     for chunk in range(SMALL // CHUNK):
-        reader.take()
         part = pieces[chunk].astype(F32)
         lanes = slice(chunk * CHUNK, (chunk + 1) * CHUNK)
         if chunk < Q_END // CHUNK:
             query[:, lanes] = part
-            weight = w_query[:, lanes]
+            weight = w_query[l, :, lanes]
         elif chunk == Q_END // CHUNK:
             key[...] = part
-            weight = w_key[...]
+            weight = key_projection[l]
             writer.send(query, query_hbm.at[l])
             writer.send(key, key_hbm.at[l])
         elif chunk < QKV // CHUNK:
             value[...] = part
-            weight = w_value[...]
+            weight = value_projection[l]
             writer.send(value, value_hbm.at[l])
         else:
             out[:, lanes.start - QKV : lanes.stop - QKV] = part
             continue
         rows += jnp.sum(part * weight.astype(F32), axis=1, keepdims=True)
     writer.send(out, out_hbm.at[l])
-    reader.take()
     ends = pieces[CHUNKS - 2, :, :HEAD].astype(F32)
     ffn = ends[:, EXPERTS : EXPERTS + 1] + ends[:, EXPERTS + 1 : EXPERTS + 2]
     lane = lax.broadcasted_iota(jnp.int32, (SHARD, HEAD), 1)
@@ -1135,13 +1130,11 @@
     return pl.pallas_call(
         lambda *refs: finish_kernel(l, refs),
         out_shape=outs,
-        in_specs=[ANY] * 4 + [vmem] + in_specs,
+        in_specs=[vmem] * 5 + in_specs,
         out_specs=[ANY] * 4 + [vmem] * (len(outs) - 4),
         input_output_aliases=aliases,
         scratch_shapes=[pltpu.VMEM(shape, F32) for shape in slabs]
-        + [pltpu.VMEM((CHUNKS, SHARD, CHUNK), BF)]
-        + [pltpu.VMEM(shape, BF) for shape in slabs[:3]]
-        + [pltpu.SemaphoreType.DMA((2 + CHUNKS,)), pltpu.SemaphoreType.DMA((4,))],
+        + [pltpu.SemaphoreType.DMA((4,))],
         compiler_params=pltpu.CompilerParams(vmem_limit_bytes=VMEM_BYTES),
         name="finish",
     )(pieces, *weights, norm_attn, *ins)
@@ -1232,6 +1225,7 @@
     turned_w = turn_weights(0, me_dp, w[0], out_ring[1:], turned_w, (out0,))
     product = upper_product(0, me_dp, dx_rows, w_down, product, turned_w)
     turned_w1 = turn_weights(0, me_dp, w[1], [], None, product)
+    turned_w1 = turn_weights(1, me_dp, w[1], [], turned_w1, (returned0,))
     columns0 = gather(kept0["columns"])
 
     kept1 = attn_forward(
@@ -1240,9 +1234,8 @@
     )
     received1 = exchange(kept1["rows"])
     columns1 = gather(kept1["columns"])
-    turned_w1 = turn_weights(1, me_dp, w[1], [], turned_w1, (received1,))
     hidden1, dgate1, dup1, back1 = experts_both(
-        me_expert, received1, product[0], w[1], experts, tuple(turned_w1)
+        me_expert, received1, product[0], w[1], experts, ()
     )
     back1 = exchange(back1)
     *parts, dslot1 = experts_out(me_expert, hidden1, received1, dx_rows, w[1], w_down, ())

time: 500 us -> 494 us (0.988)
  blocking collectives: 143 us -> 137 us
    all_to_all x3, blocking collectives: 88.6 us -> 82.7 us  [exchange(): lax.all_to_all(rows.reshape(EXPERTS, -1, width), 'expert', split_axis=0,...]
where the time goes in v4:
time: 494 us; the launch traced here: 485 us
  Pallas kernels  181 us (37%)
  blocking collectives  137 us (28%)
  waiting for transfers between devices  63.6 us (13%)
  starting transfers between devices  52.7 us (11%)
  local copies, waits for them, and re-layouts  15.3 us (3%)
  between operations  15.2 us (3%)
  other arithmetic  10.3 us (2%)
  matrix products  9.79 us (2%)
    all_to_all x3, blocking collectives, exchange(): lax.all_to_all(rows.reshape(EXPERTS, -1, width), 'expert', split_axis=0,...  82.7 us
    all_to_all x2, blocking collectives, to_expert_peers(): lax.all_to_all(pieces, 'expert', split_axis=0, concat_axis=0, tiled=True)  54.2 us
    pallas_call x4, Pallas kernels, run_attn(): pl.pallas_call(body, out_shape=[sd(shape, kind) for shape, kind in outs],...  44.4 us
    pallas_call x4, Pallas kernels, run_experts(): pl.pallas_call(body, out_shape=[sd(shape, BF) for shape in outs], in_spec...  44.1 us
    all_to_all x7, starting transfers between devices, exchange(): lax.all_to_all(rows.reshape(EXPERTS, -1, width), 'expert', split_axis=0,...  36.4 us
    all_gather x6, waiting for transfers between devices, gather(): return lax.all_gather(values, 'dp', axis=0, tiled=True)  30.7 us
    pallas_call x6, Pallas kernels, on_core(): pl.pallas_call(body, out_shape=[sd(shape, kind) for shape, kind in outs],...  27 us
    pallas_call x2, Pallas kernels, expert_grads(): pl.pallas_call(expert_grads_kernel, grid=(2,), out_shape=[jax.ShapeDtypeS...  21.6 us
  transfers between devices with their start and end apart: 26, of which 10 were waited for; matrix products, arithmetic and copies ran while one was open for 5% of the time, Pallas kernels for 36%

profile of v4, /device:TPU:0, one launch (start us, length us, event | category | flops | bytes accessed | tf_op | source)
XLA Modules:
  0.0 485.2 jit_solution(17810498005329663612)
XLA Ops:
  21.4 7.0 %all-to-all-start = ((bf16[16,48,1536]{2,1,0:T(8,128)(2,1)}), bf16[16,48,1536]{2,1,0:T(8,128)(2,1)S(1)}, u32[]{:S(2)}, u32[]{:S(2)}) async-start(bf16[16,48,1536]{2,1,0:T(8,128)(2,1)} %bitcast.61), calls=%async_computation | async-start | bytes 4718592 | tf_op jit(solution)/shard_map/all_to_all | solution.py:899
  49.5 7.9 %collective-permute-done.2.refs_5_.refs_11_ = bf16[96,1536]{1,0:T(8,128)(2,1)} collective-permute-done((bf16[96,1536]{1,0:T(8,128)(2,1)}, bf16[96,1536]{1,0:T(8,128)(2,1)}, u32[]{:S(2)}, u32[]{:S(2)}) %collective-permute-start.2) | collective-permute-done | bytes 294944 | tf_op jit(solution)/shard_map/ppermute | solution.py:853
  68.6 8.7 %attn_forward.2 = (bf16[128,4608]{1,0:T(8,128)(2,1)}, bf16[12,128,128]{2,1,0:T(8,128)(2,1)}, bf16[2,128,128]{2,1,0:T(8,128)(2,1)}, bf16[2,128,128]{2,1,0:T(8,128...) custom-call(bf16[128,1536]{1,0:T(8,128)(2,1)} %refs_9_.1, ...), custom_call_target="tpu_custom_call" | custom-call | flops 1459617792 | bytes 20971520 | tf_op jit(solution)/shard_map/attn_forward/pallas_call | solution.py:263
  77.3 27.3 %all_to_all.70 = bf16[16,48,1536]{2,1,0:T(8,128)(2,1)} all-to-all(bf16[16,48,1536]{2,1,0:T(8,128)(2,1)} %bitcast.77), channel_id=1, replica_groups=mesh['dp'=8,'expert'=16] {'expert'}, dimensions={0} | all-to-all | bytes 4718592 | tf_op jit(solution)/shard_map/all_to_all | solution.py:899
  104.6 10.8 %experts_forward.1 = (bf16[768,768]{1,0:T(8,128)(2,1)}, bf16[768,768]{1,0:T(8,128)(2,1)}, bf16[768,768]{1,0:T(8,128)(2,1)}, bf16[768,1536]{1,0:T(8,128)(2,1)}) custom-call(bf16[768,1536]{1,0:T(8,128)(2,1)} %bitcast.70, bf16[2,1,1536,768]{3,2,1,0:T(8,128)(2,1)} %refs_3_.9, bf16[2,1,1536,768]{3,2,1,0:T(8,128)(2,1)} %refs_4_.5, bf16[2,1,768,1536]{3,2,1,0:T(8,128)(2,1)} %refs_5_.9), custom_call_target="tpu_custom_call" | custom-call | flops 5435817984 | bytes 20971520 | tf_op jit(solution)/shard_map/experts_forward/pallas_call | solution.py:471
  120.2 9.5 %turn_weights.5.refs_4_.refs_3_ = bf16[3584,1536]{1,0:T(8,128)(2,1)} custom-call(s32[1]{0:T(128)} %bitcast.7.refs_0_.refs_7_.me, bf16[1536,2176]{1,0:T(8,128)(2,1)} %all-gather.7.cloned.1.call-done.refs_1_.refs_2_, bf16[192,1536]{1,0:T(8,128)(2,1)} %get-tuple-element.73.refs_2_.refs_8_, ...), custom_call_target="tpu_custom_call", output_to_operand_aliasing={{}: (12, {})} | custom-call | tf_op jit(solution)/shard_map/turn_weights/pallas_call | solution.py:698
  129.7 6.9 %upper_product.3.refs_2_ = f32[768,768]{1,0:T(8,128)} custom-call(s32[1]{0:T(128)} %bitcast.7.refs_0_.refs_7_.me, bf16[768,1536]{1,0:T(8,128)(2,1)} %bitcast.50, bf16[2,1,768,1536]{3,2,1,0:T(8,128)(2,1)} %refs_5_.9, f32[768,768]{1,0:T(8,128)} %upper_product.2.refs_18_.refs_3_, ...), custom_call_target="tpu_custom_call", output_to_operand_aliasing={{}: (3, {})} | custom-call | tf_op jit(solution)/shard_map/upper_product/pallas_call | solution.py:698
  136.6 8.9 %turn_weights.6.refs_2_ = bf16[3584,1536]{1,0:T(8,128)(2,1)} custom-call(s32[1]{0:T(128)} %bitcast.7.refs_0_.refs_7_.me, bf16[1536,3712]{1,0:T(8,128)(2,1)} %all-gather.9.cloned.1.call-done.refs_1_.refs_3_.refs_4_.refs_2_, f32[768,768]{1,0:T(8,128)} %upper_product.3.refs_2_), custom_call_target="tpu_custom_call" | custom-call | tf_op jit(solution)/shard_map/turn_weights/pallas_call | solution.py:698
  147.8 11.7 %attn_forward.3 = (bf16[128,4608]{1,0:T(8,128)(2,1)}, bf16[12,128,128]{2,1,0:T(8,128)(2,1)}, bf16[2,128,128]{2,1,0:T(8,128)(2,1)}, bf16[2,128,128]{2,1,0:T(8,128...) custom-call(f32[128,1536]{1,0:T(8,128)} %get-tuple-element.74.refs_0, ...), custom_call_target="tpu_custom_call" | custom-call | flops 1459617792 | bytes 20971520 | tf_op jit(solution)/shard_map/attn_forward/pallas_call | solution.py:263
  159.5 27.6 %all_to_all.71 = bf16[16,48,1536]{2,1,0:T(8,128)(2,1)} all-to-all(bf16[16,48,1536]{2,1,0:T(8,128)(2,1)} %bitcast.76), channel_id=1, replica_groups=mesh['dp'=8,'expert'=16] {'expert'}, dimensions={0} | all-to-all | bytes 4718592 | tf_op jit(solution)/shard_map/all_to_all | solution.py:899
  187.1 13.8 %experts_both.1 = (bf16[768,768]{1,0:T(8,128)(2,1)}, bf16[768,768]{1,0:T(8,128)(2,1)}, bf16[768,768]{1,0:T(8,128)(2,1)}, bf16[768,1664]{1,0:T(8,128)(2,1)}) custom-call(s32[1]{0:T(128)} %bitcast.11.refs_21_.refs_0_, bf16[768,1536]{1,0:T(8,128)(2,1)} %bitcast.58, f32[768,768]{1,0:T(8,128)} %upper_product.3.refs_2_, ...), custom_call_target="tpu_custom_call" | custom-call | flops 7247757312 | bytes 20971520 | tf_op jit(solution)/shard_map/experts_both/pallas_call | solution.py:471
  204.9 8.2 %experts_out.1 = (bf16[16,16,1536]{2,1,0:T(8,128)(2,1)}, bf16[16,16,1536]{2,1,0:T(8,128)(2,1)}, bf16[16,16,1536]{2,1,0:T(8,128)(2,1)}, bf16[768,1536]{1,0:T(8,128)(2,1)}) custom-call(s32[1]{0:T(128)} %bitcast.11.refs_21_.refs_0_, bf16[768,768]{1,0:T(8,128)(2,1)} %get-tuple-element.83.refs_1_.hidden, bf16[768,1536]{1,0:T(8,128)(2,1)} %bitcast.59, ...), custom_call_target="tpu_custom_call" | custom-call | flops 1811939328 | bytes 20971520 | tf_op jit(solution)/shard_map/experts_out/pallas_call | solution.py:471
  213.1 10.0 %expert_grads.2 = (bf16[8,192,1536]{2,1,0:T(8,128)(2,1)}, bf16[8,96,1536]{2,1,0:T(8,128)(2,1)}) custom-call(bf16[768,1536]{1,0:T(8,128)(2,1)} %bitcast.60, bf16[768,768]{1,0:T(8,128)(2,1)} %get-tuple-element.85.dgate_pre, bf16[768,768]{1,0:T(8,128)(2,1)} %get-tuple-element.86.dup_pre, bf16[768,768]{1,0:T(8,128)(2,1)} %get-tuple-element.83.refs_1_.hidden, ...), custom_call_target="tpu_custom_call" | custom-call | flops 5435817984 | bytes 14680064 | tf_op jit(solution)/shard_map/expert_grads/pallas_call | solution.py:785
  231.0 6.0 %all-to-all-start.4 = ((bf16[16,16,1536]{2,1,0:T(8,128)(2,1)}), bf16[16,16,1536]{2,1,0:T(8,128)(2,1)S(1)}, u32[]{:S(2)}, u32[]{:S(2)}) async-start(bf16[16,16,1536]{2,1,0:T(8,128)(2,1)} %after.8), calls=%async_computation.4 | async-start | bytes 1572864 | tf_op jit(solution)/shard_map/all_to_all | solution.py:899
  237.1 11.6 %attn_backward.2 = (f32[128,1536]{1,0:T(8,128)}, bf16[128,3712]{1,0:T(8,128)(2,1)}, bf16[768,1536]{1,0:T(8,128)(2,1)}) custom-call(bf16[128,1536]{1,0:T(8,128)(2,1)} %refs_0_.7, bf16[768,1664]{1,0:T(8,128)(2,1)} %bitcast.55, bf16[1536,3712]{1,0:T(8,128)(2,1)} %all-gather.9.cloned.1.call-done.refs_1_.refs_3_.refs_4_.refs_2_, ...), custom_call_target="tpu_custom_call" | custom-call | flops 1459617792 | bytes 20971520 | tf_op jit(solution)/shard_map/attn_backward/pallas_call | solution.py:263
  252.0 27.8 %all_to_all.72 = bf16[16,48,1536]{2,1,0:T(8,128)(2,1)} all-to-all(bf16[16,48,1536]{2,1,0:T(8,128)(2,1)S(1)} %bitcast.72), channel_id=1, replica_groups=mesh['dp'=8,'expert'=16] {'expert'}, dimensions={0} | all-to-all | bytes 4718592 | tf_op jit(solution)/shard_map/all_to_all | solution.py:899
  283.6 11.3 %experts_backward.1 = (bf16[768,768]{1,0:T(8,128)(2,1)}, bf16[768,768]{1,0:T(8,128)(2,1)}, bf16[768,1536]{1,0:T(8,128)(2,1)}) custom-call(bf16[768,1536]{1,0:T(8,128)(2,1)} %bitcast.74, bf16[768,768]{1,0:T(8,128)(2,1)} %get-tuple-element.101.refs_1_, bf16[768,768]{1,0:T(8,128)(2,1)} %get-tuple-element.102.refs_2_, bf16[2,1,1536,768]{3,2,1,0:T(8,128)(2,1)} %refs_3_.9, ...), custom_call_target="tpu_custom_call" | custom-call | flops 5435817984 | bytes 20971520 | tf_op jit(solution)/shard_map/experts_backward/pallas_call | solution.py:471
  296.4 6.5 %all-to-all-start.9 = ((bf16[16,48,1536]{2,1,0:T(8,128)(2,1)}), bf16[16,48,1536]{2,1,0:T(8,128)(2,1)S(1)}, u32[]{:S(2)}, u32[]{:S(2)}) async-start(bf16[16,48,1536]{2,1,0:T(8,128)(2,1)} %bitcast.73), calls=%async_computation.9 | async-start | bytes 4718592 | tf_op jit(solution)/shard_map/all_to_all | solution.py:899
  302.9 11.6 %expert_grads.3.refs_1_.refs_0_ = bf16[8,384,1536]{2,1,0:T(8,128)(2,1)} custom-call(bf16[768,1536]{1,0:T(8,128)(2,1)} %bitcast.71, bf16[768,768]{1,0:T(8,128)(2,1)} %get-tuple-element.103.dgate_pre, bf16[768,768]{1,0:T(8,128)(2,1)} %get-tuple-element.104.dup_pre, bf16[768,768]{1,0:T(8,128)(2,1)} %get-tuple-element.105.hidden, bf16[768,1536]{1,0:T(8,128)(2,1)} %bitcast.75, ...), custom_call_target="tpu_custom_call" | custom-call | flops 5435817984 | bytes 14680064 | tf_op jit(solution)/shard_map/expert_grads/pallas_call | solution.py:785
  334.2 12.4 %attn_backward.3 = (f32[128,1536]{1,0:T(8,128)}, bf16[128,3712]{1,0:T(8,128)(2,1)}) custom-call(f32[128,1536]{1,0:T(8,128)} %get-tuple-element.109.refs_0_, bf16[768,1536]{1,0:T(8,128)(2,1)} %bitcast.56, bf16[1536,2176]{1,0:T(8,128)(2,1)} %all-gather.7.cloned.1.call-done.refs_1_.refs_2_, bf16[3584,1536]{1,0:T(8,128)(2,1)} %turn_weights.5.refs_4_.refs_3_, ...), custom_call_target="tpu_custom_call" | custom-call | flops 1459617792 | bytes 20971520 | tf_op jit(solution)/shard_map/attn_backward/pallas_call | solution.py:263
  348.4 24.1 %all_to_all.74.pieces_hbm = bf16[16,192,256]{2,1,0:T(8,128)(2,1)} all-to-all(bf16[16,192,256]{2,1,0:T(8,128)(2,1)S(1)} %copy-done.3), channel_id=1, replica_groups=mesh['dp'=8,'expert'=16] {'expert'}, dimensions={0} | all-to-all | bytes 3145728 | tf_op jit(solution)/shard_map/all_to_all | solution.py:1028
  379.0 26.5 %all-gather.17.cloned.1.call-done.refs_2_ = bf16[1024,3712]{1,0:T(8,128)(2,1)} async-done(((bf16[128,3712]{1,0:T(8,128)(2,1)}), bf16[1024,3712]{1,0:T(8,128)(2,1)}) %all-gather.17.cloned.1.call-update) | async-done | bytes 7602192 | tf_op jit(solution)/shard_map/all_gather | solution.py:1207
  412.7 30.1 %all_to_all.73.pieces_hbm = bf16[16,192,256]{2,1,0:T(8,128)(2,1)} all-to-all(bf16[16,192,256]{2,1,0:T(8,128)(2,1)} %after.12), channel_id=1, replica_groups=mesh['dp'=8,'expert'=16] {'expert'}, dimensions={0} | all-to-all | bytes 3145728 | tf_op jit(solution)/shard_map/all_to_all | solution.py:1028
  457.3 8.3 %reduce-scatter.5.cloned.1.call-done.shares0 = bf16[384,1536]{1,0:T(8,128)(2,1)} async-done(((bf16[3072,1536]{1,0:T(8,128)(2,1)}), bf16[384,1536]{1,0:T(8,128)(2,1)}) %reduce-scatter.5.cloned.1.call-update) | async-done | bytes 1179664 | tf_op jit(solution)/shard_map/reduce_scatter | solution.py:1268
  (149 shorter events, 135.5 us)
Async XLA Ops:
  7.2 59.0 %all-gather.7.cloned.1.call-start = ((), (), s32[]{:S(2)}) async-start(), calls=%async_computation.16 | async-start | bytes 7520256 | tf_op jit(solution)/shard_map/all_gather | solution.py:1207
  10.2 126.4 %all-gather.9.cloned.1.call-start = ((), (), s32[]{:S(2)}) async-start(), calls=%async_computation.17 | async-start | bytes 12828672 | tf_op jit(solution)/shard_map/all_gather | solution.py:1207
  13.5 25.6 %collective-permute-start = (bf16[192,1536]{1,0:T(8,128)(2,1)}, bf16[192,1536]{1,0:T(8,128)(2,1)S(1)}, u32[]{:S(2)}, u32[]{:S(2)}) collective-permute-start(bf16[192,1536]{1,0:T(8,128)(2,1)} %get-tuple-element.73.refs_2_.refs_8_), channel_id=1, source_target_pairs={{0,32},{16,48},{32,64},{48,80},{64,96},{80,112},{96,0},{112,16},{1... | collective-permute-start | bytes 1769480 | tf_op jit(solution)/shard_map/ppermute | solution.py:853
  15.6 24.3 %collective-permute-start.1 = (bf16[192,1536]{1,0:T(8,128)(2,1)}, bf16[192,1536]{1,0:T(8,128)(2,1)S(1)}, u32[]{:S(2)}, u32[]{:S(2)}) collective-permute-start(bf16[192,1536]{1,0:T(8,128)(2,1)} %get-tuple-element.73.refs_2_.refs_8_), channel_id=1, source_target_pairs={{0,96},{16,112},{32,0},{48,16},{64,32},{80,48},{96,64},{112,80},{1... | collective-permute-start | bytes 1769480 | tf_op jit(solution)/shard_map/ppermute | solution.py:853
  17.8 43.3 %collective-permute-start.4 = (bf16[192,1536]{1,0:T(8,128)(2,1)}, bf16[192,1536]{1,0:T(8,128)(2,1)}, u32[]{:S(2)}, u32[]{:S(2)}) collective-permute-start(bf16[192,1536]{1,0:T(8,128)(2,1)} %get-tuple-element.73.refs_2_.refs_8_), channel_id=1, source_target_pairs={{0,16},{16,0},{32,48},{48,32},{64,80},{80,64},{96,112},{112,96},{1... | collective-permute-start | bytes 1769480 | tf_op jit(solution)/shard_map/ppermute | solution.py:860
  21.4 45.2 %all-to-all-start = ((bf16[16,48,1536]{2,1,0:T(8,128)(2,1)}), bf16[16,48,1536]{2,1,0:T(8,128)(2,1)S(1)}, u32[]{:S(2)}, u32[]{:S(2)}) async-start(bf16[16,48,1536]{2,1,0:T(8,128)(2,1)} %bitcast.61), calls=%async_computation | async-start | bytes 4718592 | tf_op jit(solution)/shard_map/all_to_all | solution.py:899
  28.5 194.7 %all-gather.11.cloned.1.call-start = ((), (), s32[]{:S(2)}) async-start(), calls=%async_computation.18 | async-start | bytes 10616832 | tf_op jit(solution)/shard_map/all_gather | solution.py:1207
  39.9 17.4 %collective-permute-start.2 = (bf16[96,1536]{1,0:T(8,128)(2,1)}, bf16[96,1536]{1,0:T(8,128)(2,1)}, u32[]{:S(2)}, u32[]{:S(2)}) collective-permute-start(bf16[96,1536]{1,0:T(8,128)(2,1)} %slice.17), channel_id=1, source_target_pairs={{0,32},{16,48},{32,64},{48,80},{64,96},{80,112},{96,0},{112,16},{1... | collective-permute-start | bytes 884744 | tf_op jit(solution)/shard_map/ppermute | solution.py:853
  40.7 16.9 %collective-permute-start.3 = (bf16[96,1536]{1,0:T(8,128)(2,1)}, bf16[96,1536]{1,0:T(8,128)(2,1)}, u32[]{:S(2)}, u32[]{:S(2)}) collective-permute-start(bf16[96,1536]{1,0:T(8,128)(2,1)} %slice.18), channel_id=1, source_target_pairs={{0,96},{16,112},{32,0},{48,16},{64,32},{80,48},{96,64},{112,80},{1... | collective-permute-start | bytes 884744 | tf_op jit(solution)/shard_map/ppermute | solution.py:853
  43.9 17.2 %collective-permute-start.5 = (bf16[192,1536]{1,0:T(8,128)(2,1)S(1)}, bf16[192,1536]{1,0:T(8,128)(2,1)}, u32[]{:S(2)}, u32[]{:S(2)}) collective-permute-start(bf16[192,1536]{1,0:T(8,128)(2,1)S(1)} %collective-permute-done.refs_3_.refs_9_), channel_id=1, source_target_pairs={{0,16},{16,0},{32,48},{48,32},{64,80},{80,64},{96,112},{112,96},{1... | collective-permute-start | bytes 1769480 | tf_op jit(solution)/shard_map/ppermute | solution.py:860
  43.9 18.0 %collective-permute-start.6 = (bf16[192,1536]{1,0:T(8,128)(2,1)S(1)}, bf16[192,1536]{1,0:T(8,128)(2,1)}, u32[]{:S(2)}, u32[]{:S(2)}) collective-permute-start(bf16[192,1536]{1,0:T(8,128)(2,1)S(1)} %collective-permute-done.1.refs_4_.refs_10_), channel_id=1, source_target_pairs={{0,16},{16,0},{32,48},{48,32},{64,80},{80,64},{96,112},{112,96},{1... | collective-permute-start | bytes 1769480 | tf_op jit(solution)/shard_map/ppermute | solution.py:860
  115.5 30.0 %all-to-all-start.2 = ((bf16[16,48,1536]{2,1,0:T(8,128)(2,1)}), bf16[16,48,1536]{2,1,0:T(8,128)(2,1)S(1)}, u32[]{:S(2)}, u32[]{:S(2)}) async-start(bf16[16,48,1536]{2,1,0:T(8,128)(2,1)} %bitcast.57), calls=%async_computation.2 | async-start | bytes 4718592 | tf_op jit(solution)/shard_map/all_to_all | solution.py:899
  119.3 195.2 %all-gather.13.cloned.1.call-start = ((), (), s32[]{:S(2)}) async-start(), calls=%async_computation.19 | async-start | bytes 10616832 | tf_op jit(solution)/shard_map/all_gather | solution.py:1207
  200.9 30.1 %all-to-all-start.6 = ((bf16[16,48,1664]{2,1,0:T(8,128)(2,1)}), bf16[16,48,1664]{2,1,0:T(8,128)(2,1)S(1)}, u32[]{:S(2)}, u32[]{:S(2)}) async-start(bf16[16,48,1664]{2,1,0:T(8,128)(2,1)} %bitcast.69), calls=%async_computation.6 | async-start | bytes 5111808 | tf_op jit(solution)/shard_map/all_to_all | solution.py:899
  231.0 18.3 %all-to-all-start.4 = ((bf16[16,16,1536]{2,1,0:T(8,128)(2,1)}), bf16[16,16,1536]{2,1,0:T(8,128)(2,1)S(1)}, u32[]{:S(2)}, u32[]{:S(2)}) async-start(bf16[16,16,1536]{2,1,0:T(8,128)(2,1)} %after.8), calls=%async_computation.4 | async-start | bytes 1572864 | tf_op jit(solution)/shard_map/all_to_all | solution.py:899
  237.0 80.0 %all-gather.15.cloned.1.call-start = ((), (), s32[]{:S(2)}) async-start(), calls=%async_computation.20 | async-start | bytes 8552448 | tf_op jit(solution)/shard_map/all_gather | solution.py:1207
  250.3 125.0 %reduce-scatter.3.cloned.1.call-start = ((), (), s32[]{:S(2)}) async-start(), calls=%async_computation.22 | async-start | bytes 5308416 | tf_op jit(solution)/shard_map/reduce_scatter | solution.py:1253
  279.8 15.7 %all-to-all-start.5 = ((bf16[16,16,1536]{2,1,0:T(8,128)(2,1)}), bf16[16,16,1536]{2,1,0:T(8,128)(2,1)S(1)}, u32[]{:S(2)}, u32[]{:S(2)}) async-start(bf16[16,16,1536]{2,1,0:T(8,128)(2,1)} %get-tuple-element.90), calls=%async_computation.5 | async-start | bytes 1572864 | tf_op jit(solution)/shard_map/all_to_all | solution.py:899
  296.4 32.3 %all-to-all-start.9 = ((bf16[16,48,1536]{2,1,0:T(8,128)(2,1)}), bf16[16,48,1536]{2,1,0:T(8,128)(2,1)S(1)}, u32[]{:S(2)}, u32[]{:S(2)}) async-start(bf16[16,48,1536]{2,1,0:T(8,128)(2,1)} %bitcast.73), calls=%async_computation.9 | async-start | bytes 4718592 | tf_op jit(solution)/shard_map/all_to_all | solution.py:899
  328.7 17.9 %all-to-all-start.8 = ((bf16[16,16,1536]{2,1,0:T(8,128)(2,1)}), bf16[16,16,1536]{2,1,0:T(8,128)(2,1)S(1)}, u32[]{:S(2)}, u32[]{:S(2)}) async-start(bf16[16,16,1536]{2,1,0:T(8,128)(2,1)} %after.10), calls=%async_computation.8 | async-start | bytes 1572864 | tf_op jit(solution)/shard_map/all_to_all | solution.py:899
  333.9 71.6 %all-gather.17.cloned.1.call-start = ((), (), s32[]{:S(2)}) async-start(), calls=%async_computation.21 | async-start | bytes 8552448 | tf_op jit(solution)/shard_map/all_gather | solution.py:1207
  347.6 118.0 %reduce-scatter.5.cloned.1.call-start = ((), (), s32[]{:S(2)}) async-start(), calls=%async_computation.23 | async-start | bytes 10616832 | tf_op jit(solution)/shard_map/reduce_scatter | solution.py:1268
  375.3 36.2 %all-to-all-start.11 = ((bf16[16,192,256]{2,1,0:T(8,128)(2,1)}), bf16[16,192,256]{2,1,0:T(8,128)(2,1)S(1)}, u32[]{:S(2)}, u32[]{:S(2)}) async-start(bf16[16,192,256]{2,1,0:T(8,128)(2,1)} %sum_pieces.2.refs_1_), calls=%async_computation.11 | async-start | bytes 3145728 | tf_op jit(solution)/shard_map/all_to_all | solution.py:1028
  445.7 26.8 %all-to-all-start.13 = ((bf16[16,192,256]{2,1,0:T(8,128)(2,1)}), bf16[16,192,256]{2,1,0:T(8,128)(2,1)S(1)}, u32[]{:S(2)}, u32[]{:S(2)}) async-start(bf16[16,192,256]{2,1,0:T(8,128)(2,1)} %sum_pieces.3), calls=%async_computation.13 | async-start | bytes 3145728 | tf_op jit(solution)/shard_map/all_to_all | solution.py:1028
  (24 other events, 117.9 us)
Sparse Core Ops, SparseCore 0:
  10.3 55.7 all-gather.6
  67.8 63.8 all-gather.8
  134.0 54.5 all-gather.10
  190.1 54.4 all-gather.12
  250.4 60.0 all-gather.14
  312.7 39.6 reduce-scatter.2
  354.6 50.8 all-gather.16
  407.9 57.6 reduce-scatter.4

commit v5 on v4

--- a/solution.py
+++ b/solution.py
@@ -1214,16 +1214,16 @@
     dx_rows = exchange(dot(take[1], cotangent).astype(BF))
 
     turned_w = turn_weights(1, me_dp, w[0], out_ring[1:], None, ())
-    product = upper_product(1, me_dp, dx_rows, w_down, None, turned_w)
     kept0 = attn_forward(
         tokens, None, w[0], out_ring, tables, take[0], give[0],
-        (*product, give[1], give_parts, me_expert),
+        (dx_rows, *turned_w, give[1], give_parts, me_expert),
     )
     received0 = exchange(kept0["rows"])
     act0, slope0, hidden0, out0 = experts_forward(received0, experts, ())
     returned0 = exchange(out0)
     turned_w = turn_weights(0, me_dp, w[0], out_ring[1:], turned_w, (out0,))
-    product = upper_product(0, me_dp, dx_rows, w_down, product, turned_w)
+    product = upper_product(0, me_dp, dx_rows, w_down, None, turned_w)
+    product = upper_product(1, me_dp, dx_rows, w_down, product, turned_w)
     turned_w1 = turn_weights(0, me_dp, w[1], [], None, product)
     turned_w1 = turn_weights(1, me_dp, w[1], [], turned_w1, (returned0,))
     columns0 = gather(kept0["columns"])

time: 494 us -> 498 us (level)
  blocking collectives: 137 us -> 147 us
  waiting for transfers between devices: 63.6 us -> 56.6 us
    all_gather x6, waiting for transfers between devices: 30.7 us -> 22.5 us  [gather(): return lax.all_gather(values, 'dp', axis=0, tiled=True)]
    all_to_all x3, blocking collectives: 82.7 us -> 89.9 us  [exchange(): lax.all_to_all(rows.reshape(EXPERTS, -1, width), 'expert', split_axis=0,...]
where the time goes in v5:
time: 498 us; the launch traced here: 490 us
  Pallas kernels  182 us (37%)
  blocking collectives  147 us (30%)
  waiting for transfers between devices  56.6 us (11%)
  starting transfers between devices  53.3 us (11%)
  local copies, waits for them, and re-layouts  15.2 us (3%)
  between operations  15.2 us (3%)
  other arithmetic  10.3 us (2%)
  matrix products  9.8 us (2%)
    all_to_all x3, blocking collectives, exchange(): lax.all_to_all(rows.reshape(EXPERTS, -1, width), 'expert', split_axis=0,...  89.9 us
    all_to_all x2, blocking collectives, to_expert_peers(): lax.all_to_all(pieces, 'expert', split_axis=0, concat_axis=0, tiled=True)  57.2 us
    pallas_call x4, Pallas kernels, run_attn(): pl.pallas_call(body, out_shape=[sd(shape, kind) for shape, kind in outs],...  44.6 us
    pallas_call x4, Pallas kernels, run_experts(): pl.pallas_call(body, out_shape=[sd(shape, BF) for shape in outs], in_spec...  44.1 us
    all_to_all x7, starting transfers between devices, exchange(): lax.all_to_all(rows.reshape(EXPERTS, -1, width), 'expert', split_axis=0,...  37 us
    pallas_call x6, Pallas kernels, on_core(): pl.pallas_call(body, out_shape=[sd(shape, kind) for shape, kind in outs],...  27.6 us
    all_gather x6, waiting for transfers between devices, gather(): return lax.all_gather(values, 'dp', axis=0, tiled=True)  22.5 us
    pallas_call x2, Pallas kernels, expert_grads(): pl.pallas_call(expert_grads_kernel, grid=(2,), out_shape=[jax.ShapeDtypeS...  21.7 us
  transfers between devices with their start and end apart: 26, of which 10 were waited for; matrix products, arithmetic and copies ran while one was open for 5% of the time, Pallas kernels for 36%

profile of v5, /device:TPU:0, one launch (start us, length us, event | category | flops | bytes accessed | tf_op | source)
XLA Modules:
  0.0 489.7 jit_solution(9025234233539451011)
XLA Ops:
  21.4 7.0 %all-to-all-start = ((bf16[16,48,1536]{2,1,0:T(8,128)(2,1)}), bf16[16,48,1536]{2,1,0:T(8,128)(2,1)S(1)}, u32[]{:S(2)}, u32[]{:S(2)}) async-start(bf16[16,48,1536]{2,1,0:T(8,128)(2,1)} %bitcast.62), calls=%async_computation | async-start | bytes 4718592 | tf_op jit(solution)/shard_map/all_to_all | solution.py:899
  49.5 7.9 %collective-permute-done.2.refs_5_.refs_11_ = bf16[96,1536]{1,0:T(8,128)(2,1)} collective-permute-done((bf16[96,1536]{1,0:T(8,128)(2,1)}, bf16[96,1536]{1,0:T(8,128)(2,1)}, u32[]{:S(2)}, u32[]{:S(2)}) %collective-permute-start.2) | collective-permute-done | bytes 294944 | tf_op jit(solution)/shard_map/ppermute | solution.py:853
  68.2 8.6 %attn_forward.2 = (bf16[128,4608]{1,0:T(8,128)(2,1)}, bf16[12,128,128]{2,1,0:T(8,128)(2,1)}, bf16[2,128,128]{2,1,0:T(8,128)(2,1)}, bf16[2,128,128]{2,1,0:T(8,128...) custom-call(bf16[128,1536]{1,0:T(8,128)(2,1)} %refs_9_.1, ...), custom_call_target="tpu_custom_call" | custom-call | flops 1459617792 | bytes 20971520 | tf_op jit(solution)/shard_map/attn_forward/pallas_call | solution.py:263
  76.8 31.1 %all_to_all.70 = bf16[16,48,1536]{2,1,0:T(8,128)(2,1)} all-to-all(bf16[16,48,1536]{2,1,0:T(8,128)(2,1)} %bitcast.78), channel_id=1, replica_groups=mesh['dp'=8,'expert'=16] {'expert'}, dimensions={0} | all-to-all | bytes 4718592 | tf_op jit(solution)/shard_map/all_to_all | solution.py:899
  107.9 10.8 %experts_forward.1 = (bf16[768,768]{1,0:T(8,128)(2,1)}, bf16[768,768]{1,0:T(8,128)(2,1)}, bf16[768,768]{1,0:T(8,128)(2,1)}, bf16[768,1536]{1,0:T(8,128)(2,1)}) custom-call(bf16[768,1536]{1,0:T(8,128)(2,1)} %bitcast.71, bf16[2,1,1536,768]{3,2,1,0:T(8,128)(2,1)} %refs_3_.9, bf16[2,1,1536,768]{3,2,1,0:T(8,128)(2,1)} %refs_4_.5, bf16[2,1,768,1536]{3,2,1,0:T(8,128)(2,1)} %refs_5_.9), custom_call_target="tpu_custom_call" | custom-call | flops 5435817984 | bytes 20971520 | tf_op jit(solution)/shard_map/experts_forward/pallas_call | solution.py:471
  123.5 9.5 %turn_weights.5.refs_3_.refs_4_ = bf16[3584,1536]{1,0:T(8,128)(2,1)} custom-call(s32[1]{0:T(128)} %bitcast.7.refs_0_.refs_7_.me, bf16[1536,2176]{1,0:T(8,128)(2,1)} %all-gather.7.cloned.1.call-done.refs_1_.refs_2_, bf16[192,1536]{1,0:T(8,128)(2,1)} %get-tuple-element.73.refs_2_.refs_8_, ...), custom_call_target="tpu_custom_call", output_to_operand_aliasing={{}: (12, {})} | custom-call | tf_op jit(solution)/shard_map/turn_weights/pallas_call | solution.py:698
  133.0 6.8 %upper_product.2.refs_3_ = f32[768,768]{1,0:T(8,128)} custom-call(s32[1]{0:T(128)} %bitcast.7.refs_0_.refs_7_.me, bf16[768,1536]{1,0:T(8,128)(2,1)} %bitcast.49, bf16[2,1,768,1536]{3,2,1,0:T(8,128)(2,1)} %refs_5_.9, bf16[3584,1536]{1,0:T(8,128)(2,1)} %turn_weights.5.refs_3_.refs_4_), custom_call_target="tpu_custom_call" | custom-call | tf_op jit(solution)/shard_map/upper_product/pallas_call | solution.py:698
  140.3 9.5 %turn_weights.6.refs_2_ = bf16[3584,1536]{1,0:T(8,128)(2,1)} custom-call(s32[1]{0:T(128)} %bitcast.7.refs_0_.refs_7_.me, bf16[1536,3712]{1,0:T(8,128)(2,1)} %all-gather.9.cloned.1.call-done.refs_1_.refs_3_.refs_4_.refs_2_, f32[768,768]{1,0:T(8,128)} %upper_product.3.refs_2_), custom_call_target="tpu_custom_call" | custom-call | tf_op jit(solution)/shard_map/turn_weights/pallas_call | solution.py:698
  152.1 11.8 %attn_forward.3 = (bf16[128,4608]{1,0:T(8,128)(2,1)}, bf16[12,128,128]{2,1,0:T(8,128)(2,1)}, bf16[2,128,128]{2,1,0:T(8,128)(2,1)}, bf16[2,128,128]{2,1,0:T(8,128...) custom-call(f32[128,1536]{1,0:T(8,128)} %get-tuple-element.74.refs_0, ...), custom_call_target="tpu_custom_call" | custom-call | flops 1459617792 | bytes 20971520 | tf_op jit(solution)/shard_map/attn_forward/pallas_call | solution.py:263
  164.0 27.7 %all_to_all.71 = bf16[16,48,1536]{2,1,0:T(8,128)(2,1)} all-to-all(bf16[16,48,1536]{2,1,0:T(8,128)(2,1)} %bitcast.77), channel_id=1, replica_groups=mesh['dp'=8,'expert'=16] {'expert'}, dimensions={0} | all-to-all | bytes 4718592 | tf_op jit(solution)/shard_map/all_to_all | solution.py:899
  191.7 13.7 %experts_both.1 = (bf16[768,768]{1,0:T(8,128)(2,1)}, bf16[768,768]{1,0:T(8,128)(2,1)}, bf16[768,768]{1,0:T(8,128)(2,1)}, bf16[768,1664]{1,0:T(8,128)(2,1)}) custom-call(s32[1]{0:T(128)} %bitcast.11.refs_22_.refs_0_, bf16[768,1536]{1,0:T(8,128)(2,1)} %bitcast.59, f32[768,768]{1,0:T(8,128)} %upper_product.3.refs_2_, ...), custom_call_target="tpu_custom_call" | custom-call | flops 7247757312 | bytes 20971520 | tf_op jit(solution)/shard_map/experts_both/pallas_call | solution.py:471
  209.3 8.3 %experts_out.1 = (bf16[16,16,1536]{2,1,0:T(8,128)(2,1)}, bf16[16,16,1536]{2,1,0:T(8,128)(2,1)}, bf16[16,16,1536]{2,1,0:T(8,128)(2,1)}, bf16[768,1536]{1,0:T(8,128)(2,1)}) custom-call(s32[1]{0:T(128)} %bitcast.11.refs_22_.refs_0_, bf16[768,768]{1,0:T(8,128)(2,1)} %get-tuple-element.83.refs_1_.hidden, bf16[768,1536]{1,0:T(8,128)(2,1)} %bitcast.60, ...), custom_call_target="tpu_custom_call" | custom-call | flops 1811939328 | bytes 20971520 | tf_op jit(solution)/shard_map/experts_out/pallas_call | solution.py:471
  217.6 10.1 %expert_grads.2 = (bf16[8,192,1536]{2,1,0:T(8,128)(2,1)}, bf16[8,96,1536]{2,1,0:T(8,128)(2,1)}) custom-call(bf16[768,1536]{1,0:T(8,128)(2,1)} %bitcast.61, bf16[768,768]{1,0:T(8,128)(2,1)} %get-tuple-element.85.dgate_pre, bf16[768,768]{1,0:T(8,128)(2,1)} %get-tuple-element.86.dup_pre, bf16[768,768]{1,0:T(8,128)(2,1)} %get-tuple-element.83.refs_1_.hidden, ...), custom_call_target="tpu_custom_call" | custom-call | flops 5435817984 | bytes 14680064 | tf_op jit(solution)/shard_map/expert_grads/pallas_call | solution.py:785
  242.0 11.7 %attn_backward.2 = (f32[128,1536]{1,0:T(8,128)}, bf16[128,3712]{1,0:T(8,128)(2,1)}, bf16[768,1536]{1,0:T(8,128)(2,1)}) custom-call(bf16[128,1536]{1,0:T(8,128)(2,1)} %refs_0_.7, bf16[768,1664]{1,0:T(8,128)(2,1)} %bitcast.56, bf16[1536,3712]{1,0:T(8,128)(2,1)} %all-gather.9.cloned.1.call-done.refs_1_.refs_3_.refs_4_.refs_2_, ...), custom_call_target="tpu_custom_call" | custom-call | flops 1459617792 | bytes 20971520 | tf_op jit(solution)/shard_map/attn_backward/pallas_call | solution.py:263
  256.4 31.1 %all_to_all.72 = bf16[16,48,1536]{2,1,0:T(8,128)(2,1)} all-to-all(bf16[16,48,1536]{2,1,0:T(8,128)(2,1)S(1)} %bitcast.73), channel_id=1, replica_groups=mesh['dp'=8,'expert'=16] {'expert'}, dimensions={0} | all-to-all | bytes 4718592 | tf_op jit(solution)/shard_map/all_to_all | solution.py:899
  291.3 11.3 %experts_backward.1 = (bf16[768,768]{1,0:T(8,128)(2,1)}, bf16[768,768]{1,0:T(8,128)(2,1)}, bf16[768,1536]{1,0:T(8,128)(2,1)}) custom-call(bf16[768,1536]{1,0:T(8,128)(2,1)} %bitcast.75, bf16[768,768]{1,0:T(8,128)(2,1)} %get-tuple-element.101.refs_1_, bf16[768,768]{1,0:T(8,128)(2,1)} %get-tuple-element.102.refs_2_, bf16[2,1,1536,768]{3,2,1,0:T(8,128)(2,1)} %refs_3_.9, ...), custom_call_target="tpu_custom_call" | custom-call | flops 5435817984 | bytes 20971520 | tf_op jit(solution)/shard_map/experts_backward/pallas_call | solution.py:471
  303.7 6.9 %all-to-all-start.9 = ((bf16[16,48,1536]{2,1,0:T(8,128)(2,1)}), bf16[16,48,1536]{2,1,0:T(8,128)(2,1)S(1)}, u32[]{:S(2)}, u32[]{:S(2)}) async-start(bf16[16,48,1536]{2,1,0:T(8,128)(2,1)} %bitcast.74), calls=%async_computation.9 | async-start | bytes 4718592 | tf_op jit(solution)/shard_map/all_to_all | solution.py:899
  310.6 11.6 %expert_grads.3.refs_1_.refs_0_ = bf16[8,384,1536]{2,1,0:T(8,128)(2,1)} custom-call(bf16[768,1536]{1,0:T(8,128)(2,1)} %bitcast.72, bf16[768,768]{1,0:T(8,128)(2,1)} %get-tuple-element.103.dgate_pre, bf16[768,768]{1,0:T(8,128)(2,1)} %get-tuple-element.104.dup_pre, bf16[768,768]{1,0:T(8,128)(2,1)} %get-tuple-element.105.hidden, bf16[768,1536]{1,0:T(8,128)(2,1)} %bitcast.76, ...), custom_call_target="tpu_custom_call" | custom-call | flops 5435817984 | bytes 14680064 | tf_op jit(solution)/shard_map/expert_grads/pallas_call | solution.py:785
  330.7 7.4 %all-to-all-done.9 = bf16[16,48,1536]{2,1,0:T(8,128)(2,1)S(1)} async-done(((bf16[16,48,1536]{2,1,0:T(8,128)(2,1)}), bf16[16,48,1536]{2,1,0:T(8,128)(2,1)S(1)}, u32[]{:S(2)}, u32[]{:S(2)}) %all-to-all-start.9) | async-done | bytes 2359328 | tf_op jit(solution)/shard_map/all_to_all | solution.py:899
  344.0 12.4 %attn_backward.3 = (f32[128,1536]{1,0:T(8,128)}, bf16[128,3712]{1,0:T(8,128)(2,1)}) custom-call(f32[128,1536]{1,0:T(8,128)} %get-tuple-element.109.refs_0_, bf16[768,1536]{1,0:T(8,128)(2,1)} %bitcast.57, bf16[1536,2176]{1,0:T(8,128)(2,1)} %all-gather.7.cloned.1.call-done.refs_1_.refs_2_, bf16[3584,1536]{1,0:T(8,128)(2,1)} %turn_weights.5.refs_3_.refs_4_, ...), custom_call_target="tpu_custom_call" | custom-call | flops 1459617792 | bytes 20971520 | tf_op jit(solution)/shard_map/attn_backward/pallas_call | solution.py:263
  358.1 27.1 %all_to_all.74.pieces_hbm = bf16[16,192,256]{2,1,0:T(8,128)(2,1)} all-to-all(bf16[16,192,256]{2,1,0:T(8,128)(2,1)S(1)} %copy-done.3), channel_id=1, replica_groups=mesh['dp'=8,'expert'=16] {'expert'}, dimensions={0} | all-to-all | bytes 3145728 | tf_op jit(solution)/shard_map/all_to_all | solution.py:1028
  391.8 18.3 %all-gather.17.cloned.1.call-done.refs_2_ = bf16[1024,3712]{1,0:T(8,128)(2,1)} async-done(((bf16[128,3712]{1,0:T(8,128)(2,1)}), bf16[1024,3712]{1,0:T(8,128)(2,1)}) %all-gather.17.cloned.1.call-update) | async-done | bytes 7602192 | tf_op jit(solution)/shard_map/all_gather | solution.py:1207
  417.2 30.1 %all_to_all.73.pieces_hbm = bf16[16,192,256]{2,1,0:T(8,128)(2,1)} all-to-all(bf16[16,192,256]{2,1,0:T(8,128)(2,1)} %after.12), channel_id=1, replica_groups=mesh['dp'=8,'expert'=16] {'expert'}, dimensions={0} | all-to-all | bytes 3145728 | tf_op jit(solution)/shard_map/all_to_all | solution.py:1028
  461.9 8.3 %reduce-scatter.5.cloned.1.call-done.shares0 = bf16[384,1536]{1,0:T(8,128)(2,1)} async-done(((bf16[3072,1536]{1,0:T(8,128)(2,1)}), bf16[384,1536]{1,0:T(8,128)(2,1)}) %reduce-scatter.5.cloned.1.call-update) | async-done | bytes 1179664 | tf_op jit(solution)/shard_map/reduce_scatter | solution.py:1268
  (149 shorter events, 135.5 us)
Async XLA Ops:
  7.2 59.0 %all-gather.7.cloned.1.call-start = ((), (), s32[]{:S(2)}) async-start(), calls=%async_computation.16 | async-start | bytes 7520256 | tf_op jit(solution)/shard_map/all_gather | solution.py:1207
  10.2 130.0 %all-gather.9.cloned.1.call-start = ((), (), s32[]{:S(2)}) async-start(), calls=%async_computation.17 | async-start | bytes 12828672 | tf_op jit(solution)/shard_map/all_gather | solution.py:1207
  13.5 25.6 %collective-permute-start = (bf16[192,1536]{1,0:T(8,128)(2,1)}, bf16[192,1536]{1,0:T(8,128)(2,1)S(1)}, u32[]{:S(2)}, u32[]{:S(2)}) collective-permute-start(bf16[192,1536]{1,0:T(8,128)(2,1)} %get-tuple-element.73.refs_2_.refs_8_), channel_id=1, source_target_pairs={{0,32},{16,48},{32,64},{48,80},{64,96},{80,112},{96,0},{112,16},{1... | collective-permute-start | bytes 1769480 | tf_op jit(solution)/shard_map/ppermute | solution.py:853
  15.6 24.3 %collective-permute-start.1 = (bf16[192,1536]{1,0:T(8,128)(2,1)}, bf16[192,1536]{1,0:T(8,128)(2,1)S(1)}, u32[]{:S(2)}, u32[]{:S(2)}) collective-permute-start(bf16[192,1536]{1,0:T(8,128)(2,1)} %get-tuple-element.73.refs_2_.refs_8_), channel_id=1, source_target_pairs={{0,96},{16,112},{32,0},{48,16},{64,32},{80,48},{96,64},{112,80},{1... | collective-permute-start | bytes 1769480 | tf_op jit(solution)/shard_map/ppermute | solution.py:853
  17.8 43.4 %collective-permute-start.4 = (bf16[192,1536]{1,0:T(8,128)(2,1)}, bf16[192,1536]{1,0:T(8,128)(2,1)}, u32[]{:S(2)}, u32[]{:S(2)}) collective-permute-start(bf16[192,1536]{1,0:T(8,128)(2,1)} %get-tuple-element.73.refs_2_.refs_8_), channel_id=1, source_target_pairs={{0,16},{16,0},{32,48},{48,32},{64,80},{80,64},{96,112},{112,96},{1... | collective-permute-start | bytes 1769480 | tf_op jit(solution)/shard_map/ppermute | solution.py:860
  21.4 45.4 %all-to-all-start = ((bf16[16,48,1536]{2,1,0:T(8,128)(2,1)}), bf16[16,48,1536]{2,1,0:T(8,128)(2,1)S(1)}, u32[]{:S(2)}, u32[]{:S(2)}) async-start(bf16[16,48,1536]{2,1,0:T(8,128)(2,1)} %bitcast.62), calls=%async_computation | async-start | bytes 4718592 | tf_op jit(solution)/shard_map/all_to_all | solution.py:899
  28.4 199.3 %all-gather.11.cloned.1.call-start = ((), (), s32[]{:S(2)}) async-start(), calls=%async_computation.18 | async-start | bytes 10616832 | tf_op jit(solution)/shard_map/all_gather | solution.py:1207
  39.9 17.4 %collective-permute-start.2 = (bf16[96,1536]{1,0:T(8,128)(2,1)}, bf16[96,1536]{1,0:T(8,128)(2,1)}, u32[]{:S(2)}, u32[]{:S(2)}) collective-permute-start(bf16[96,1536]{1,0:T(8,128)(2,1)} %slice.17), channel_id=1, source_target_pairs={{0,32},{16,48},{32,64},{48,80},{64,96},{80,112},{96,0},{112,16},{1... | collective-permute-start | bytes 884744 | tf_op jit(solution)/shard_map/ppermute | solution.py:853
  40.7 16.9 %collective-permute-start.3 = (bf16[96,1536]{1,0:T(8,128)(2,1)}, bf16[96,1536]{1,0:T(8,128)(2,1)}, u32[]{:S(2)}, u32[]{:S(2)}) collective-permute-start(bf16[96,1536]{1,0:T(8,128)(2,1)} %slice.18), channel_id=1, source_target_pairs={{0,96},{16,112},{32,0},{48,16},{64,32},{80,48},{96,64},{112,80},{1... | collective-permute-start | bytes 884744 | tf_op jit(solution)/shard_map/ppermute | solution.py:853
  43.9 17.3 %collective-permute-start.5 = (bf16[192,1536]{1,0:T(8,128)(2,1)S(1)}, bf16[192,1536]{1,0:T(8,128)(2,1)}, u32[]{:S(2)}, u32[]{:S(2)}) collective-permute-start(bf16[192,1536]{1,0:T(8,128)(2,1)S(1)} %collective-permute-done.refs_3_.refs_9_), channel_id=1, source_target_pairs={{0,16},{16,0},{32,48},{48,32},{64,80},{80,64},{96,112},{112,96},{1... | collective-permute-start | bytes 1769480 | tf_op jit(solution)/shard_map/ppermute | solution.py:860
  43.9 18.0 %collective-permute-start.6 = (bf16[192,1536]{1,0:T(8,128)(2,1)S(1)}, bf16[192,1536]{1,0:T(8,128)(2,1)}, u32[]{:S(2)}, u32[]{:S(2)}) collective-permute-start(bf16[192,1536]{1,0:T(8,128)(2,1)S(1)} %collective-permute-done.1.refs_4_.refs_10_), channel_id=1, source_target_pairs={{0,16},{16,0},{32,48},{48,32},{64,80},{80,64},{96,112},{112,96},{1... | collective-permute-start | bytes 1769480 | tf_op jit(solution)/shard_map/ppermute | solution.py:860
  118.7 31.2 %all-to-all-start.2 = ((bf16[16,48,1536]{2,1,0:T(8,128)(2,1)}), bf16[16,48,1536]{2,1,0:T(8,128)(2,1)S(1)}, u32[]{:S(2)}, u32[]{:S(2)}) async-start(bf16[16,48,1536]{2,1,0:T(8,128)(2,1)} %bitcast.58), calls=%async_computation.2 | async-start | bytes 4718592 | tf_op jit(solution)/shard_map/all_to_all | solution.py:899
  122.6 199.6 %all-gather.13.cloned.1.call-start = ((), (), s32[]{:S(2)}) async-start(), calls=%async_computation.19 | async-start | bytes 10616832 | tf_op jit(solution)/shard_map/all_gather | solution.py:1207
  205.4 30.6 %all-to-all-start.6 = ((bf16[16,48,1664]{2,1,0:T(8,128)(2,1)}), bf16[16,48,1664]{2,1,0:T(8,128)(2,1)S(1)}, u32[]{:S(2)}, u32[]{:S(2)}) async-start(bf16[16,48,1664]{2,1,0:T(8,128)(2,1)} %bitcast.70), calls=%async_computation.6 | async-start | bytes 5111808 | tf_op jit(solution)/shard_map/all_to_all | solution.py:899
  236.0 17.7 %all-to-all-start.4 = ((bf16[16,16,1536]{2,1,0:T(8,128)(2,1)}), bf16[16,16,1536]{2,1,0:T(8,128)(2,1)S(1)}, u32[]{:S(2)}, u32[]{:S(2)}) async-start(bf16[16,16,1536]{2,1,0:T(8,128)(2,1)} %after.8), calls=%async_computation.4 | async-start | bytes 1572864 | tf_op jit(solution)/shard_map/all_to_all | solution.py:899
  241.9 82.8 %all-gather.15.cloned.1.call-start = ((), (), s32[]{:S(2)}) async-start(), calls=%async_computation.20 | async-start | bytes 8552448 | tf_op jit(solution)/shard_map/all_gather | solution.py:1207
  254.6 133.4 %reduce-scatter.3.cloned.1.call-start = ((), (), s32[]{:S(2)}) async-start(), calls=%async_computation.22 | async-start | bytes 5308416 | tf_op jit(solution)/shard_map/reduce_scatter | solution.py:1253
  287.4 15.4 %all-to-all-start.5 = ((bf16[16,16,1536]{2,1,0:T(8,128)(2,1)}), bf16[16,16,1536]{2,1,0:T(8,128)(2,1)S(1)}, u32[]{:S(2)}, u32[]{:S(2)}) async-start(bf16[16,16,1536]{2,1,0:T(8,128)(2,1)} %get-tuple-element.90), calls=%async_computation.5 | async-start | bytes 1572864 | tf_op jit(solution)/shard_map/all_to_all | solution.py:899
  303.7 34.5 %all-to-all-start.9 = ((bf16[16,48,1536]{2,1,0:T(8,128)(2,1)}), bf16[16,48,1536]{2,1,0:T(8,128)(2,1)S(1)}, u32[]{:S(2)}, u32[]{:S(2)}) async-start(bf16[16,48,1536]{2,1,0:T(8,128)(2,1)} %bitcast.74), calls=%async_computation.9 | async-start | bytes 4718592 | tf_op jit(solution)/shard_map/all_to_all | solution.py:899
  338.2 18.3 %all-to-all-start.8 = ((bf16[16,16,1536]{2,1,0:T(8,128)(2,1)}), bf16[16,16,1536]{2,1,0:T(8,128)(2,1)S(1)}, u32[]{:S(2)}, u32[]{:S(2)}) async-start(bf16[16,16,1536]{2,1,0:T(8,128)(2,1)} %after.10), calls=%async_computation.8 | async-start | bytes 1572864 | tf_op jit(solution)/shard_map/all_to_all | solution.py:899
  343.7 66.4 %all-gather.17.cloned.1.call-start = ((), (), s32[]{:S(2)}) async-start(), calls=%async_computation.21 | async-start | bytes 8552448 | tf_op jit(solution)/shard_map/all_gather | solution.py:1207
  357.3 112.8 %reduce-scatter.5.cloned.1.call-start = ((), (), s32[]{:S(2)}) async-start(), calls=%async_computation.23 | async-start | bytes 10616832 | tf_op jit(solution)/shard_map/reduce_scatter | solution.py:1268
  388.1 28.0 %all-to-all-start.11 = ((bf16[16,192,256]{2,1,0:T(8,128)(2,1)}), bf16[16,192,256]{2,1,0:T(8,128)(2,1)S(1)}, u32[]{:S(2)}, u32[]{:S(2)}) async-start(bf16[16,192,256]{2,1,0:T(8,128)(2,1)} %sum_pieces.2.refs_1_), calls=%async_computation.11 | async-start | bytes 3145728 | tf_op jit(solution)/shard_map/all_to_all | solution.py:1028
  450.2 26.7 %all-to-all-start.13 = ((bf16[16,192,256]{2,1,0:T(8,128)(2,1)}), bf16[16,192,256]{2,1,0:T(8,128)(2,1)S(1)}, u32[]{:S(2)}, u32[]{:S(2)}) async-start(bf16[16,192,256]{2,1,0:T(8,128)(2,1)} %sum_pieces.3), calls=%async_computation.13 | async-start | bytes 3145728 | tf_op jit(solution)/shard_map/all_to_all | solution.py:1028
  (24 other events, 118.0 us)
Sparse Core Ops, SparseCore 0:
  10.3 55.7 all-gather.6
  67.8 63.8 all-gather.8
  134.0 54.5 all-gather.10
  190.2 54.4 all-gather.12
  254.8 58.1 all-gather.14
  315.3 39.6 reduce-scatter.2
  357.4 52.5 all-gather.16
  412.5 57.6 reduce-scatter.4
